TPU v7x, 32 devices: a whole 2x2x4 slice. The times are simulated.
32 devices in a mesh: seq: 8 (over y, x, core), rec: 4 (over z).
Axes of the slice: x: 2, y: 2, z: 4, core: 2. Of those that a mesh axis runs over, the one named last changes fastest.
Arguments:
- features: bfloat16 [16, 8192, 80], P('rec', 'seq'), may hold values from -16 to 16, as said below
- time_keep: int32 [16, 8192], P('rec', 'seq'), may hold values 0 or 1
- freq_keep: int32 [16, 80], P('rec'), may hold values 0 or 1
- block_flags: int32 [16, 8], P('rec'), may hold values from 0 to 1, as said below
- decays: float32 [16, 8, 2048], P('rec', None, 'seq'), may hold values from 0.5 to 1, as said below
- w_sub: bfloat16 [512, 320], replicated, may hold values from -0.3125 to 0.3125
- ln1_gain: float32 [512], replicated, may hold values from 0.25 to 1.75
- ffn1_in: bfloat16 [512, 2048], replicated, may hold values from -0.25 to 0.25
- ffn1_out: bfloat16 [2048, 512], replicated, may hold values from -0.125 to 0.125
- ln2_gain: float32 [512], replicated, may hold values from 0.25 to 1.75
- ssm_in: bfloat16 [512, 1536], replicated, may hold values from -0.25 to 0.25
- ssm_out: bfloat16 [512, 512], replicated, may hold values from -0.25 to 0.25
- ln3_gain: float32 [512], replicated, may hold values from 0.25 to 1.75
- conv_in: bfloat16 [512, 1024], replicated, may hold values from -0.25 to 0.25
- conv_depth: float32 [512, 15], replicated, may hold values from -1.5 to 1.5
- bn_gain: float32 [512], replicated, may hold values from 0.25 to 1.75
- bn_shift: float32 [512], replicated, may hold values from -3 to 3
- conv_out: bfloat16 [512, 512], replicated, may hold values from -0.25 to 0.25
- ln4_gain: float32 [512], replicated, may hold values from 0.25 to 1.75
- ffn2_in: bfloat16 [512, 2048], replicated, may hold values from -0.25 to 0.25
- ffn2_out: bfloat16 [2048, 512], replicated, may hold values from -0.125 to 0.125
- ln5_gain: float32 [512], replicated, may hold values from 0.25 to 1.75
- out_grad: bfloat16 [16, 2048, 512], P('rec', 'seq'), may hold values from -6 to 6
Outputs:
- output: bfloat16 [16, 2048, 512], P('rec', 'seq')
- features_grad: float32 [16, 8192, 80], P('rec', 'seq')
- w_sub_grad: float32 [512, 320], P('seq')
- ln1_gain_grad: float32 [512], P('seq')
- ffn1_in_grad: float32 [512, 2048], P('seq')
- ffn1_out_grad: float32 [2048, 512], P('seq')
- ln2_gain_grad: float32 [512], P('seq')
- ssm_in_grad: float32 [512, 1536], P('seq')
- ssm_out_grad: float32 [512, 512], P('seq')
- ln3_gain_grad: float32 [512], P('seq')
- conv_in_grad: float32 [512, 1024], P('seq')
- conv_depth_grad: float32 [512, 15], P('seq')
- bn_gain_grad: float32 [512], P('seq')
- bn_shift_grad: float32 [512], P('seq')
- conv_out_grad: float32 [512, 512], P('seq')
- ln4_gain_grad: float32 [512], P('seq')
- ffn2_in_grad: float32 [512, 2048], P('seq')
- ffn2_out_grad: float32 [2048, 512], P('seq')
- ln5_gain_grad: float32 [512], P('seq')
Inputs may be any that keep to these rules, and one draw needn't show every extreme that they name: `features`: entries are the input frames with a ramp along time; all finite. decays[r, h, t] is the factor by which head h of row r keeps its state at frame t; strictly below 1. block_flags[r, 0] is 1 in every row; after block 0 a 1 stands only at blocks whose number is a multiple of 4; in every draw some row has no 1 after block 0.
All inputs are finite; a program needn't handle non-finite values. No bound on the sum of `time_keep` or of `freq_keep` on one device may be relied on, other than what follows from the above.
Results may differ from a plain program's by a relative error of at most 0.012.
Values sent between devices are 32-bit elements; how exact they have to be, the bound alone decides.
No kernel may reach another device: no remote copies, remote signals or barrier semaphores. Data moves between devices by JAX's collectives and lax.ppermute only.
A program may use at most 256 MiB of HBM per device.

v0:
```python
import jax
import jax.numpy as jnp
from jax import lax
from jax.sharding import PartitionSpec as P

D = 512
HEADS = 8
STATE = 32
SUB = 4
KERNEL = 15
HEADP = 64


norm_eps = 1e-05
batch_eps = 1e-05
highest = lax.Precision.HIGHEST


def entering(value, axis, join, neutral, backward):
    count, mine = (lax.axis_size(axis), lax.axis_index(axis))
    pieces = jax.tree.map(lambda part: lax.all_gather(part, axis), value)
    if backward:
        pieces = jax.tree.map(lambda part: part[::-1], pieces)
        mine = count - 1 - mine
    total = jax.tree.map(
        lambda part, zero: jnp.full_like(part, 0) + jnp.asarray(zero, part.dtype), value, neutral
    )

    def hop(position, total):
        longer = join(total, jax.tree.map(lambda part: part[position], pieces))
        return jax.tree.map(lambda new, old: jnp.where(position < mine, new, old), longer, total)

    return lax.fori_loop(0, count - 1, hop, total)


def extended(cells, sides, width):
    for axis, dim in sides:
        count = lax.axis_size(axis)
        ends = count - 1
        head = lax.slice_in_dim(cells, 0, width, axis=dim)
        tail = lax.slice_in_dim(cells, cells.shape[dim] - width, cells.shape[dim], axis=dim)
        cells = jnp.concatenate(
            [
                lax.ppermute(tail, axis, [(i, (i + 1) % count) for i in range(ends)]),
                cells,
                lax.ppermute(head, axis, [((i + 1) % count, i) for i in range(ends)]),
            ],
            axis=dim,
        )
    return cells


def plain_dot(matrix_a, matrix_b):
    return jnp.dot(matrix_a, matrix_b, preferred_element_type=jnp.float32)


def dot_transposed(matrix_a, matrix_b):
    return lax.dot_general(
        matrix_a, matrix_b, (((1,), (1,)), ((), ())), preferred_element_type=jnp.float32
    )


def dot_outer(matrix_a, matrix_b):
    return lax.dot_general(
        matrix_a, matrix_b, (((0,), (0,)), ((), ())), preferred_element_type=jnp.float32
    )


def contract(formula, tensor_a, tensor_b):
    return jnp.einsum(formula, tensor_a, tensor_b, precision=highest)


def norm_forward(signal, norm_gain):
    centred = signal - jnp.mean(signal, axis=-1, keepdims=True)
    inv_scale = lax.rsqrt(jnp.mean(centred * centred, axis=-1, keepdims=True) + norm_eps)
    unit_part = centred * inv_scale
    return (unit_part * norm_gain, (unit_part, inv_scale))


def norm_backward(incoming, saved_norm, norm_gain):
    unit_part, inv_scale = saved_norm
    scaled = incoming * norm_gain
    inner_part = (
        scaled
        - jnp.mean(scaled, axis=-1, keepdims=True)
        - unit_part * jnp.mean(scaled * unit_part, axis=-1, keepdims=True)
    )
    return (inner_part * inv_scale, jnp.sum(incoming * unit_part, axis=0))


def silu_slope(signal):
    sigmoid = jax.nn.sigmoid(signal)
    return sigmoid * (1.0 + signal * (1.0 - sigmoid))


def ffn_forward(signal, norm_gain, weight_in, weight_out):
    standardized_input, saved_norm = norm_forward(signal, norm_gain)
    lowered = standardized_input.astype(jnp.bfloat16)
    hidden = plain_dot(lowered, weight_in)
    active = jax.nn.silu(hidden).astype(jnp.bfloat16)
    return (signal + 0.5 * plain_dot(active, weight_out), (saved_norm, lowered, hidden, active))


def ffn_backward(incoming, saved_set, norm_gain, weight_in, weight_out):
    saved_norm, lowered, hidden, active = saved_set
    out_low = (0.5 * incoming).astype(jnp.bfloat16)
    out_weight_grad = dot_outer(active, out_low)
    hidden_low = (dot_transposed(out_low, weight_out) * silu_slope(hidden)).astype(jnp.bfloat16)
    in_weight_grad = dot_outer(lowered, hidden_low)
    back_part, gain_grad = norm_backward(
        dot_transposed(hidden_low, weight_in), saved_norm, norm_gain
    )
    return (incoming + back_part, gain_grad, in_weight_grad, out_weight_grad)


def link_blocks(earlier, later):
    return (earlier[0] * later[0], later[0][:, :, None, None] * earlier[1] + later[1])


def depth_apply(padded, depth_weight, step_count, flipped):
    running = jnp.zeros(padded.shape[:1] + (step_count,) + padded.shape[2:], jnp.float32)
    for offset in range(KERNEL):
        first_row = KERNEL - 1 - offset if flipped else offset
        running = (
            running + padded[:, first_row : first_row + step_count, :] * depth_weight[:, offset]
        )
    return running


def local(
    features,
    time_keep,
    freq_keep,
    block_flags,
    decays,
    w_sub,
    ln1_gain,
    ffn1_in,
    ffn1_out,
    ln2_gain,
    ssm_in,
    ssm_out,
    ln3_gain,
    conv_in,
    conv_depth,
    bn_gain,
    bn_shift,
    conv_out,
    ln4_gain,
    ffn2_in,
    ffn2_out,
    ln5_gain,
    out_grad,
):
    row_count, frame_count, mel_count = features.shape
    step_count = frame_count // SUB
    token_count = row_count * step_count
    block_count = lax.axis_size("seq")
    seq_place = lax.axis_index("seq")
    device_count = block_count * lax.axis_size("rec")
    frame_total = float(token_count * device_count)
    here_start = lax.dynamic_index_in_dim(block_flags, seq_place, 1, keepdims=False)
    next_start = lax.dynamic_index_in_dim(
        block_flags, jnp.minimum(seq_place + 1, block_count - 1), 1, keepdims=False
    )
    keep_here = (1 - here_start).astype(jnp.float32)
    keep_next = jnp.where(seq_place + 1 < block_count, 1 - next_start, 0).astype(jnp.float32)
    keep_mask = time_keep[:, :, None] * freq_keep[:, None, :]
    masked = features * keep_mask.astype(jnp.bfloat16)
    flat_in = masked.reshape(token_count, SUB * mel_count)
    layer_in = dot_transposed(flat_in, w_sub)
    after_ffn, ffn1_saved = ffn_forward(layer_in, ln1_gain, ffn1_in, ffn1_out)
    normed_ssm, ssm_norm = norm_forward(after_ffn, ln2_gain)
    lowered_ssm = normed_ssm.astype(jnp.bfloat16)
    projected = plain_dot(lowered_ssm, ssm_in)
    width_bc = HEADS * STATE

    def by_head(column_block, head_width):
        return column_block.reshape(row_count, step_count, HEADS, head_width).transpose(0, 2, 1, 3)

    def by_token(head_block):
        return head_block.transpose(0, 2, 1, 3).reshape(token_count, -1)

    attention_contents = by_head(projected[:, :D], HEADP)
    gate_in = projected[:, D : 2 * D]
    read_vecs = by_head(projected[:, 2 * D + width_bc :], STATE)
    log_decay = jnp.log(decays)
    input_scale = jnp.sqrt(-2.0 * log_decay)
    keys_in = by_head(projected[:, 2 * D : 2 * D + width_bc], STATE) * input_scale[..., None]
    cumulative = jnp.cumsum(log_decay, axis=-1)
    causal = jnp.arange(step_count)[:, None] >= jnp.arange(step_count)[None, :]
    weights = jnp.where(
        causal,
        jnp.exp(jnp.where(causal, cumulative[..., :, None] - cumulative[..., None, :], 0.0)),
        0.0,
    )
    head_weight = jnp.exp(cumulative)
    tail_weight = jnp.exp(cumulative[..., -1:] - cumulative)
    block_decay = keep_here[:, None] * jnp.exp(cumulative[..., -1])
    local_end = contract("rhsn,rhsp->rhnp", keys_in * tail_weight[..., None], attention_contents)
    identity = (jnp.ones_like(block_decay), jnp.zeros_like(local_end))
    before = entering((block_decay, local_end), "seq", link_blocks, identity, False)
    start_state = before[1] * keep_here[:, None, None, None]
    scores = contract("rhtn,rhsn->rhts", read_vecs, keys_in) * weights
    reads_start = read_vecs * head_weight[..., None]
    mixed_out = contract("rhts,rhsp->rhtp", scores, attention_contents) + contract(
        "rhtn,rhnp->rhtp", reads_start, start_state
    )
    mixed_flat = by_token(mixed_out) * STATE ** (-0.5)
    gate_sig = jax.nn.sigmoid(gate_in)
    gated = (mixed_flat * gate_in * gate_sig).astype(jnp.bfloat16)
    after_ssm = after_ffn + plain_dot(gated, ssm_out)
    normed_conv, conv_norm = norm_forward(after_ssm, ln3_gain)
    lowered_conv = normed_conv.astype(jnp.bfloat16)
    lifted = plain_dot(lowered_conv, conv_in)
    lift_sig = jax.nn.sigmoid(lifted[:, D:])
    glu_out = (lifted[:, :D] * lift_sig).reshape(row_count, step_count, D)
    half_span = KERNEL // 2
    rim_pos = jnp.arange(step_count + 2 * half_span)[None, :]
    rim_keep = jnp.where(
        rim_pos < half_span,
        keep_here[:, None],
        jnp.where(rim_pos >= step_count + half_span, keep_next[:, None], 1.0),
    )[:, :, None]
    padded = extended(glu_out, (("seq", 1),), half_span) * rim_keep
    depth_out = depth_apply(padded, conv_depth, step_count, False)
    batch_statistic_sums = lax.psum(
        (jnp.sum(depth_out, axis=(0, 1)), jnp.sum(depth_out * depth_out, axis=(0, 1))),
        ("seq", "rec"),
    )
    batch_mean = batch_statistic_sums[0] / frame_total
    batch_inv = lax.rsqrt(
        batch_statistic_sums[1] / frame_total - batch_mean * batch_mean + batch_eps
    )
    batch_unit = (depth_out - batch_mean) * batch_inv
    batch_out = (batch_unit * bn_gain + bn_shift).reshape(token_count, D)
    active_conv = jax.nn.silu(batch_out).astype(jnp.bfloat16)
    after_conv = after_ssm + plain_dot(active_conv, conv_out)
    after_late, ffn2_saved = ffn_forward(after_conv, ln4_gain, ffn2_in, ffn2_out)
    result, final_norm = norm_forward(after_late, ln5_gain)
    late_grad, ln5_grad = norm_backward(
        out_grad.reshape(token_count, D).astype(jnp.float32), final_norm, ln5_gain
    )
    conv_grad, ln4_grad, ffn2_in_grad, ffn2_out_grad = ffn_backward(
        late_grad, ffn2_saved, ln4_gain, ffn2_in, ffn2_out
    )
    conv_low = conv_grad.astype(jnp.bfloat16)
    conv_out_grad = dot_outer(active_conv, conv_low)
    batch_grad = (dot_transposed(conv_low, conv_out) * silu_slope(batch_out)).reshape(
        row_count, step_count, D
    )
    back_stats = lax.psum(
        (jnp.sum(batch_grad * batch_unit, axis=(0, 1)), jnp.sum(batch_grad, axis=(0, 1))),
        ("seq", "rec"),
    )
    depth_grad = (
        bn_gain
        * batch_inv
        * (batch_grad - (back_stats[1] + batch_unit * back_stats[0]) / frame_total)
    )
    conv_depth_grad = jnp.stack(
        [
            jnp.sum(depth_grad * padded[:, offset : offset + step_count, :], axis=(0, 1))
            for offset in range(KERNEL)
        ],
        axis=1,
    )
    grad_padded = extended(depth_grad, (("seq", 1),), half_span) * rim_keep
    glu_grad = depth_apply(grad_padded, conv_depth, step_count, True).reshape(token_count, D)
    lifted_low = jnp.concatenate(
        [glu_grad * lift_sig, glu_grad * lifted[:, :D] * lift_sig * (1.0 - lift_sig)], axis=1
    ).astype(jnp.bfloat16)
    conv_in_grad = dot_outer(lowered_conv, lifted_low)
    conv_back, ln3_grad = norm_backward(dot_transposed(lifted_low, conv_in), conv_norm, ln3_gain)
    ssm_grad = conv_grad + conv_back
    ssm_low = ssm_grad.astype(jnp.bfloat16)
    ssm_out_grad = dot_outer(gated, ssm_low)
    gated_grad = dot_transposed(ssm_low, ssm_out)
    mixed_grad = by_head(gated_grad * gate_in * gate_sig * STATE ** (-0.5), HEADP)
    gate_grad = gated_grad * mixed_flat * silu_slope(gate_in)
    pulled = contract("rhtn,rhtp->rhnp", reads_start, mixed_grad)
    from_later = entering(
        (block_decay, keep_here[:, None, None, None] * pulled), "seq", link_blocks, identity, True
    )
    end_grad = from_later[1]
    paired = contract("rhtp,rhsp->rhts", mixed_grad, attention_contents) * weights
    reads_grad = contract("rhts,rhsn->rhtn", paired, keys_in) + head_weight[..., None] * contract(
        "rhtp,rhnp->rhtn", mixed_grad, start_state
    )
    values_grad = contract("rhts,rhtp->rhsp", scores, mixed_grad) + tail_weight[
        ..., None
    ] * contract("rhsn,rhnp->rhsp", keys_in, end_grad)
    keys_grad = (
        contract("rhts,rhtn->rhsn", paired, read_vecs)
        + tail_weight[..., None] * contract("rhsp,rhnp->rhsn", attention_contents, end_grad)
    ) * input_scale[..., None]
    proj_low = jnp.concatenate(
        [by_token(values_grad), gate_grad, by_token(keys_grad), by_token(reads_grad)], axis=1
    ).astype(jnp.bfloat16)
    ssm_in_grad = dot_outer(lowered_ssm, proj_low)
    ssm_back, ln2_grad = norm_backward(dot_transposed(proj_low, ssm_in), ssm_norm, ln2_gain)
    front_grad = ssm_grad + ssm_back
    entry_grad, ln1_grad, ffn1_in_grad, ffn1_out_grad = ffn_backward(
        front_grad, ffn1_saved, ln1_gain, ffn1_in, ffn1_out
    )
    entry_low = entry_grad.astype(jnp.bfloat16)
    w_sub_grad = dot_outer(entry_low, flat_in)
    features_grad = plain_dot(entry_low, w_sub).reshape(
        row_count, frame_count, mel_count
    ) * keep_mask.astype(jnp.float32)
    share_rows = D // block_count
    offset_start = seq_place * share_rows
    bn_gain_grad = lax.dynamic_slice_in_dim(back_stats[0], offset_start, share_rows)
    bn_shift_grad = lax.dynamic_slice_in_dim(back_stats[1], offset_start, share_rows)
    shares = (
        lax.psum_scatter(w_sub_grad, "seq", scatter_dimension=0, tiled=True),
        lax.psum_scatter(ln1_grad, "seq", scatter_dimension=0, tiled=True),
        lax.psum_scatter(ffn1_in_grad, "seq", scatter_dimension=0, tiled=True),
        lax.psum_scatter(ffn1_out_grad, "seq", scatter_dimension=0, tiled=True),
        lax.psum_scatter(ln2_grad, "seq", scatter_dimension=0, tiled=True),
        lax.psum_scatter(ssm_in_grad, "seq", scatter_dimension=0, tiled=True),
        lax.psum_scatter(ssm_out_grad, "seq", scatter_dimension=0, tiled=True),
        lax.psum_scatter(ln3_grad, "seq", scatter_dimension=0, tiled=True),
        lax.psum_scatter(conv_in_grad, "seq", scatter_dimension=0, tiled=True),
        lax.psum_scatter(conv_depth_grad, "seq", scatter_dimension=0, tiled=True),
        lax.psum_scatter(conv_out_grad, "seq", scatter_dimension=0, tiled=True),
        lax.psum_scatter(ln4_grad, "seq", scatter_dimension=0, tiled=True),
        lax.psum_scatter(ffn2_in_grad, "seq", scatter_dimension=0, tiled=True),
        lax.psum_scatter(ffn2_out_grad, "seq", scatter_dimension=0, tiled=True),
        lax.psum_scatter(ln5_grad, "seq", scatter_dimension=0, tiled=True),
    )
    summed = lax.psum(
        (
            shares[0],
            shares[1],
            shares[2],
            shares[3],
            shares[4],
            shares[5],
            shares[6],
            shares[7],
            shares[8],
            shares[9],
            shares[10],
            shares[11],
            shares[12],
            shares[13],
            shares[14],
        ),
        "rec",
    )
    return (
        result.reshape(row_count, step_count, D).astype(jnp.bfloat16),
        features_grad,
        summed[0],
        summed[1],
        summed[2],
        summed[3],
        summed[4],
        summed[5],
        summed[6],
        summed[7],
        summed[8],
        summed[9],
        bn_gain_grad,
        bn_shift_grad,
        summed[10],
        summed[11],
        summed[12],
        summed[13],
        summed[14],
    )


def solution(mesh):
    return jax.shard_map(
        local,
        mesh=mesh,
        in_specs=(
            P("rec", "seq", None),
            P("rec", "seq"),
            P("rec", None),
            P("rec", None),
            P("rec", None, "seq"),
            P(),
            P(),
            P(),
            P(),
            P(),
            P(),
            P(),
            P(),
            P(),
            P(),
            P(),
            P(),
            P(),
            P(),
            P(),
            P(),
            P(),
            P("rec", "seq", None),
        ),
        out_specs=(
            P("rec", "seq", None),
            P("rec", "seq", None),
            P("seq", None),
            P("seq"),
            P("seq", None),
            P("seq", None),
            P("seq"),
            P("seq", None),
            P("seq", None),
            P("seq"),
            P("seq", None),
            P("seq", None),
            P("seq"),
            P("seq"),
            P("seq", None),
            P("seq"),
            P("seq", None),
            P("seq", None),
            P("seq"),
        ),
        check_vma=False,
    )
```

profile of v0, /device:TPU:0, one launch (start us, length us, event | category | flops | bytes accessed | tf_op | source)
XLA Modules:
  0.0 947.4 jit_solution(9921588224509101057)
XLA Ops:
  58.9 10.3 %all_gather.18 = f32[8,4,8]{2,1,0:T(4,128)S(1)} all-gather(f32[1,4,8]{2,1,0:T(4,128)S(1)} %bitcast_multiply_fusion.15), channel_id=1, replica_groups=mesh['seq'=8,'rec'=4] {'seq'}, dimensions={0}, use_global_device_ids=true | all-gather | bytes 1152 | tf_op jit(solution)/shard_map/all_gather | solution.py:21
  72.6 8.3 fusion.119
  84.2 11.8 %fusion.6 = f32[4,8,256,64]{2,3,1,0:T(8,128)} fusion(f32[4,8,256,256]{3,2,1,0:T(8,128)S(1)} %fusion.119, f32[4,8,256]{2,1,0:T(8,128)S(1)} %get-tuple-element.402, pred[256,256]{1,0:T(8,128)(4,1)S(1)} %iota_compare_fusion, f32[4,256,8,64]{1,3,2,0:T(8,128)S(1)} %copy-done.15), kind=kOutput, calls=%fused_computation.16 | convolution fusion | flops 1619001344 | bytes 12681216 | tf_op jit(solution)/shard_map/rhts,rhsp->rhtp/dot_general | solution.py:70
  95.9 8.5 while.28
  138.8 43.9 %all-reduce.6 = (f32[512]{0:T(512)S(1)}, f32[512]{0:T(512)S(1)}) all-reduce(f32[512]{0:T(512)S(1)} %get-tuple-element.351, f32[512]{0:T(512)S(1)} %get-tuple-element.350), channel_id=1, replica_groups=mesh['seq'=8,'rec'=4] {'seq','rec'}, use_global_device_ids=true, to_apply=%region_13.14 | all-reduce | flops 1024 | bytes 8192 | tf_op jit(solution)/shard_map/psum | solution.py:227
  216.0 41.8 %all-reduce.5 = (f32[512]{0:T(512)}, f32[512]{0:T(512)}) all-reduce(f32[512]{0:T(512)S(1)} %get-tuple-element.454, f32[512]{0:T(512)} %reduce_sum.412), channel_id=1, replica_groups=mesh['seq'=8,'rec'=4] {'seq','rec'}, use_global_device_ids=true, to_apply=%region_25.26 | all-reduce | flops 1024 | bytes 8192 | tf_op jit(solution)/shard_map/psum | solution.py:252
  257.8 6.7 multiply_reduce_fusion.1
  299.8 9.2 fusion.68
  309.0 9.7 %fusion.88 = f32[4,256,8,32]{1,3,2,0:T(8,128)S(1)} fusion(f32[4,8,256,256]{3,2,1,0:T(8,128)S(1)} %fusion.68, f32[4,8,256]{2,1,0:T(8,128)S(1)} %get-tuple-element.402, pred[256,256]{1,0:T(8,128)(4,1)S(1)} %iota_compare_fusion, f32[4,256,8,32]{1,0,3,2:T(4,128)S(1)} %copy-done.21, f32[4,8,256]{2,1,0:T(8,128)S(1)} %get-tuple-element.418), kind=kOutput, calls=%fused_computation.184 | convolution fusion | flops 813957120 | bytes 10616832 | tf_op jit(solution)/shard_map/rhts,rhsn->rhtn/dot_general | solution.py:70
  331.9 11.7 %fusion.85 = f32[4,256,8,32]{1,3,2,0:T(8,128)} fusion(f32[4,8,256,256]{3,2,1,0:T(8,128)} %copy-done.40, f32[4,8,256]{2,1,0:T(8,128)S(1)} %get-tuple-element.402, pred[256,256]{1,0:T(8,128)(4,1)S(1)} %iota_compare_fusion, f32[4,256,8,32]{1,0,3,2:T(4,128)} %reshape.399), kind=kOutput, calls=%fused_computation.183 | convolution fusion | flops 813694976 | bytes 10584064 | tf_op jit(solution)/shard_map/rhts,rhtn->rhsn/dot_general | solution.py:70
  343.6 11.0 %fusion.4 = f32[4,8,256,64]{2,3,1,0:T(8,128)} fusion(f32[4,8,256,256]{3,2,1,0:T(8,128)} %copy-done.25, f32[4,8,256]{2,1,0:T(8,128)S(1)} %get-tuple-element.402, pred[256,256]{1,0:T(8,128)(4,1)S(1)} %iota_compare_fusion, f32[4,8,256,64]{2,0,3,1:T(4,128)S(1)} %bitcast.253), kind=kOutput, calls=%fused_computation.15 | convolution fusion | flops 1619001344 | bytes 12681216 | tf_op jit(solution)/shard_map/rhts,rhtp->rhsp/dot_general | solution.py:70
  359.7 8.7 while.29
  424.2 7.0 fusion.164
  441.1 17.7 %reduce-scatter.23.cloned.1.call-done = f32[64,1024]{1,0:T(8,128)} async-done(((f32[512,1024]{1,0:T(8,128)}), f32[64,1024]{1,0:T(8,128)}) %reduce-scatter.23.cloned.1.call-update) | async-done | bytes 262160 | tf_op jit(solution)/shard_map/reduce_scatter | solution.py:324
  458.8 38.3 %reduce-scatter.13.cloned.1.call-done = f32[64,320]{1,0:T(8,128)} async-done(((f32[512,320]{1,0:T(8,128)}), f32[64,320]{1,0:T(8,128)}) %reduce-scatter.13.cloned.1.call-update) | async-done | bytes 81936 | tf_op jit(solution)/shard_map/reduce_scatter | solution.py:316
  497.1 55.1 %reduce-scatter.27.cloned.1.call-done = f32[64,2048]{1,0:T(8,128)} async-done(((f32[512,2048]{1,0:T(8,128)}), f32[64,2048]{1,0:T(8,128)}) %reduce-scatter.27.cloned.1.call-update) | async-done | bytes 524304 | tf_op jit(solution)/shard_map/reduce_scatter | solution.py:328
  552.2 54.7 %reduce-scatter.29.cloned.1.call-done = f32[256,512]{1,0:T(8,128)} async-done(((f32[2048,512]{1,0:T(8,128)}), f32[256,512]{1,0:T(8,128)}) %reduce-scatter.29.cloned.1.call-update) | async-done | bytes 524304 | tf_op jit(solution)/shard_map/reduce_scatter | solution.py:329
  606.9 50.1 %reduce-scatter.19.cloned.1.call-done = f32[64,1536]{1,0:T(8,128)} async-done(((f32[512,1536]{1,0:T(8,128)}), f32[64,1536]{1,0:T(8,128)}) %reduce-scatter.19.cloned.1.call-update) | async-done | bytes 393232 | tf_op jit(solution)/shard_map/reduce_scatter | solution.py:321
  657.0 54.6 %reduce-scatter.15.cloned.1.call-done = f32[64,2048]{1,0:T(8,128)} async-done(((f32[512,2048]{1,0:T(8,128)}), f32[64,2048]{1,0:T(8,128)}) %reduce-scatter.15.cloned.1.call-update) | async-done | bytes 524304 | tf_op jit(solution)/shard_map/reduce_scatter | solution.py:318
  711.5 55.1 %reduce-scatter.17.cloned.1.call-done = f32[256,512]{1,0:T(8,128)} async-done(((f32[2048,512]{1,0:T(8,128)}), f32[256,512]{1,0:T(8,128)}) %reduce-scatter.17.cloned.1.call-update) | async-done | bytes 524304 | tf_op jit(solution)/shard_map/reduce_scatter | solution.py:319
  770.4 33.3 %reduce-scatter.31.cloned.1.call-done = f32[64,15]{1,0:T(8,128)} async-done(((f32[512,15]{1,0:T(8,128)}), f32[64,15]{1,0:T(8,128)}) %reduce-scatter.31.cloned.1.call-update) | async-done | bytes 3856
  813.3 24.2 %all-reduce.7 = (f32[512]{0:T(512)S(1)}, f32[512]{0:T(512)S(1)}, f32[512]{0:T(512)S(1)}, f32[512]{0:T(512)S(1)}, f32[512]{0:T(512)S(1)}) all-reduce(f32[512]{0:T(512)S(1)} %get-tuple-element.342, f32[512]{0:T(512)S(1)} %get-tuple-element.340, f32[512]{0:T(512)S(1)} %get-tuple-element.338, ...), channel_id=5, replica_groups=mesh['seq'=8,'rec'=4] {'seq'}, use_global_device_ids=true, to_apply=%region_37.38.clone | all-reduce | flops 2560 | bytes 20480
  837.8 20.6 %all-reduce.8 = (f32[64]{0:T(128)}, f32[64]{0:T(128)}, f32[64]{0:T(128)}, f32[64,15]{0,1:T(8,128)}, f32[64]{0:T(128)}, /*index=5*/f32[64]{0:T(128)}) all-reduce(f32[64]{0:T(128)S(1)} %dynamic-slice.1, f32[64]{0:T(128)S(1)} %dynamic-slice.3, f32[64]{0:T(128)S(1)} %dynamic-slice.5, ...), channel_id=1, replica_groups=mesh['seq'=8,'rec'=4] {'rec'}, use_global_device_ids=true, to_apply=%region_38.39 | all-reduce | flops 1280 | bytes 10240 | tf_op jit(solution)/shard_map/psum | solution.py:332
  858.5 72.3 %all-reduce.12.cloned.1.call-done = (f32[64,320]{1,0:T(8,128)}, f32[64,2048]{1,0:T(8,128)}, f32[256,512]{1,0:T(8,128)}, f32[64,1536]{1,0:T(8,128)}, f32[64,512]{...) async-done(((f32[64,320]{1,0:T(8,128)}, f32[64,2048]{1,0:T(8,128)}, f32[256,512]{1,0:T(8,128)}, ...) | async-done | bytes 3096592 | tf_op jit(solution)/shard_map/psum | solution.py:332
  (490 shorter events, 283.0 us)
Async XLA Ops:
  7.2 181.2 %copy-start = (bf16[512,2048]{1,0:T(8,128)(2,1)S(1)}, bf16[512,2048]{1,0:T(8,128)(2,1)}, u32[]{:S(2)}) copy-start(bf16[512,2048]{1,0:T(8,128)(2,1)} %param.46) | copy-start | bytes 6291460
  7.2 88.7 %all-gather.5.cloned.1.call-start = ((), (), s32[]{:S(2)}) async-start(), calls=%async_computation.19 | async-start | bytes 4718592 | tf_op jit(solution)/shard_map/all_gather | solution.py:21
  52.4 302.3 %all-gather.7.cloned.1.call-start = ((), (), s32[]{:S(2)}) async-start(), calls=%async_computation.20 | async-start | bytes 4718592 | tf_op jit(solution)/shard_map/all_gather | solution.py:21
  72.6 61.0 %copy-start.75 = (f32[512,1]{0,1:T(1,128)}, f32[512,1]{0,1:T(1,128)S(1)}, u32[]{:S(2)}) copy-start(f32[512,1]{0,1:T(1,128)S(1)} %get-tuple-element.425) | copy-start | bytes 6148
  72.6 61.0 %copy-start.77 = (f32[512,1]{0,1:T(1,128)}, f32[512,1]{0,1:T(1,128)S(1)}, u32[]{:S(2)}) copy-start(f32[512,1]{0,1:T(1,128)S(1)} %get-tuple-element.426) | copy-start | bytes 6148
  72.6 61.0 %copy-start.79 = (f32[512,1]{0,1:T(1,128)}, f32[512,1]{0,1:T(1,128)S(1)}, u32[]{:S(2)}) copy-start(f32[512,1]{0,1:T(1,128)S(1)} %get-tuple-element.427) | copy-start | bytes 6148
  72.6 61.0 %copy-start.81 = (f32[512,1]{0,1:T(1,128)}, f32[512,1]{0,1:T(1,128)S(1)}, u32[]{:S(2)}) copy-start(f32[512,1]{0,1:T(1,128)S(1)} %get-tuple-element.428) | copy-start | bytes 6148
  128.0 5.1 collective-permute-start.1
  129.3 3.9 collective-permute-start
  264.5 4.5 collective-permute-start.3
  265.9 3.9 collective-permute-start.2
  296.0 145.1 %reduce-scatter.25.cloned.1.call-start = ((), (), s32[]{:S(2)}) async-start(), calls=%async_computation.16 | async-start | bytes 1179648 | tf_op jit(solution)/shard_map/reduce_scatter | solution.py:326
  299.8 141.4 %reduce-scatter.21.cloned.1.call-start = ((), (), s32[]{:S(2)}) async-start(), calls=%async_computation.14 | async-start | bytes 1179648 | tf_op jit(solution)/shard_map/reduce_scatter | solution.py:322
  331.7 127.1 %reduce-scatter.23.cloned.1.call-start = ((), (), s32[]{:S(2)}) async-start(), calls=%async_computation.15 | async-start | bytes 2359296 | tf_op jit(solution)/shard_map/reduce_scatter | solution.py:324
  354.6 142.5 %reduce-scatter.13.cloned.1.call-start = ((), (), s32[]{:S(2)}) async-start(), calls=%async_computation.10 | async-start | bytes 884736 | tf_op jit(solution)/shard_map/reduce_scatter | solution.py:316
  400.6 151.6 %reduce-scatter.27.cloned.1.call-start = ((), (), s32[]{:S(2)}) async-start(), calls=%async_computation.17 | async-start | bytes 4718592 | tf_op jit(solution)/shard_map/reduce_scatter | solution.py:328
  407.4 199.5 %reduce-scatter.29.cloned.1.call-start = ((), (), s32[]{:S(2)}) async-start(), calls=%async_computation.18 | async-start | bytes 4718592 | tf_op jit(solution)/shard_map/reduce_scatter | solution.py:329
  415.6 241.3 %reduce-scatter.19.cloned.1.call-start = ((), (), s32[]{:S(2)}) async-start(), calls=%async_computation.13 | async-start | bytes 3538944 | tf_op jit(solution)/shard_map/reduce_scatter | solution.py:321
  422.7 288.8 %reduce-scatter.15.cloned.1.call-start = ((), (), s32[]{:S(2)}) async-start(), calls=%async_computation.11 | async-start | bytes 4718592 | tf_op jit(solution)/shard_map/reduce_scatter | solution.py:318
  431.2 335.4 %reduce-scatter.17.cloned.1.call-start = ((), (), s32[]{:S(2)}) async-start(), calls=%async_computation.12 | async-start | bytes 4718592 | tf_op jit(solution)/shard_map/reduce_scatter | solution.py:319
  439.4 327.2 %copy-start.136 = (u32[32]{0:T(128)S(1)}, u32[32]{0:T(128)}, u32[]{:S(2)}) copy-start(u32[32]{0:T(128)} %constant.126) | copy-start | bytes 388
  439.5 365.1 %copy-start.49 = (bf16[512,320]{0,1:T(8,128)(2,1)S(1)}, bf16[512,320]{0,1:T(8,128)(2,1)}, u32[]{:S(2)}) copy-start(bf16[512,320]{0,1:T(8,128)(2,1)} %param.32) | copy-start | bytes 983044
  439.5 364.2 %reduce-scatter.31.cloned.1.call-start = ((), (), s32[]{:S(2)}) async-start(), calls=%async_computation.21 | async-start | bytes 294912
  441.0 489.7 %all-reduce.12.cloned.1.call-start = ((), (), s32[]{:S(2)}) async-start(), calls=%async_computation.22 | async-start | bytes 6225920 | tf_op jit(solution)/shard_map/psum | solution.py:332
  (133 other events, 787.3 us)
Sparse Core Ops, SparseCore 0:
  52.5 39.4 all-gather.4
  296.2 39.8 all-gather.6
  339.3 36.0 reduce-scatter.24
  378.4 35.9 reduce-scatter.20
  417.6 41.1 reduce-scatter.22
  462.1 34.9 reduce-scatter.12
  500.8 51.3 reduce-scatter.26
  555.6 51.2 reduce-scatter.28
  610.6 46.2 reduce-scatter.18
  660.2 51.3 reduce-scatter.14
  715.2 51.3 reduce-scatter.16
  770.1 33.6 reduce-scatter.30
  807.2 123.5 all-reduce.11
where the time goes:
time: 958 us; the launch traced here: 947 us
  waiting for transfers between devices  432 us (45%)
  matrix products  185 us (19%)
  blocking collectives  141 us (15%)
  local copies, waits for them, and re-layouts  97.3 us (10%)
  other arithmetic  64.3 us (7%)
  between operations  16.5 us (2%)
  starting transfers between devices  10 us (1%)
    dot_general x12, matrix products, contract(): return jnp.einsum(formula, tensor_a, tensor_b, precision=highest)  84.1 us
    psum x1, waiting for transfers between devices, local(): lax.psum((shares[0], shares[1], shares[2], shares[3], shares[4], shares[5...  72.3 us
    reduce_scatter x1, waiting for transfers between devices, local(): lax.psum_scatter(ffn1_out_grad, 'seq', scatter_dimension=0, tiled=True)  55.1 us
    reduce_scatter x1, waiting for transfers between devices, local(): lax.psum_scatter(ffn2_in_grad, 'seq', scatter_dimension=0, tiled=True)  55.1 us
    reduce_scatter x1, waiting for transfers between devices, local(): lax.psum_scatter(ffn2_out_grad, 'seq', scatter_dimension=0, tiled=True)  54.7 us
    reduce_scatter x1, waiting for transfers between devices, local(): lax.psum_scatter(ffn1_in_grad, 'seq', scatter_dimension=0, tiled=True)  54.6 us
    reduce_scatter x1, waiting for transfers between devices, local(): lax.psum_scatter(ssm_in_grad, 'seq', scatter_dimension=0, tiled=True)  50.1 us
    dot_general x9, matrix products, dot_outer(): lax.dot_general(matrix_a, matrix_b, (((0,), (0,)), ((), ())), preferred_e...  45.4 us
  transfers between devices with their start and end apart: 17, of which 11 were waited for; matrix products, arithmetic and copies ran while one was open for 19% of the time, Pallas kernels for 0%

commit v1 on v0

--- a/solution.py
+++ b/solution.py
@@ -16,21 +16,92 @@
 highest = lax.Precision.HIGHEST
 
 
-def entering(value, axis, join, neutral, backward):
-    count, mine = (lax.axis_size(axis), lax.axis_index(axis))
-    pieces = jax.tree.map(lambda part: lax.all_gather(part, axis), value)
-    if backward:
-        pieces = jax.tree.map(lambda part: part[::-1], pieces)
-        mine = count - 1 - mine
-    total = jax.tree.map(
-        lambda part, zero: jnp.full_like(part, 0) + jnp.asarray(zero, part.dtype), value, neutral
-    )
-
-    def hop(position, total):
-        longer = join(total, jax.tree.map(lambda part: part[position], pieces))
-        return jax.tree.map(lambda new, old: jnp.where(position < mine, new, old), longer, total)
-
-    return lax.fori_loop(0, count - 1, hop, total)
+def flip_pairs(count, mask):
+    return [(i, i ^ mask) for i in range(count)]
+
+
+def entering(decay, state, backward):
+    count, mine = lax.axis_size("seq"), lax.axis_index("seq")
+    before_decay, before_state = jnp.ones_like(decay), jnp.zeros_like(state)
+    mask = 1
+    while mask < count:
+        pairs = flip_pairs(count, mask)
+        other_decay = lax.ppermute(decay, "seq", pairs)
+        other_state = lax.ppermute(state, "seq", pairs)
+        second = ((mine & mask) != 0) != backward
+        wide, other_wide = decay[:, :, None, None], other_decay[:, :, None, None]
+        before_state = jnp.where(
+            second, before_decay[:, :, None, None] * other_state + before_state, before_state
+        )
+        before_decay = jnp.where(second, before_decay * other_decay, before_decay)
+        state = jnp.where(
+            second, wide * other_state + state, other_wide * state + other_state
+        )
+        decay = decay * other_decay
+        mask *= 2
+    return before_state
+
+
+def sum_over_all(value):
+    count = lax.axis_size("seq") * lax.axis_size("rec")
+    copies = jnp.broadcast_to(value[None], (count,) + value.shape)
+    return jnp.sum(lax.all_to_all(copies, ("rec", "seq"), 0, 0), axis=0)
+
+
+def halve(value, axis, bit, dim):
+    place = lax.axis_index(axis)
+    mine = (place >> bit) & 1
+    sent = lax.dynamic_index_in_dim(value, 1 - mine, dim, keepdims=False)
+    kept = lax.dynamic_index_in_dim(value, mine, dim, keepdims=False)
+    return kept + lax.ppermute(sent, axis, flip_pairs(lax.axis_size(axis), 1 << bit))
+
+
+def scatter_rows(value, parts):
+    count = lax.axis_size("seq")
+    bits = count.bit_length() - 1
+    rows, columns = value.shape
+    split = value.reshape((2,) * bits + (rows // count, columns))
+    split = halve(split, "seq", 0, bits - 1)
+    pieces = []
+    half = (bits - 1) // 2
+    orders = (
+        list(range(1, bits)),
+        list(range(1 + half, bits)) + list(range(1, 1 + half)),
+    )
+    start = 0
+    for part, order in zip(parts, orders):
+        piece = lax.slice_in_dim(split, start, start + part, axis=split.ndim - 1)
+        left = list(range(bits - 1, 0, -1))
+        for bit in order:
+            piece = halve(piece, "seq", bit, left.index(bit))
+            left.remove(bit)
+        pieces.append(piece)
+        start += part
+    return jnp.concatenate(pieces, axis=1)
+
+
+def sum_over_rec(value):
+    count = lax.axis_size("rec")
+    bits = count.bit_length() - 1
+    rows, columns = value.shape
+    piece = value.reshape(rows, count, columns // count).transpose(1, 0, 2)
+    piece = piece.reshape((2,) * bits + (rows, columns // count))
+    place = lax.axis_index("rec")
+    for bit in range(bits):
+        piece = halve(piece, "rec", bit, 0)
+    piece = piece[None]
+    for bit in reversed(range(bits)):
+        other = lax.ppermute(piece, "rec", flip_pairs(count, 1 << bit))
+        mine = (place >> bit) & 1
+        low = jnp.where(mine == 0, piece, other)
+        high = jnp.where(mine == 0, other, piece)
+        piece = jnp.stack([low, high])
+        piece = piece.reshape((-1,) + piece.shape[2:])
+    order = [sum(((i >> k) & 1) << (bits - 1 - k) for k in range(bits)) for i in range(count)]
+    piece = piece.reshape((2,) * bits + (rows, columns // count))
+    piece = piece.reshape(count, rows, columns // count)
+    piece = piece.transpose(1, 0, 2)
+    return piece.reshape(rows, columns)
 
 
 def extended(cells, sides, width):
@@ -67,7 +138,12 @@
 
 
 def contract(formula, tensor_a, tensor_b):
-    return jnp.einsum(formula, tensor_a, tensor_b, precision=highest)
+    return jnp.einsum(
+        formula,
+        tensor_a.astype(jnp.bfloat16),
+        tensor_b.astype(jnp.bfloat16),
+        preferred_element_type=jnp.float32,
+    )
 
 
 def norm_forward(signal, norm_gain):
@@ -111,10 +187,6 @@
         dot_transposed(hidden_low, weight_in), saved_norm, norm_gain
     )
     return (incoming + back_part, gain_grad, in_weight_grad, out_weight_grad)
-
-
-def link_blocks(earlier, later):
-    return (earlier[0] * later[0], later[0][:, :, None, None] * earlier[1] + later[1])
 
 
 def depth_apply(padded, depth_weight, step_count, flipped):
@@ -187,8 +259,10 @@
     log_decay = jnp.log(decays)
     input_scale = jnp.sqrt(-2.0 * log_decay)
     keys_in = by_head(projected[:, 2 * D : 2 * D + width_bc], STATE) * input_scale[..., None]
-    cumulative = jnp.cumsum(log_decay, axis=-1)
     causal = jnp.arange(step_count)[:, None] >= jnp.arange(step_count)[None, :]
+    cumulative = jnp.einsum(
+        "rhs,ts->rht", log_decay, causal.astype(jnp.float32), precision=highest
+    )
     weights = jnp.where(
         causal,
         jnp.exp(jnp.where(causal, cumulative[..., :, None] - cumulative[..., None, :], 0.0)),
@@ -198,9 +272,7 @@
     tail_weight = jnp.exp(cumulative[..., -1:] - cumulative)
     block_decay = keep_here[:, None] * jnp.exp(cumulative[..., -1])
     local_end = contract("rhsn,rhsp->rhnp", keys_in * tail_weight[..., None], attention_contents)
-    identity = (jnp.ones_like(block_decay), jnp.zeros_like(local_end))
-    before = entering((block_decay, local_end), "seq", link_blocks, identity, False)
-    start_state = before[1] * keep_here[:, None, None, None]
+    start_state = entering(block_decay, local_end, False) * keep_here[:, None, None, None]
     scores = contract("rhtn,rhsn->rhts", read_vecs, keys_in) * weights
     reads_start = read_vecs * head_weight[..., None]
     mixed_out = contract("rhts,rhsp->rhtp", scores, attention_contents) + contract(
@@ -224,9 +296,8 @@
     )[:, :, None]
     padded = extended(glu_out, (("seq", 1),), half_span) * rim_keep
     depth_out = depth_apply(padded, conv_depth, step_count, False)
-    batch_statistic_sums = lax.psum(
-        (jnp.sum(depth_out, axis=(0, 1)), jnp.sum(depth_out * depth_out, axis=(0, 1))),
-        ("seq", "rec"),
+    batch_statistic_sums = sum_over_all(
+        jnp.stack([jnp.sum(depth_out, axis=(0, 1)), jnp.sum(depth_out * depth_out, axis=(0, 1))])
     )
     batch_mean = batch_statistic_sums[0] / frame_total
     batch_inv = lax.rsqrt(
@@ -249,9 +320,8 @@
     batch_grad = (dot_transposed(conv_low, conv_out) * silu_slope(batch_out)).reshape(
         row_count, step_count, D
     )
-    back_stats = lax.psum(
-        (jnp.sum(batch_grad * batch_unit, axis=(0, 1)), jnp.sum(batch_grad, axis=(0, 1))),
-        ("seq", "rec"),
+    back_stats = sum_over_all(
+        jnp.stack([jnp.sum(batch_grad * batch_unit, axis=(0, 1)), jnp.sum(batch_grad, axis=(0, 1))])
     )
     depth_grad = (
         bn_gain
@@ -279,10 +349,7 @@
     mixed_grad = by_head(gated_grad * gate_in * gate_sig * STATE ** (-0.5), HEADP)
     gate_grad = gated_grad * mixed_flat * silu_slope(gate_in)
     pulled = contract("rhtn,rhtp->rhnp", reads_start, mixed_grad)
-    from_later = entering(
-        (block_decay, keep_here[:, None, None, None] * pulled), "seq", link_blocks, identity, True
-    )
-    end_grad = from_later[1]
+    end_grad = entering(block_decay, keep_here[:, None, None, None] * pulled, True)
     paired = contract("rhtp,rhsp->rhts", mixed_grad, attention_contents) * weights
     reads_grad = contract("rhts,rhsn->rhtn", paired, keys_in) + head_weight[..., None] * contract(
         "rhtp,rhnp->rhtn", mixed_grad, start_state
@@ -312,63 +379,61 @@
     offset_start = seq_place * share_rows
     bn_gain_grad = lax.dynamic_slice_in_dim(back_stats[0], offset_start, share_rows)
     bn_shift_grad = lax.dynamic_slice_in_dim(back_stats[1], offset_start, share_rows)
-    shares = (
-        lax.psum_scatter(w_sub_grad, "seq", scatter_dimension=0, tiled=True),
-        lax.psum_scatter(ln1_grad, "seq", scatter_dimension=0, tiled=True),
-        lax.psum_scatter(ffn1_in_grad, "seq", scatter_dimension=0, tiled=True),
-        lax.psum_scatter(ffn1_out_grad, "seq", scatter_dimension=0, tiled=True),
-        lax.psum_scatter(ln2_grad, "seq", scatter_dimension=0, tiled=True),
-        lax.psum_scatter(ssm_in_grad, "seq", scatter_dimension=0, tiled=True),
-        lax.psum_scatter(ssm_out_grad, "seq", scatter_dimension=0, tiled=True),
-        lax.psum_scatter(ln3_grad, "seq", scatter_dimension=0, tiled=True),
-        lax.psum_scatter(conv_in_grad, "seq", scatter_dimension=0, tiled=True),
-        lax.psum_scatter(conv_depth_grad, "seq", scatter_dimension=0, tiled=True),
-        lax.psum_scatter(conv_out_grad, "seq", scatter_dimension=0, tiled=True),
-        lax.psum_scatter(ln4_grad, "seq", scatter_dimension=0, tiled=True),
-        lax.psum_scatter(ffn2_in_grad, "seq", scatter_dimension=0, tiled=True),
-        lax.psum_scatter(ffn2_out_grad, "seq", scatter_dimension=0, tiled=True),
-        lax.psum_scatter(ln5_grad, "seq", scatter_dimension=0, tiled=True),
-    )
-    summed = lax.psum(
-        (
-            shares[0],
-            shares[1],
-            shares[2],
-            shares[3],
-            shares[4],
-            shares[5],
-            shares[6],
-            shares[7],
-            shares[8],
-            shares[9],
-            shares[10],
-            shares[11],
-            shares[12],
-            shares[13],
-            shares[14],
-        ),
-        "rec",
-    )
+    def by_share(grad):
+        wide = grad.reshape(block_count, -1, share_rows, grad.shape[1])
+        return wide.transpose(0, 2, 1, 3).reshape(D, -1)
+
+    def from_share(block, columns):
+        wide = block.reshape(share_rows, -1, columns)
+        return wide.transpose(1, 0, 2).reshape(-1, columns)
+
+    small = jnp.concatenate(
+        [
+            jnp.stack([ln1_grad, ln2_grad, ln3_grad, ln4_grad, ln5_grad], axis=1),
+            conv_depth_grad,
+            jnp.zeros((D, 44), jnp.float32),
+        ],
+        axis=1,
+    )
+    group_a = lax.psum_scatter(
+        jnp.concatenate([ffn2_in_grad, by_share(ffn2_out_grad), conv_out_grad], axis=1),
+        "seq",
+        scatter_dimension=0,
+        tiled=True,
+    )
+    group_b = lax.psum_scatter(
+        jnp.concatenate([conv_in_grad, ssm_out_grad, ssm_in_grad], axis=1),
+        "seq",
+        scatter_dimension=0,
+        tiled=True,
+    )
+    group_c = scatter_rows(
+        jnp.concatenate([by_share(ffn1_out_grad), ffn1_in_grad, w_sub_grad, small], axis=1),
+        (2048, 2432),
+    )
+    late = sum_over_rec(jnp.concatenate([group_a, group_b], axis=1))
+    last = sum_over_rec(group_c)
+    gains = last[:, 4416:]
     return (
         result.reshape(row_count, step_count, D).astype(jnp.bfloat16),
         features_grad,
-        summed[0],
-        summed[1],
-        summed[2],
-        summed[3],
-        summed[4],
-        summed[5],
-        summed[6],
-        summed[7],
-        summed[8],
-        summed[9],
+        last[:, 4096:4416],
+        gains[:, 0],
+        last[:, 2048:4096],
+        from_share(last[:, :2048], D),
+        gains[:, 1],
+        late[:, 6144:7680],
+        late[:, 5632:6144],
+        gains[:, 2],
+        late[:, 4608:5632],
+        gains[:, 5 : 5 + KERNEL],
         bn_gain_grad,
         bn_shift_grad,
-        summed[10],
-        summed[11],
-        summed[12],
-        summed[13],
-        summed[14],
+        late[:, 4096:4608],
+        gains[:, 3],
+        late[:, :2048],
+        from_share(late[:, 2048:4096], D),
+        gains[:, 4],
     )
 
 

time: 958 us -> 655 us (0.68)
  waiting for transfers between devices: 432 us -> 182 us
  blocking collectives: 141 us -> 11.9 us
  local copies, waits for them, and re-layouts: 97.3 us -> 177 us
  matrix products: 185 us -> 113 us
  other arithmetic: 64.3 us -> 99.5 us
  starting transfers between devices: 10 us -> 45 us
    reduce_scatter x9 -> x2, waiting for transfers between devices: 325 us -> 0.01 us  [the longest x1 0.01 us: local(): lax.psum_scatter(jnp.concatenate([conv_in_grad, ssm_out_grad, ssm_in_grad...]
    ppermute x0 -> x21, waiting for transfers between devices: none -> 179 us  [the longest x9 81.9 us: halve(): lax.ppermute(sent, axis, flip_pairs(lax.axis_size(axis), 1 << bit))]
    psum x3 -> x0, blocking collectives: 106 us -> none  [the longest x1 43.9 us: local(): lax.psum((jnp.sum(depth_out, axis=(0, 1)), jnp.sum(depth_out * depth_out,...]
    psum x1 -> x0, waiting for transfers between devices: 72.3 us -> none  [local(): lax.psum((shares[0], shares[1], shares[2], shares[3], shares[4], shares[5...]
    dot_general x12 -> x13, matrix products: 84.1 us -> 31.7 us  [the longest x12 30.6 us: contract(): jnp.einsum(formula, tensor_a.astype(jnp.bfloat16), tensor_b.astype(jnp.bf...]
    concatenate x0 -> x22, local copies, waits for them, and re-layouts: none -> 38.5 us  [local(): jnp.concatenate([by_share(ffn1_out_grad), ffn1_in_grad, w_sub_grad, small...]
    unnamed x14 -> x2, waiting for transfers between devices: 33.5 us -> 0.03 us
    ppermute x0 -> x21, starting transfers between devices: none -> 27.8 us  [the longest x9 13.1 us: halve(): lax.ppermute(sent, axis, flip_pairs(lax.axis_size(axis), 1 << bit))]
  transfers between devices with their start and end apart: 17 -> 28, of which waited for: 11 -> 20; matrix products, arithmetic and copies ran while one was open for 19% -> 30% of each run, Pallas kernels for 0% -> 0%
where the time goes in v1:
time: 655 us; the launch traced here: 645 us
  waiting for transfers between devices  182 us (28%)
  local copies, waits for them, and re-layouts  177 us (27%)
  matrix products  113 us (17%)
  other arithmetic  99.5 us (15%)
  starting transfers between devices  45 us (7%)
  between operations  16.8 us (3%)
  blocking collectives  11.9 us (2%)
    ppermute x9, waiting for transfers between devices, halve(): lax.ppermute(sent, axis, flip_pairs(lax.axis_size(axis), 1 << bit))  81.9 us
    ppermute x4, waiting for transfers between devices, sum_over_rec(): other = lax.ppermute(piece, 'rec', flip_pairs(count, 1 << bit))  54.6 us
    unnamed x393, local copies, waits for them, and re-layouts  42.1 us
    concatenate x22, local copies, waits for them, and re-layouts, local(): jnp.concatenate([by_share(ffn1_out_grad), ffn1_in_grad, w_sub_grad, small...  38.5 us
    dot_general x9, matrix products, dot_transposed(): lax.dot_general(matrix_a, matrix_b, (((1,), (1,)), ((), ())), preferred_e...  31.1 us
    dot_general x12, matrix products, contract(): jnp.einsum(formula, tensor_a.astype(jnp.bfloat16), tensor_b.astype(jnp.bf...  30.6 us
    ppermute x6, waiting for transfers between devices, entering(): other_state = lax.ppermute(state, 'seq', pairs)  30.5 us
    dot_general x9, matrix products, dot_outer(): lax.dot_general(matrix_a, matrix_b, (((0,), (0,)), ((), ())), preferred_e...  28.4 us
  transfers between devices with their start and end apart: 28, of which 20 were waited for; matrix products, arithmetic and copies ran while one was open for 30% of the time, Pallas kernels for 0%

profile of v1, /device:TPU:0, one launch (start us, length us, event | category | flops | bytes accessed | tf_op | source)
XLA Modules:
  0.0 644.8 jit_solution(3675515472692298373)
XLA Ops:
  18.3 5.9 multiply_convert_fusion.5
  55.7 5.5 multiply_convert_fusion.4
  72.0 11.7 %collective-permute-done.1 = f32[4,8]{1,0:T(4,128)S(1)} collective-permute-done((f32[4,8]{1,0:T(4,128)S(1)}, f32[4,8]{1,0:T(4,128)S(1)}, u32[]{:S(2)}, u32[]{:S(2)}) %collective-permute-start.1) | collective-permute-done | bytes 160 | tf_op jit(solution)/shard_map/ppermute | solution.py:29
  88.8 10.7 %collective-permute-done.4 = f32[4,8,32,64]{3,2,1,0:T(8,128)} collective-permute-done((f32[4,8,32,64]{3,2,1,0:T(8,128)}, f32[4,8,32,64]{3,2,1,0:T(8,128)}, u32[]{:S(2)}, u32[]{:S(2)}) %collective-permute-start.4) | collective-permute-done | bytes 262176 | tf_op jit(solution)/shard_map/ppermute | solution.py:30
  134.0 8.1 %all-to-all-start = ((f32[32,2,512]{2,1,0:T(2,128)}), f32[32,2,512]{2,1,0:T(2,128)S(1)}, u32[]{:S(2)}, u32[]{:S(2)}) async-start(f32[32,2,512]{2,1,0:T(2,128)} %broadcast_in_dim.70), calls=%async_computation | async-start | bytes 262144 | tf_op jit(solution)/shard_map/all_to_all | solution.py:48
  180.7 11.9 %all_to_all.10 = f32[32,2,512]{2,1,0:T(2,128)} all-to-all(f32[32,2,512]{2,1,0:T(2,128)S(1)} %broadcast_in_dim.71), channel_id=1, replica_groups=mesh['seq'=8,'rec'=4] {'rec','seq'}, dimensions={0} | all-to-all | bytes 262144 | tf_op jit(solution)/shard_map/all_to_all | solution.py:48
  195.0 6.7 %multiply_reduce_fusion = (f32[512]{0:T(512)}, f32[512]{0:T(512)}, f32[512]{0:T(512)}, f32[512]{0:T(512)}, f32[512]{0:T(512)}, /*index=5*/f32[512]{0:T(512)}, f3...) fusion(f32[4,270,512]{2,1,0:T(8,128)S(1)} %copy-done.3, ...), kind=kLoop, calls=%fused_computation.74 | loop fusion | flops 19390976 | bytes 37789696 | tf_op jit(solution)/shard_map/reduce_sum | solution.py:333
  219.8 5.1 multiply_convert_fusion.9
  252.9 9.8 %collective-permute-done.10 = f32[4,8,32,64]{3,2,1,0:T(8,128)S(1)} collective-permute-done((f32[4,8,32,64]{3,2,1,0:T(8,128)S(1)}, f32[4,8,32,64]{3,2,1,0:T(8,128)S(1)}, u32[]{:S(2)}, u32[]{:S(2)}) %collective-permute-start.10) | collective-permute-done | bytes 262176 | tf_op jit(solution)/shard_map/ppermute | solution.py:30
  267.2 9.9 %collective-permute-done.11 = f32[4,8,32,64]{3,2,1,0:T(8,128)S(1)} collective-permute-done((f32[4,8,32,64]{3,2,1,0:T(8,128)S(1)}, f32[4,8,32,64]{3,2,1,0:T(8,128)S(1)}, u32[]{:S(2)}, u32[]{:S(2)}) %collective-permute-start.11) | collective-permute-done | bytes 262176 | tf_op jit(solution)/shard_map/ppermute | solution.py:30
  301.5 5.9 fusion.72
  320.5 8.9 %pad_maximum_fusion = f32[512,4608]{1,0:T(8,128)} fusion(f32[512,512]{1,0:T(8,128)S(1)} %fusion.65, f32[512,2048]{1,0:T(8,128)} %bitcast.335, f32[512,2048]{1,0:T(8,128)} %fusion.103), kind=kLoop, calls=%fused_computation | loop fusion | flops 4718592 | bytes 18874368 | tf_op jit(solution)/shard_map/concatenate | solution.py:399
  354.0 6.4 multiply_convert_fusion
  369.4 6.8 %concatenate.78 = f32[2,2,2,64,2048]{4,3,2,1,0:T(8,128)} reshape(f32[8,64,4,512]{3,2,1,0:T(4,128)} %bitcast.334) | data formatting | bytes 8388608 | tf_op jit(solution)/shard_map/concatenate | solution.py:411
  387.4 13.3 %concatenate.100 = f32[2,2,2,64,4480]{4,3,2,1,0:T(8,128)} concatenate(f32[2,2,2,64,2048]{4,3,2,1,0:T(8,128)} %concatenate.78, f32[2,2,2,64,2048]{4,3,2,1,0:T(8,128)} %bitcast.355, f32[2,2,2,64,320]{4,3,2,1,0:T(8,128)} %fusion.49, f32[2,2,2,64,1]{4,3,2,1,0:T(8,128)} %concatenate.105, f32[2,2,2,64,1]{4,3,2,1,0:T(8,128)} %concatenate.106, f32[2,2,2,64,1]{4,3,2,1,0:T(8,128)} %concatenate.107, ...), dimensions={4} | concatenate | bytes 18350080 | tf_op jit(solution)/shard_map/concatenate | solution.py:411
  405.8 8.1 %collective-permute-done.12 = f32[2,2,64,4480]{3,2,1,0:T(8,128)} collective-permute-done((f32[2,2,64,4480]{3,2,1,0:T(8,128)}, f32[2,2,64,4480]{3,2,1,0:T(8,128)}, u32[]{:S(2)}, u32[]{:S(2)}) %collective-permute-start.12) | collective-permute-done | bytes 4587552 | tf_op jit(solution)/shard_map/ppermute | solution.py:56
  413.8 6.4 bitcast_add_fusion
  430.3 30.2 %collective-permute-done.13 = f32[2,64,2048]{2,1,0:T(8,128)} collective-permute-done((f32[2,64,2048]{2,1,0:T(8,128)}, f32[2,64,2048]{2,1,0:T(8,128)}, u32[]{:S(2)}, u32[]{:S(2)}) %collective-permute-start.13) | collective-permute-done | bytes 1048608 | tf_op jit(solution)/shard_map/ppermute | solution.py:56
  468.7 8.3 %collective-permute-done.14 = f32[64,2048]{1,0:T(8,128)} collective-permute-done((f32[64,2048]{1,0:T(8,128)}, f32[64,2048]{1,0:T(8,128)}, u32[]{:S(2)}, u32[]{:S(2)}) %collective-permute-start.14) | collective-permute-done | bytes 524320 | tf_op jit(solution)/shard_map/ppermute | solution.py:56
  493.1 9.1 %collective-permute-done.17 = f32[2,64,1120]{2,1,0:T(8,128)S(1)} collective-permute-done((f32[2,64,1120]{2,1,0:T(8,128)}, f32[2,64,1120]{2,1,0:T(8,128)S(1)}, u32[]{:S(2)}, u32[]{:S(2)}) %collective-permute-start.17) | collective-permute-done | bytes 573472 | tf_op jit(solution)/shard_map/ppermute | solution.py:56
  524.0 17.3 %collective-permute-done.19 = f32[1,64,1120]{2,1,0:T(8,128)} collective-permute-done((f32[1,64,1120]{2,1,0:T(8,128)}, f32[1,64,1120]{2,1,0:T(8,128)}, u32[]{:S(2)}, u32[]{:S(2)}) %collective-permute-start.19) | collective-permute-done | bytes 286752 | tf_op jit(solution)/shard_map/ppermute | solution.py:94
  559.1 15.3 %collective-permute-done.22 = f32[64,1920]{1,0:T(8,128)} collective-permute-done((f32[64,1920]{1,0:T(8,128)}, f32[64,1920]{1,0:T(8,128)}, u32[]{:S(2)}, u32[]{:S(2)}) %collective-permute-start.22) | collective-permute-done | bytes 491552 | tf_op jit(solution)/shard_map/ppermute | solution.py:56
  578.6 21.2 %collective-permute-done.23 = f32[1,64,1920]{2,0,1:T(1,128)S(1)} collective-permute-done((f32[1,64,1920]{2,0,1:T(1,128)S(1)}, f32[1,64,1920]{2,0,1:T(1,128)S(1)}, u32[]{:S(2)}, u32[]{:S(2)}) %collective-permute-start.23) | collective-permute-done | bytes 491552 | tf_op jit(solution)/shard_map/ppermute | solution.py:94
  611.4 14.6 %collective-permute-done.24 = f32[2,64,1920]{2,0,1:T(2,128)} collective-permute-done((f32[2,64,1920]{2,0,1:T(2,128)}, f32[2,64,1920]{2,0,1:T(2,128)}, u32[]{:S(2)}, u32[]{:S(2)}) %collective-permute-start.24) | collective-permute-done | bytes 983072 | tf_op jit(solution)/shard_map/ppermute | solution.py:94
  (641 shorter events, 371.0 us)
Async XLA Ops:
  46.9 19.2 %collective-permute-start.2 = (f32[4,8,32,64]{3,2,1,0:T(8,128)}, f32[4,8,32,64]{3,2,1,0:T(8,128)}, u32[]{:S(2)}, u32[]{:S(2)}) collective-permute-start(f32[4,8,32,64]{3,2,1,0:T(8,128)} %fusion.43), channel_id=1, source_target_pairs={{0,4},{4,0},{8,12},{12,8},{16,20},{20,16},{24,28},{28,24},{1,5},{5... | collective-permute-start | bytes 786440 | tf_op jit(solution)/shard_map/ppermute | solution.py:30
  48.1 18.0 %collective-permute-start = (f32[4,8]{1,0:T(4,128)S(1)}, f32[4,8]{1,0:T(4,128)S(1)}, u32[]{:S(2)}, u32[]{:S(2)}) collective-permute-start(f32[4,8]{1,0:T(4,128)S(1)} %exponential_multiply_fusion), channel_id=1, source_target_pairs={{0,4},{4,0},{8,12},{12,8},{16,20},{20,16},{24,28},{28,24},{1,5},{5... | collective-permute-start | bytes 392 | tf_op jit(solution)/shard_map/ppermute | solution.py:29
  68.3 15.4 %collective-permute-start.3 = (f32[4,8,32,64]{3,2,1,0:T(8,128)}, f32[4,8,32,64]{3,2,1,0:T(8,128)}, u32[]{:S(2)}, u32[]{:S(2)}) collective-permute-start(f32[4,8,32,64]{3,2,1,0:T(8,128)} %add_select_fusion.7), channel_id=1, source_target_pairs={{0,8},{4,12},{8,0},{12,4},{16,24},{20,28},{24,16},{28,20},{1,9},{5... | collective-permute-start | bytes 786440 | tf_op jit(solution)/shard_map/ppermute | solution.py:30
  72.0 11.7 %collective-permute-start.1 = (f32[4,8]{1,0:T(4,128)S(1)}, f32[4,8]{1,0:T(4,128)S(1)}, u32[]{:S(2)}, u32[]{:S(2)}) collective-permute-start(f32[4,8]{1,0:T(4,128)S(1)} %fusion.165), channel_id=1, source_target_pairs={{0,8},{4,12},{8,0},{12,4},{16,24},{20,28},{24,16},{28,20},{1,9},{5... | collective-permute-start | bytes 392 | tf_op jit(solution)/shard_map/ppermute | solution.py:29
  85.9 13.7 %collective-permute-start.4 = (f32[4,8,32,64]{3,2,1,0:T(8,128)}, f32[4,8,32,64]{3,2,1,0:T(8,128)}, u32[]{:S(2)}, u32[]{:S(2)}) collective-permute-start(f32[4,8,32,64]{3,2,1,0:T(8,128)} %add_select_fusion.6), channel_id=1, source_target_pairs={{0,16},{4,20},{8,24},{12,28},{16,0},{20,4},{24,8},{28,12},{1,17},{... | collective-permute-start | bytes 786440 | tf_op jit(solution)/shard_map/ppermute | solution.py:30
  134.0 16.3 %all-to-all-start = ((f32[32,2,512]{2,1,0:T(2,128)}), f32[32,2,512]{2,1,0:T(2,128)S(1)}, u32[]{:S(2)}, u32[]{:S(2)}) async-start(f32[32,2,512]{2,1,0:T(2,128)} %broadcast_in_dim.70), calls=%async_computation | async-start | bytes 262144 | tf_op jit(solution)/shard_map/all_to_all | solution.py:48
  142.1 364.1 %reduce-scatter.5.cloned.1.call-start = ((), (), s32[]{:S(2)}) async-start(), calls=%async_computation.5 | async-start | bytes 7077888 | tf_op jit(solution)/shard_map/reduce_scatter | solution.py:404
  241.2 6.5 %collective-permute-start.9 = (f32[4,8,32,64]{3,2,1,0:T(8,128)}, f32[4,8,32,64]{3,2,1,0:T(8,128)S(1)}, u32[]{:S(2)}, u32[]{:S(2)}) collective-permute-start(f32[4,8,32,64]{3,2,1,0:T(8,128)} %convolution_multiply_fusion), channel_id=1, source_target_pairs={{0,4},{4,0},{8,12},{12,8},{16,20},{20,16},{24,28},{28,24},{1,5},{5... | collective-permute-start | bytes 786440 | tf_op jit(solution)/shard_map/ppermute | solution.py:30
  247.8 14.9 %collective-permute-start.10 = (f32[4,8,32,64]{3,2,1,0:T(8,128)S(1)}, f32[4,8,32,64]{3,2,1,0:T(8,128)S(1)}, u32[]{:S(2)}, u32[]{:S(2)}) collective-permute-start(f32[4,8,32,64]{3,2,1,0:T(8,128)S(1)} %add_select_fusion.5), channel_id=1, source_target_pairs={{0,8},{4,12},{8,0},{12,4},{16,24},{20,28},{24,16},{28,20},{1,9},{5... | collective-permute-start | bytes 786440 | tf_op jit(solution)/shard_map/ppermute | solution.py:30
  262.9 14.1 %collective-permute-start.11 = (f32[4,8,32,64]{3,2,1,0:T(8,128)S(1)}, f32[4,8,32,64]{3,2,1,0:T(8,128)S(1)}, u32[]{:S(2)}, u32[]{:S(2)}) collective-permute-start(f32[4,8,32,64]{3,2,1,0:T(8,128)S(1)} %add_select_fusion.4), channel_id=1, source_target_pairs={{0,16},{4,20},{8,24},{12,28},{16,0},{20,4},{24,8},{28,12},{1,17},{... | collective-permute-start | bytes 786440 | tf_op jit(solution)/shard_map/ppermute | solution.py:30
  299.0 207.2 %reduce-scatter.3.cloned.1.call-start = ((), (), s32[]{:S(2)}) async-start(), calls=%async_computation.4 | async-start | bytes 10616832 | tf_op jit(solution)/shard_map/reduce_scatter | solution.py:398
  405.8 8.1 %collective-permute-start.12 = (f32[2,2,64,4480]{3,2,1,0:T(8,128)}, f32[2,2,64,4480]{3,2,1,0:T(8,128)}, u32[]{:S(2)}, u32[]{:S(2)}) collective-permute-start(f32[2,2,64,4480]{3,2,1,0:T(8,128)} %dynamic-slice_bitcast_fusion), channel_id=1, source_target_pairs={{0,4},{4,0},{8,12},{12,8},{16,20},{20,16},{24,28},{28,24},{1,5},{5... | collective-permute-start | bytes 13762568 | tf_op jit(solution)/shard_map/ppermute | solution.py:56
  424.5 36.0 %collective-permute-start.13 = (f32[2,64,2048]{2,1,0:T(8,128)}, f32[2,64,2048]{2,1,0:T(8,128)}, u32[]{:S(2)}, u32[]{:S(2)}) collective-permute-start(f32[2,64,2048]{2,1,0:T(8,128)} %dynamic-slice_bitcast_fusion.2), channel_id=1, source_target_pairs={{0,8},{4,12},{8,0},{12,4},{16,24},{20,28},{24,16},{28,20},{1,9},{5... | collective-permute-start | bytes 3145736 | tf_op jit(solution)/shard_map/ppermute | solution.py:56
  429.2 35.5 %collective-permute-start.15 = (f32[2,64,2432]{2,1,0:T(8,128)}, f32[2,64,2432]{2,1,0:T(8,128)}, u32[]{:S(2)}, u32[]{:S(2)}) collective-permute-start(f32[2,64,2432]{2,1,0:T(8,128)} %dynamic-slice_bitcast_fusion.1), channel_id=1, source_target_pairs={{0,16},{4,20},{8,24},{12,28},{16,0},{20,4},{24,8},{28,12},{1,17},{... | collective-permute-start | bytes 3735560 | tf_op jit(solution)/shard_map/ppermute | solution.py:56
  463.1 14.0 %collective-permute-start.14 = (f32[64,2048]{1,0:T(8,128)}, f32[64,2048]{1,0:T(8,128)}, u32[]{:S(2)}, u32[]{:S(2)}) collective-permute-start(f32[64,2048]{1,0:T(8,128)} %dynamic-slice_bitcast_fusion.5), channel_id=1, source_target_pairs={{0,16},{4,20},{8,24},{12,28},{16,0},{20,4},{24,8},{28,12},{1,17},{... | collective-permute-start | bytes 1572872 | tf_op jit(solution)/shard_map/ppermute | solution.py:56
  467.2 15.7 %collective-permute-start.16 = (f32[64,2432]{1,0:T(8,128)S(1)}, f32[64,2432]{1,0:T(8,128)S(1)}, u32[]{:S(2)}, u32[]{:S(2)}) collective-permute-start(f32[64,2432]{1,0:T(8,128)S(1)} %dynamic-slice_bitcast_fusion.4), channel_id=1, source_target_pairs={{0,8},{4,12},{8,0},{12,4},{16,24},{20,28},{24,16},{28,20},{1,9},{5... | collective-permute-start | bytes 1867784 | tf_op jit(solution)/shard_map/ppermute | solution.py:56
  487.7 14.5 %collective-permute-start.17 = (f32[2,64,1120]{2,1,0:T(8,128)}, f32[2,64,1120]{2,1,0:T(8,128)S(1)}, u32[]{:S(2)}, u32[]{:S(2)}) collective-permute-start(f32[2,64,1120]{2,1,0:T(8,128)} %bitcast.326), channel_id=1, source_target_pairs={{0,1},{1,0},{2,3},{3,2},{4,5},{5,4},{6,7},{7,6},{8,9},{9,8},{10,11... | collective-permute-start | bytes 1720328 | tf_op jit(solution)/shard_map/ppermute | solution.py:56
  503.8 14.6 %collective-permute-start.18 = (f32[64,1120]{1,0:T(8,128)}, f32[64,1120]{1,0:T(8,128)}, u32[]{:S(2)}, u32[]{:S(2)}) collective-permute-start(f32[64,1120]{1,0:T(8,128)} %dynamic-slice_bitcast_fusion.6), channel_id=1, source_target_pairs={{0,2},{1,3},{2,0},{3,1},{4,6},{5,7},{6,4},{7,5},{8,10},{9,11},{10,... | collective-permute-start | bytes 860168 | tf_op jit(solution)/shard_map/ppermute | solution.py:56
  513.9 31.8 %collective-permute-start.21 = (f32[2,64,1920]{2,0,1:T(2,128)}, f32[2,64,1920]{2,0,1:T(2,128)}, u32[]{:S(2)}, u32[]{:S(2)}) collective-permute-start(f32[2,64,1920]{2,0,1:T(2,128)} %dynamic-slice_bitcast_fusion.3), channel_id=1, source_target_pairs={{0,1},{1,0},{2,3},{3,2},{4,5},{5,4},{6,7},{7,6},{8,9},{9,8},{10,11... | collective-permute-start | bytes 2949128 | tf_op jit(solution)/shard_map/ppermute | solution.py:56
  520.1 21.1 %collective-permute-start.19 = (f32[1,64,1120]{2,1,0:T(8,128)}, f32[1,64,1120]{2,1,0:T(8,128)}, u32[]{:S(2)}, u32[]{:S(2)}) collective-permute-start(f32[1,64,1120]{2,1,0:T(8,128)} %fusion.74), channel_id=1, source_target_pairs={{0,2},{1,3},{2,0},{3,1},{4,6},{5,7},{6,4},{7,5},{8,10},{9,11},{10,... | collective-permute-start | bytes 860168 | tf_op jit(solution)/shard_map/ppermute | solution.py:94
  549.4 25.0 %collective-permute-start.22 = (f32[64,1920]{1,0:T(8,128)}, f32[64,1920]{1,0:T(8,128)}, u32[]{:S(2)}, u32[]{:S(2)}) collective-permute-start(f32[64,1920]{1,0:T(8,128)} %bitcast.328), channel_id=1, source_target_pairs={{0,2},{1,3},{2,0},{3,1},{4,6},{5,7},{6,4},{7,5},{8,10},{9,11},{10,... | collective-permute-start | bytes 1474568 | tf_op jit(solution)/shard_map/ppermute | solution.py:56
  551.6 25.8 %collective-permute-start.20 = (f32[2,64,1120]{2,1,0:T(8,128)}, f32[2,64,1120]{2,1,0:T(8,128)}, u32[]{:S(2)}, u32[]{:S(2)}) collective-permute-start(f32[2,64,1120]{2,1,0:T(8,128)} %maximum_bitcast_fusion.1), channel_id=1, source_target_pairs={{0,1},{1,0},{2,3},{3,2},{4,5},{5,4},{6,7},{7,6},{8,9},{9,8},{10,11... | collective-permute-start | bytes 1720328 | tf_op jit(solution)/shard_map/ppermute | solution.py:94
  575.8 23.9 %collective-permute-start.23 = (f32[1,64,1920]{2,0,1:T(1,128)S(1)}, f32[1,64,1920]{2,0,1:T(1,128)S(1)}, u32[]{:S(2)}, u32[]{:S(2)}) collective-permute-start(f32[1,64,1920]{2,0,1:T(1,128)S(1)} %broadcast_in_dim.74), channel_id=1, source_target_pairs={{0,2},{1,3},{2,0},{3,1},{4,6},{5,7},{6,4},{7,5},{8,10},{9,11},{10,... | collective-permute-start | bytes 1474568 | tf_op jit(solution)/shard_map/ppermute | solution.py:94
  602.3 23.6 %collective-permute-start.24 = (f32[2,64,1920]{2,0,1:T(2,128)}, f32[2,64,1920]{2,0,1:T(2,128)}, u32[]{:S(2)}, u32[]{:S(2)}) collective-permute-start(f32[2,64,1920]{2,0,1:T(2,128)} %maximum_bitcast_fusion), channel_id=1, source_target_pairs={{0,1},{1,0},{2,3},{3,2},{4,5},{5,4},{6,7},{7,6},{8,9},{9,8},{10,11... | collective-permute-start | bytes 2949128 | tf_op jit(solution)/shard_map/ppermute | solution.py:94
  (195 other events, 1453.1 us)
Sparse Core Ops, SparseCore 0:
  299.1 59.9 reduce-scatter.4
  363.0 86.8 reduce-scatter.2

commit v2 on v0

v2 whole, which is shorter than its diff:
```python
import jax
import jax.numpy as jnp
from jax import lax
from jax.experimental import pallas as pl
from jax.experimental.pallas import tpu as pltpu
from jax.sharding import PartitionSpec as P

D = 512
FF = 2048
HEADS = 8
STATE = 32
SUB = 4
KERNEL = 15
HEADP = 64
PROJ = 1536
WIDE = 512
EPS = 1e-05
F32 = jnp.float32
BF16 = jnp.bfloat16
LIMIT = 56
READ_SCALE = STATE ** (-0.5)


def dot(a, b):
    return lax.dot_general(a, b, (((1,), (0,)), ((), ())), preferred_element_type=F32)


def dot_t(a, b):
    return lax.dot_general(a, b, (((1,), (1,)), ((), ())), preferred_element_type=F32)


def t_dot(a, b):
    return lax.dot_general(a, b, (((0,), (0,)), ((), ())), preferred_element_type=F32)


def sigmoid(x):
    return 0.5 * jnp.tanh(0.5 * x) + 0.5


def mean(x):
    return jnp.mean(x, axis=-1, keepdims=True)


def norm(x, gain):
    centred = x - mean(x)
    scale = lax.rsqrt(mean(centred * centred) + EPS)
    return (centred * scale * gain).astype(BF16), scale


def norm_back(grad, normed, scale, gain):
    wide = normed.astype(F32)
    inverse = 1.0 / gain
    both = grad * wide
    inner = grad * gain
    back = scale * (inner - mean(inner) - wide * inverse * mean(both))
    return back, jnp.sum(both, axis=0, keepdims=True) * inverse


def split_two(x):
    high = x.astype(BF16)
    return high, (x - high.astype(F32)).astype(BF16)


def split_three(x):
    high, rest = split_two(x)
    return high, rest, (x - high.astype(F32) - rest.astype(F32)).astype(BF16)


def iota(shape, dim):
    return lax.broadcasted_iota(jnp.int32, shape, dim)


def lane_mask(columns, width, index):
    lane = iota((16, columns), 1)
    inside = (lane >= width * index) & (lane < width * (index + 1))
    return jnp.where(inside, 1.0, 0.0).astype(BF16)[:1]


def pack_state(full):
    lane = iota((STATE, 128), 1)
    return [
        jnp.where(
            lane < HEADP,
            full[64 * a : 64 * a + 32, 128 * a : 128 * a + 128],
            full[64 * a + 32 : 64 * a + 64, 128 * a : 128 * a + 128],
        )
        for a in range(4)
    ]


def unpack_state(ref, full):
    lane = iota((STATE, 128), 1)
    full[...] = jnp.zeros_like(full)
    for a in range(4):
        pair = ref[0, a, :STATE, :]
        full[64 * a : 64 * a + 32, 128 * a : 128 * a + 128] = jnp.where(
            lane < HEADP, pair, 0.0
        ).astype(BF16)
        full[64 * a + 32 : 64 * a + 64, 128 * a : 128 * a + 128] = jnp.where(
            lane < HEADP, 0.0, pair
        ).astype(BF16)


def accumulate(ref, value):
    first = pl.program_id(0) == 0

    @pl.when(first)
    def _():
        ref[...] = value

    @pl.when(jnp.logical_not(first))
    def _():
        ref[...] += value


def front_kernel(
    feat, tk, fk, dec, dec_t, keep, w_sub, g1, w1, w2, g2, w_in,
    flat, x1, a1, r1, s1, d1, a2, r2, u, g, bs, c, ce, bt, se, ee, te, cum, cum_t, state,
    frames,
):
    steps = x1.shape[1]
    frames[...] = feat[0].astype(F32)
    parts = [
        frames[pl.ds(j, steps, stride=SUB), :] * (tk[0][:, j : j + 1] * fk[0]) for j in range(SUB)
    ]
    parts.append(jnp.zeros((steps, WIDE - SUB * parts[0].shape[1]), F32))
    stacked = jnp.concatenate(parts, axis=1).astype(BF16)
    flat[0] = stacked
    x0 = dot(stacked, w_sub[...])
    low, scale = norm(x0, g1[...])
    a1[0] = low
    r1[0] = scale
    total = jnp.zeros((steps, D), F32)
    for at in range(0, FF, D):
        hidden = dot(low, w1[:, at : at + D])
        gate = sigmoid(hidden)
        active = hidden * gate
        d1[0, :, at : at + D] = (gate * (1.0 + hidden - active)).astype(BF16)
        active = active.astype(BF16)
        s1[0, :, at : at + D] = active
        total += dot(active, w2[at : at + D, :])
    after = x0 + 0.5 * total
    x1[0] = after
    low, scale = norm(after, g2[...])
    a2[0] = low
    r2[0] = scale
    u_low = dot(low, w_in[:, :D]).astype(BF16)
    u[0] = u_low
    g[0] = dot(low, w_in[:, D : 2 * D]).astype(BF16)
    keys = dot(low, w_in[:, 2 * D : 2 * D + 256])
    reads = dot(low, w_in[:, 2 * D + 256 :])
    log_decay = jnp.log(dec_t[0])
    lower = jnp.where(iota((steps, steps), 0) >= iota((steps, steps), 1), 1.0, 0.0).astype(BF16)
    running = sum(dot(lower, part) for part in split_three(log_decay))
    running_t = sum(dot_t(part, lower) for part in split_three(jnp.log(dec[0])))
    cum[0] = running
    cum_t[0] = running_t
    spread = jnp.where(iota((HEADS, 256), 1) // STATE == iota((HEADS, 256), 0), 1.0, 0.0).astype(BF16)

    def over_columns(value):
        return sum(dot(part, spread) for part in split_two(value))

    scale_wide = over_columns(jnp.sqrt(-2.0 * log_decay))
    head = jnp.exp(running)
    head_wide = over_columns(head)
    tail_wide = over_columns(jnp.exp(running[steps - 1 :, :] - running))
    se[0] = scale_wide.astype(BF16)
    ee[0] = head_wide.astype(BF16)
    te[0] = tail_wide.astype(BF16)
    keys = keys * scale_wide
    bs[0] = keys.astype(BF16)
    c[0] = reads.astype(BF16)
    ce[0] = (reads * head_wide).astype(BF16)
    tailed = (keys * tail_wide).astype(BF16)
    bt[0] = tailed
    spread_values = jnp.where(iota((HEADS, D), 1) // HEADP == iota((HEADS, D), 0), 1.0, 0.0).astype(BF16)
    block = sum(dot(part, spread_values) for part in split_three(head[steps - 8 :, :]))
    block = block[7:8, :] * keep[0, pl.program_id(0)]
    for a, pair in enumerate(pack_state(t_dot(tailed, u_low))):
        state[0, a, :STATE, :] = pair
        state[0, a, STATE:, :] = jnp.broadcast_to(block[:, 128 * a : 128 * a + 128], (8, 128))


def mix_kernel(u, bs, c, cum, cum_t, mixed, pairs, decay_pairs):
    steps = u.shape[1]
    causal = iota((steps, steps), 0) >= iota((steps, steps), 1)
    keys = bs[0]
    reads = c[0]
    for q in range(2):
        values = u[0, :, 256 * q : 256 * q + 256]
        total = jnp.zeros((steps, 256), F32)
        for b in range(4):
            h = 4 * q + b
            weights = jnp.exp(
                jnp.where(causal, cum[0, :, h : h + 1] - cum_t[0, h : h + 1, :], -1e30)
            )
            scores = (dot_t(reads * lane_mask(256, STATE, h), keys) * weights).astype(BF16)
            decay_pairs[0, h] = weights.astype(BF16)
            pairs[0, h] = scores
            total += dot(scores, values * lane_mask(256, HEADP, b))
        mixed[0, :, 256 * q : 256 * q + 256] = total


def lift_kernel(
    mixed, ce, start, g, x1, w_out, g3, w_conv,
    z, gs, yd, x2, a3, r3, v, sq, cq, top, bottom,
    full,
):
    steps = x1.shape[1]
    unpack_state(start, full)
    y = (mixed[0] + dot(ce[0], full[...])) * READ_SCALE
    gate = g[0].astype(F32)
    sig = sigmoid(gate)
    active = gate * sig
    gs[0] = (active * READ_SCALE).astype(BF16)
    yd[0] = (y * sig * (1.0 + gate - active)).astype(BF16)
    gated = (y * active).astype(BF16)
    z[0] = gated
    after = x1[0] + dot(gated, w_out[...])
    x2[0] = after
    low, scale = norm(after, g3[...])
    a3[0] = low
    r3[0] = scale
    first = dot(low, w_conv[:, :D])
    sig = sigmoid(dot(low, w_conv[:, D:]))
    out = first * sig
    v[0] = out
    sq[0] = sig.astype(BF16)
    cq[0] = (out * (1.0 - sig)).astype(BF16)
    top[0] = out[:8, :]
    bottom[0] = out[steps - 8 :, :]


def fill_padded(padded, body, before, after, keep):
    steps = body.shape[1]
    row = pl.program_id(0)
    for i in range(D // 128):
        columns = slice(128 * i, 128 * i + 128)
        padded[i, :8, :] = before[0, :, columns] * keep[0, row]
        padded[i, 8 : 8 + steps, :] = body[0, :, columns]
        padded[i, 8 + steps :, :] = after[0, :, columns] * keep[1, row]


def depth_kernel(v, before, after, keep, taps, dc, sums, padded):
    steps = v.shape[1]
    fill_padded(padded, v, before, after, keep)
    total, square = [], []
    for at in range(0, D, 128):
        running = jnp.zeros((steps, 128), F32)
        for k in range(KERNEL):
            running += padded[at // 128, k + 1 : k + 1 + steps, :] * taps[k : k + 1, at : at + 128]
        dc[0, :, at : at + 128] = running
        total.append(jnp.sum(running, axis=0, keepdims=True))
        square.append(jnp.sum(running * running, axis=0, keepdims=True))
    accumulate(sums, jnp.concatenate([jnp.concatenate(total, axis=1), jnp.concatenate(square, axis=1)], axis=0))


def batch_stats(stats, count):
    middle = stats[0:1, :] / count
    return middle, lax.rsqrt(stats[1:2, :] / count - middle * middle + EPS)


def late_kernel(count):
    def kernel(
        dc, x2, og, stats, bn_gain, bn_shift, w_conv, g4, w3, w4, g5,
        out, e, a4, s4, gf, gh, ge, gx3, gbn, sums, ln4, ln5,
        slope,
    ):
        middle, inv = batch_stats(stats, count)
        unit = (dc[0] - middle) * inv
        batch = unit * bn_gain[...] + bn_shift[...]
        sig = sigmoid(batch)
        active = batch * sig
        conv_slope = sig * (1.0 + batch - active)
        active = active.astype(BF16)
        e[0] = active
        x3 = x2[0] + dot(active, w_conv[...])
        low, scale4 = norm(x3, g4[...])
        a4[0] = low
        total = jnp.zeros_like(x3)
        for at in range(0, FF, D):
            hidden = dot(low, w3[:, at : at + D])
            gate = sigmoid(hidden)
            active = hidden * gate
            slope[:, at : at + D] = (gate * (1.0 + hidden - active)).astype(BF16)
            active = active.astype(BF16)
            s4[0, :, at : at + D] = active
            total += dot(active, w4[at : at + D, :])
        x4 = x3 + 0.5 * total
        centred = x4 - mean(x4)
        scale = lax.rsqrt(mean(centred * centred) + EPS)
        unit5 = centred * scale
        out[0] = (unit5 * g5[...]).astype(BF16)
        grad = og[0].astype(F32)
        both = grad * unit5
        inner = grad * g5[...]
        accumulate(ln5, jnp.sum(both, axis=0, keepdims=True))
        gx4 = scale * (inner - mean(inner) - unit5 * mean(inner * unit5))
        gf_low = (0.5 * gx4).astype(BF16)
        gf[0] = gf_low
        back = jnp.zeros_like(x3)
        for at in range(0, FF, D):
            hidden = (dot_t(gf_low, w4[at : at + D, :]) * slope[:, at : at + D].astype(F32)).astype(BF16)
            gh[0, :, at : at + D] = hidden
            back += dot_t(hidden, w3[:, at : at + D])
        back, gain4 = norm_back(back, low, scale4, g4[...])
        accumulate(ln4, gain4)
        grad3 = gx4 + back
        gx3[0] = grad3
        ge_low = grad3.astype(BF16)
        ge[0] = ge_low
        batch_grad = dot_t(ge_low, w_conv[...]) * conv_slope
        gbn[0] = batch_grad
        accumulate(
            sums,
            jnp.concatenate(
                [
                    jnp.sum(batch_grad * unit, axis=0, keepdims=True),
                    jnp.sum(batch_grad, axis=0, keepdims=True),
                ],
                axis=0,
            ),
        )

    return kernel


def batch_back(gbn, dc, stats, back, bn_gain, count):
    middle, inv = batch_stats(stats, count)
    unit = (dc - middle) * inv
    return bn_gain * inv * (gbn - (back[1:2, :] + unit * back[0:1, :]) / count)


def depth_grad_kernel(count):
    def kernel(gbn, dc, stats, back, bn_gain, v, before, after, keep, _, gd, taps_grad, padded):
        steps = v.shape[1]
        fill_padded(padded, v, before, after, keep)
        grad = batch_back(gbn[0], dc[0], stats, back, bn_gain[...], count)
        gd[0] = grad
        columns = []
        for at in range(0, D, 128):
            piece = gd[0, :, at : at + 128]
            rows = [
                jnp.sum(padded[at // 128, k + 1 : k + 1 + steps, :] * piece, axis=0, keepdims=True)
                for k in range(KERNEL)
            ]
            columns.append(jnp.concatenate(rows + [jnp.zeros((1, 128), F32)], axis=0))
        accumulate(taps_grad, jnp.concatenate(columns, axis=1))

    return kernel


def conv_back_kernel(
    gd, before, after, keep, taps, sq, cq, w_conv, a3, r3, g3, gx3, w_out, gs, yd, ce, block,
    gq, gx2, gz, gy, gg, pulled, ln3,
    padded,
):
    steps = gd.shape[1]
    fill_padded(padded, gd, before, after, keep)
    for at in range(0, D, 128):
        running = jnp.zeros((steps, 128), F32)
        for k in range(KERNEL):
            running += padded[at // 128, 15 - k : 15 - k + steps, :] * taps[k : k + 1, at : at + 128]
        gq[0, :, at : at + 128] = (running * sq[0, :, at : at + 128].astype(F32)).astype(BF16)
        gq[0, :, D + at : D + at + 128] = (running * cq[0, :, at : at + 128].astype(F32)).astype(BF16)
    back, gain = norm_back(dot_t(gq[0], w_conv[...]), a3[0], r3[0], g3[...])
    accumulate(ln3, gain)
    grad = gx3[0] + back
    gx2[0] = grad
    low = grad.astype(BF16)
    gz[0] = low
    inner = dot_t(low, w_out[...])
    gg[0] = (inner * yd[0].astype(F32)).astype(BF16)
    read_grad = (inner * gs[0].astype(F32)).astype(BF16)
    gy[0] = read_grad
    row = pl.program_id(0)
    for a, pair in enumerate(pack_state(t_dot(ce[0], read_grad))):
        pulled[0, a, :STATE, :] = pair * keep[0, row]
        pulled[0, a, STATE:, :] = block[0, a, STATE:, :]


def mix_back_kernel(u, bs, c, ee, gy, start, pairs, decay_pairs, _, gu, gb, gc, full):
    steps = u.shape[1]
    unpack_state(start, full)
    reads_grad = dot_t(gy[0], full[...]) * ee[0].astype(F32)
    keys_grad = jnp.zeros((steps, 256), F32)
    keys = bs[0]
    reads = c[0]
    for q in range(2):
        values = u[0, :, 256 * q : 256 * q + 256]
        grads = gy[0, :, 256 * q : 256 * q + 256]
        total = jnp.zeros((steps, 256), F32)
        for b in range(4):
            h = 4 * q + b
            masked = grads * lane_mask(256, HEADP, b)
            scores = (dot_t(masked, values) * decay_pairs[0, h].astype(F32)).astype(BF16)
            mask = lane_mask(256, STATE, h)
            reads_grad += dot(scores, keys * mask)
            keys_grad += t_dot(scores, reads * mask)
            total += t_dot(pairs[0, h], masked)
        gu[0, :, 256 * q : 256 * q + 256] = total
    gc[0] = reads_grad.astype(BF16)
    gb[0] = keys_grad


def mix_end_kernel(
    end, u, bt, te, se, gu, gb, gc, gg, w_in, a2, r2, g2, gx2, _,
    gp, gx1, gf, ln2,
    full,
):
    unpack_state(end, full)
    gp[0, :, :D] = (gu[0] + dot(bt[0], full[...])).astype(BF16)
    gp[0, :, D : 2 * D] = gg[0]
    keys_grad = gb[0] + te[0].astype(F32) * dot_t(u[0], full[...])
    gp[0, :, 2 * D : 2 * D + 256] = (keys_grad * se[0].astype(F32)).astype(BF16)
    gp[0, :, 2 * D + 256 :] = gc[0]
    back, gain = norm_back(dot_t(gp[0], w_in[...]), a2[0], r2[0], g2[...])
    accumulate(ln2, gain)
    grad = gx2[0] + back
    gx1[0] = grad
    gf[0] = (0.5 * grad).astype(BF16)


def front_back_kernel(
    gx1, gf, w2, d1, w1, a1, r1, g1, w_sub, tk, fk, _,
    gh, gxr, fg, ln1,
):
    steps = gx1.shape[1]
    low = gf[0]
    back = jnp.zeros((steps, D), F32)
    for at in range(0, FF, D):
        hidden = (dot_t(low, w2[at : at + D, :]) * d1[0, :, at : at + D].astype(F32)).astype(BF16)
        gh[0, :, at : at + D] = hidden
        back += dot_t(hidden, w1[:, at : at + D])
    back, gain = norm_back(back, a1[0], r1[0], g1[...])
    accumulate(ln1, gain)
    low = (gx1[0] + back).astype(BF16)
    gxr[0] = low
    frames = dot(low, w_sub[...])
    mels = fk.shape[2]
    for j in range(SUB):
        fg[0, pl.ds(j, steps, stride=SUB), :] = frames[:, mels * j : mels * (j + 1)] * (
            tk[0][:, j : j + 1] * fk[0]
        )


def by_share_store(out, at, share, start, block):
    for piece in range(block.shape[0] // share):
        row = start + share * piece
        place = row // (4 * share) * share
        k = row % (4 * share) // share
        out[place : place + share, at + D * k : at + D * (k + 1)] = block[
            share * piece : share * (piece + 1), :
        ]


def late_weights_kernel(share):
    def kernel(a4, e, s4, gh, ge, gf, out):
        left = a4[...].T
        for at in range(0, FF, D):
            out[:, at : at + D] = dot(left, gh[:, at : at + D])
        for at in range(0, 1024, 256):
            by_share_store(out, FF, share, at, dot(s4[:, at : at + 256].T, gf[...]))
        out[:, 2 * FF :] = dot(e[...].T, ge[...])

    return kernel


def turned(place, share, core, block):
    rows = block.T
    half = rows.shape[0] // 2
    for s in range(rows.shape[0] // share):
        side = core if s % 2 == 0 else 1 - core
        at = pl.multiple_of(side * half + s // 2 * share, 16)
        place[pl.ds(at, share), :] = rows[s * share : (s + 1) * share, :]


def turned_by_share(place, share, core, block):
    for at in range(0, block.shape[1], 256):
        rows = block[:, at : at + 256].T
        for piece in range(256 // share):
            row = at + share * piece
            s, k = row // (4 * share), row % (4 * share) // share
            side = core if s % 2 == 0 else 1 - core
            to = pl.multiple_of(side * (D // 2) + D * k + s // 2 * share, 16)
            place[pl.ds(to, share), :] = rows[share * piece : share * (piece + 1), :]


def weights_kernel(pairs, share, waits):
    has_small = pairs[-1] == (1, 0)

    def kernel(core_ref, *refs):
        count = len(pairs)
        lefts, rights = refs[:count], refs[count : 2 * count]
        extra = refs[2 * count] if has_small else None
        kept, sent = refs[2 * count + has_small + waits :][:2]
        places = refs[2 * count + has_small + waits + 2 :]
        step = pl.program_id(0)
        core = core_ref[0]
        start = 0
        for (wide, long), left, right, place in zip(pairs, lefts, rights, places):
            steps = max(wide, long)

            @pl.when(step == start)
            def _(left=left, place=place, wide=wide):
                if wide == 1:
                    turned(place, share, core, left[...])
                else:
                    turned_by_share(place, share, core, left)

            @pl.when((step >= start) & (step < start + steps))
            def _(right=right, place=place, wide=wide, start=start):
                if wide == 1:
                    rows = place[...]
                else:
                    rows = place[pl.ds(pl.multiple_of((step - start) * D, D), D), :]
                block = dot(rows, right[...])
                kept[...] = block[: D // 2, :]
                sent[...] = block[D // 2 :, :]

            start += steps
        if has_small:

            @pl.when(step == start - 1)
            def _():
                for s in range(D // share // 2):
                    for out, side in ((kept, core), (sent, 1 - core)):
                        at = pl.multiple_of((2 * s + side) * share, 8)
                        out[s * share : (s + 1) * share, :] += extra[pl.ds(at, share), :]

    return kernel


def weight_sums(pairs, share, core, small=None, after=()):
    tokens = pairs[0][0].shape[0]
    sizes = [(l.shape[1] // D, r.shape[1] // D) for l, r in pairs]
    if small is not None:
        sizes[-1] = (1, 0)
    lefts, rights, start = [], [], 0
    for (left, right), (wide, long) in zip(pairs, sizes):
        steps = max(wide, long)
        lefts.append((left, "all"))
        if wide == 1 and long > 1:
            index = lambda j, start=start, last=steps - 1: (0, jnp.clip(j - start, 0, last))
            rights.append((right, pl.BlockSpec((tokens, D), index)))
        else:
            rights.append((right, "all"))
        start += steps
    columns = start * D
    extra = [] if small is None else [(small, "all")]
    half = ((D // 2, columns), F32, pl.BlockSpec((D // 2, D), lambda j: (0, j)))
    return call(
        weights_kernel(sizes, share, len(after)),
        (start,),
        [(core, scalars())] + lefts + rights + extra + [(a, anywhere()) for a in after],
        [half, half],
        [pltpu.VMEM((D * wide, tokens), BF16) for wide, _ in sizes],
        2 * tokens * D * columns,
        "weights",
    )


def row_spec(shape):
    rest = len(shape) - 1
    return pl.BlockSpec((1,) + tuple(shape[1:]), lambda r: (r,) + (0,) * rest)


def whole_spec(shape):
    return pl.BlockSpec(tuple(shape), lambda r: (0,) * len(shape))


def held_spec(shape):
    return pl.BlockSpec(tuple(shape), lambda r: (0,) * len(shape), pipeline_mode=pl.Buffered(1))


def scalars():
    return pl.BlockSpec(memory_space=pltpu.SMEM)


def anywhere():
    return pl.BlockSpec(memory_space=pl.ANY)


TIMES = {'front': 19, 'mix': 6, 'lift': 8, 'depth': 6, 'late': 22, 'late_weights': 10, 'depth_grad': 7, 'conv_back': 11, 'mix_back': 11, 'mix_end': 8, 'front_back': 13, 'weights': 9}


def call(kernel, grid, ins, outs, scratch=(), flops=0, name=None, room=LIMIT):
    def made(kind, shape):
        if kind == "row":
            return row_spec(shape)
        return whole_spec(shape) if kind == "all" else kind

    moved = sum(a.size * a.dtype.itemsize for a, _ in ins)
    return pl.pallas_call(
        kernel,
        grid=grid,
        in_specs=[held_spec(a.shape) if kind == "all" else made(kind, a.shape) for a, kind in ins],
        out_specs=[made(kind, shape) for shape, _, kind in outs],
        out_shape=[jax.ShapeDtypeStruct(shape, kind) for shape, kind, _ in outs],
        scratch_shapes=list(scratch),
        compiler_params=pltpu.CompilerParams(
            dimension_semantics=("arbitrary",), vmem_limit_bytes=room * 2**20
        ),
        cost_estimate=pl.CostEstimate(
            flops=int(TIMES[name] * 1.15e9), bytes_accessed=0, transcendentals=0
        ),
        name=name,
    )(*[a for a, _ in ins])


def flip_pairs(count, mask):
    return [(i, i ^ mask) for i in range(count)]


def entering(value, backward):
    count, mine = lax.axis_size("seq"), lax.axis_index("seq")

    def link(earlier, later):
        decay = later[:, :, STATE : STATE + 1, :]
        state = decay * earlier[:, :, :STATE, :] + later[:, :, :STATE, :]
        return jnp.concatenate([state, decay * earlier[:, :, STATE:, :]], axis=2)

    shape = value.shape[:2] + (STATE, value.shape[3])
    before = jnp.concatenate(
        [jnp.zeros(shape, F32), jnp.ones(value.shape[:2] + (8, value.shape[3]), F32)], axis=2
    )
    mask = 1
    while mask < count:
        other = lax.ppermute(value, "seq", flip_pairs(count, mask))
        second = ((mine & mask) != 0) != backward
        before = jnp.where(second, link(other, before), before)
        value = jnp.where(second, link(other, value), link(value, other))
        mask *= 2
    return before


def halos(top, bottom):
    count = lax.axis_size("seq")
    ends = range(count - 1)
    return (
        lax.ppermute(bottom, "seq", [(i, i + 1) for i in ends]),
        lax.ppermute(top, "seq", [(i + 1, i) for i in ends]),
    )


def sum_over_all(value):
    count = lax.axis_size("seq") * lax.axis_size("rec")
    copies = jnp.broadcast_to(value[None], (count,) + value.shape)
    return jnp.sum(lax.all_to_all(copies, ("rec", "seq"), 0, 0), axis=0)


def scatter_sum(value):
    return lax.psum_scatter(value, "seq", scatter_dimension=0, tiled=True)


def in_vmem(kernel, scalars_in, ins, outs, after, name):
    vmem = pl.BlockSpec(memory_space=pltpu.VMEM)
    return pl.pallas_call(
        kernel,
        in_specs=[scalars()] + [vmem] * len(ins) + [anywhere()] * len(after),
        out_specs=[vmem] * len(outs),
        out_shape=[jax.ShapeDtypeStruct(shape, F32) for shape in outs],
        compiler_params=pltpu.CompilerParams(vmem_limit_bytes=32 * 2**20),
        cost_estimate=pl.CostEstimate(
            flops=0, bytes_accessed=0, transcendentals=0
        ),
        name=name,
    )(scalars_in, *ins, *after)


def part_rows(ref, group, chunk, side, columns):
    if chunk % 8:
        low = ref[2 * group * chunk : (2 * group + 1) * chunk, columns]
        high = ref[(2 * group + 1) * chunk : (2 * group + 2) * chunk, columns]
        return jnp.where(side == 0, low, high)
    return ref[pl.ds(pl.multiple_of((2 * group + side) * chunk, 8), chunk), columns]


def add_and_split(bits, groups, after):
    arrays, outs, plan = [], [], []

    def known(array):
        for i, other in enumerate(arrays):
            if other is array:
                return i
        arrays.append(array)
        return len(arrays) - 1

    for items, chunk, bit in groups:
        rows = items[0][0].shape[0]
        placed, at = [], 0
        for kept, received, first, columns in items:
            placed.append(
                (known(kept), None if received is None else known(received), first, columns, at)
            )
            at += columns
        plan.append((placed, rows, chunk, bit, len(outs)))
        outs += [(rows // 2, at)] * 2
    count = len(arrays) + len(after)

    def kernel(bit_ref, *refs):
        for placed, rows, chunk, bit, out in plan:
            mine = bit_ref[bit]
            for kept, received, first, columns, at in placed:
                for target, side in ((refs[count + out], mine), (refs[count + out + 1], 1 - mine)):
                    for group in range(rows // chunk // 2):
                        value = part_rows(refs[kept], group, chunk, side, slice(first, first + columns))
                        if received is not None:
                            value = value + part_rows(
                                refs[received], group, chunk, side, slice(first, first + columns)
                            )
                        target[group * chunk : (group + 1) * chunk, at : at + columns] = value

    made = in_vmem(kernel, bits, arrays, outs, after, "add_and_split")
    return [(made[i], made[i + 1]) for i in range(0, len(made), 2)]


def add_pair(bits, kept, received, after):
    def kernel(_, a, b, *rest):
        rest[-1][...] = a[...] + b[...]

    return in_vmem(kernel, bits, [kept, received], [kept.shape], after, "add_pair")[0]


def join(bits, mine, other, bit, after, pieces=None):
    rows, columns = mine.shape
    outs = [(2 * rows, columns)]
    if pieces is not None:
        outs = [(8 * rows, D) if spread else (2 * rows, wide) for _, wide, spread in pieces]
    cuts = [(0, columns, False)] if pieces is None else pieces

    def kernel(bit_ref, mine_ref, other_ref, *rest):
        first = bit_ref[bit] == 0
        targets = rest[len(after) :]
        for target, (at, wide, spread) in zip(targets, cuts):
            for k in range(4 if spread else 1):
                width = D if spread else wide
                left = mine_ref[:, at + D * k : at + D * k + width]
                right = other_ref[:, at + D * k : at + D * k + width]
                start = 2 * rows * k
                target[start : start + rows, :] = jnp.where(first, left, right)
                target[start + rows : start + 2 * rows, :] = jnp.where(first, right, left)

    made = in_vmem(kernel, bits, [mine, other], outs, after, "join")
    return made[0] if pieces is None else made


class Sum:
    def __init__(self, bits, pieces):
        self.bits = bits
        self.pieces = pieces
        self.seq = lax.axis_size("seq")
        self.rec = lax.axis_size("rec")
        self.chip_bits = self.seq.bit_length() - 2
        self.rec_bits = self.rec.bit_length() - 1
        self.parts = []
        self.left = []
        self.steps = []
        self.done = None

    def swap(self, value, axis, bit):
        return lax.ppermute(value, axis, flip_pairs(lax.axis_size(axis), 1 << bit))

    def begin(self, kept, sent, first):
        columns = kept.shape[1]
        received = self.swap(sent, "seq", 0)
        self.parts = [[(kept, received, 0, first)], [(kept, received, first, columns - first)]]
        turn = 1 + self.chip_bits // 2
        orders = (
            list(range(1, self.chip_bits + 1)),
            list(range(turn, self.chip_bits + 1)) + list(range(1, turn)),
        )
        self.left = [list(range(self.chip_bits, 0, -1)) for _ in orders]
        self.steps += [("chips", now) for now in zip(*orders)]
        self.finish_steps()

    def finish_steps(self):
        self.steps += [("rec", bit) for bit in range(self.rec_bits)] + [("turn", self.rec_bits - 1)]
        self.steps += [("join", bit) for bit in reversed(range(self.rec_bits))]

    def advance(self, after):
        kind, now = self.steps.pop(0)
        if kind == "chips":
            groups = []
            for items, bit, left in zip(self.parts, now, self.left):
                rows = items[0][0].shape[0]
                chunk = rows >> (left.index(bit) + 1)
                left.remove(bit)
                groups.append((items, chunk, bit))
            made = add_and_split(self.bits, groups, after)
            self.parts = [
                [(kept, self.swap(sent, "seq", bit), 0, kept.shape[1])]
                for (kept, sent), bit in zip(made, now)
            ]
            return made[0][0]
        if kind == "rec":
            items = [item for part in self.parts for item in part]
            groups = [(items, items[0][0].shape[0] // 2, self.chip_bits + 1 + now)]
            [(kept, sent)] = add_and_split(self.bits, groups, after)
            self.parts = [[(kept, self.swap(sent, "rec", now), 0, kept.shape[1])]]
            return kept
        if kind == "turn":
            [[(kept, received, _, _)]] = self.parts
            self.mine = add_pair(self.bits, kept, received, after)
            self.other = self.swap(self.mine, "rec", now)
            return self.mine
        bit = self.chip_bits + 1 + now
        if now == 0:
            self.done = join(self.bits, self.mine, self.other, bit, after, self.pieces)
            return self.done[0]
        self.mine = join(self.bits, self.mine, self.other, bit, after)
        self.other = self.swap(self.mine, "rec", now - 1)
        return self.mine


def local(
    features, time_keep, freq_keep, block_flags, decays, w_sub, ln1_gain, ffn1_in, ffn1_out, ln2_gain,
    ssm_in, ssm_out, ln3_gain, conv_in, conv_depth, bn_gain, bn_shift, conv_out, ln4_gain, ffn2_in,
    ffn2_out, ln5_gain, out_grad,
):
    rows, frame_count, mels = features.shape
    steps = frame_count // SUB
    tokens = rows * steps
    blocks = lax.axis_size("seq")
    place = lax.axis_index("seq")
    count = float(tokens * blocks * lax.axis_size("rec"))
    share = D // blocks
    here = lax.dynamic_index_in_dim(block_flags, place, 1, keepdims=False)
    after = lax.dynamic_index_in_dim(
        block_flags, jnp.minimum(place + 1, blocks - 1), 1, keepdims=False
    )
    keep_here = (1 - here).astype(F32)
    keep_next = jnp.where(place + 1 < blocks, 1 - after, 0).astype(F32)
    keep = (jnp.stack([keep_here, keep_next]), scalars())
    tk = (time_keep.reshape(rows, steps, SUB).astype(F32), "row")
    fk = (freq_keep[:, None, :].astype(F32), "row")
    sub_wide = jnp.pad(w_sub, ((0, 0), (0, WIDE - SUB * mels)))
    g1, g2, g3, g4, g5, bg, bb = (
        (gain.reshape(1, D), "all")
        for gain in (ln1_gain, ln2_gain, ln3_gain, ln4_gain, ln5_gain, bn_gain, bn_shift)
    )
    taps = (jnp.pad(conv_depth.T, ((0, 1), (0, 0))), "all")

    def rows_of(width, kind=F32):
        return ((rows, steps, width), kind, "row")

    per_state = ((rows, 4, STATE + 8, 128), F32, "row")
    edge = ((rows, 8, D), F32, "row")
    line = ((1, D), F32, "all")
    two_lines = ((2, D), F32, "all")
    padded = pltpu.VMEM((D // 128, steps + 16, 128), F32)
    full = pltpu.VMEM((256, D), BF16)

    def row(value):
        return (value, "row")

    def every(value):
        return (value, "all")

    (flat, x1, a1, r1, s1, d1, a2, r2, u, g, bs, c, ce, bt, se, ee, te, cum, cum_t, state) = call(
        front_kernel,
        (rows,),
        [
            row(features), tk, fk, row(decays), row(decays.transpose(0, 2, 1)), keep,
            every(sub_wide.T), g1, every(ffn1_in), every(ffn1_out), g2, every(ssm_in),
        ],
        [
            rows_of(WIDE, BF16), rows_of(D), rows_of(D, BF16), rows_of(1), rows_of(FF, BF16),
            rows_of(FF, BF16), rows_of(D, BF16), rows_of(1), rows_of(D, BF16), rows_of(D, BF16),
            rows_of(256, BF16), rows_of(256, BF16), rows_of(256, BF16), rows_of(256, BF16),
            rows_of(256, BF16), rows_of(256, BF16), rows_of(256, BF16), rows_of(HEADS),
            ((rows, HEADS, steps), F32, "row"), per_state,
        ],
        [pltpu.VMEM((frame_count, mels), F32)],
        2 * tokens * D * (WIDE + 2 * FF + PROJ),
        "front",
    )
    before = entering(state, False)
    start = before * keep_here[:, None, None, None]
    pair_shape = ((rows, HEADS, steps, steps), BF16, "row")
    mixed, pairs, decay_pairs = call(
        mix_kernel,
        (rows,),
        [row(u), row(bs), row(c), row(cum), row(cum_t)],
        [rows_of(D), pair_shape, pair_shape],
        (),
        2 * tokens * 256 * 256 * 16,
        "mix",
    )
    z, gs, yd, x2, a3, r3, v, sq, cq, top, bottom = call(
        lift_kernel,
        (rows,),
        [row(mixed), row(ce), row(start), row(g), row(x1), every(ssm_out), g3, every(conv_in)],
        [
            rows_of(D, BF16), rows_of(D, BF16), rows_of(D, BF16), rows_of(D), rows_of(D, BF16),
            rows_of(1), rows_of(D), rows_of(D, BF16), rows_of(D, BF16), edge, edge,
        ],
        [full],
        2 * tokens * D * 4 * D,
        "lift",
    )
    v_before, v_after = halos(top, bottom)
    dc, sums = call(
        depth_kernel,
        (rows,),
        [row(v), row(v_before), row(v_after), keep, taps],
        [rows_of(D), two_lines],
        [padded],
        2 * tokens * D * 64,
        "depth",
    )
    stats = sum_over_all(sums)
    out, e, a4, s4, gf4, gh4, ge, gx3, gbn, back_sums, ln4, ln5 = call(
        late_kernel(count),
        (rows,),
        [
            row(dc), row(x2), row(out_grad), every(stats), bg, bb, every(conv_out), g4,
            every(ffn2_in), every(ffn2_out), g5,
        ],
        [
            rows_of(D, BF16), rows_of(D, BF16), rows_of(D, BF16), rows_of(FF, BF16), rows_of(D, BF16),
            rows_of(FF, BF16), rows_of(D, BF16), rows_of(D), rows_of(D), two_lines, line, line,
        ],
        [pltpu.VMEM((steps, FF), BF16)],
        2 * tokens * D * (4 * FF + 2 * D),
        "late",
    )
    back = sum_over_all(back_sums)

    def flatten(value):
        return value.reshape(tokens, value.shape[-1])

    def column_block(value, width):
        return (flatten(value), pl.BlockSpec((tokens, width), lambda i: (0, i)))

    def row_block(columns):
        return ((D, columns), F32, pl.BlockSpec((256, columns), lambda i: (i, 0)))

    (late_grads,) = call(
        late_weights_kernel(share),
        (2,),
        [
            column_block(a4, 256), column_block(e, 256), column_block(s4, 1024),
            every(flatten(gh4)), every(flatten(ge)), every(flatten(gf4)),
        ],
        [row_block(2 * FF + D)],
        (),
        2 * tokens * D * (2 * FF + D),
        "late_weights",
    )
    group_a = scatter_sum(late_grads)

    def edge_grad(at):
        return batch_back(
            lax.slice_in_dim(gbn, at, at + 8, axis=1),
            lax.slice_in_dim(dc, at, at + 8, axis=1),
            stats, back, bn_gain, count,
        )

    gd_before, gd_after = halos(edge_grad(0), edge_grad(steps - 8))
    gd, taps_grad = call(
        depth_grad_kernel(count),
        (rows,),
        [
            row(gbn), row(dc), every(stats), every(back), bg, row(v), row(v_before), row(v_after), keep,
            (late_grads, anywhere()),
        ],
        [rows_of(D), ((16, D), F32, "all")],
        [padded],
        2 * tokens * D * 64,
        "depth_grad",
    )
    gq, gx2, gz, gy, gg, pulled, ln3 = call(
        conv_back_kernel,
        (rows,),
        [
            row(gd), row(gd_before), row(gd_after), keep, taps, row(sq), row(cq), every(conv_in),
            row(a3), row(r3), g3, row(gx3), every(ssm_out), row(gs), row(yd), row(ce), row(state),
        ],
        [
            rows_of(2 * D, BF16), rows_of(D), rows_of(D, BF16), rows_of(D, BF16), rows_of(D, BF16),
            per_state, line,
        ],
        [padded],
        2 * tokens * D * 4 * D,
        "conv_back",
    )
    end = entering(pulled, True)
    core = (place % 2).reshape(1)
    kept, sent = weight_sums([(flatten(a3), flatten(gq)), (flatten(z), flatten(gz))], share, core)
    bits = jnp.stack(
        [(place >> k) & 1 for k in range(blocks.bit_length() - 1)]
        + [(lax.axis_index("rec") >> k) & 1 for k in range(lax.axis_size("rec").bit_length() - 1)]
    )
    early = Sum(
        bits,
        [
            (0, FF, False), (FF, FF, True), (2 * FF, D, False), (2 * FF + D, 2 * D, False),
            (2 * FF + 3 * D, D, False),
        ],
    )
    early.begin(kept, sent, D)
    gu, gb, gc = call(
        mix_back_kernel,
        (rows,),
        [
            row(u), row(bs), row(c), row(ee), row(gy), row(start), row(pairs), row(decay_pairs),
            (sent, anywhere()),
        ],
        [rows_of(D), rows_of(256), rows_of(256, BF16)],
        [full],
        2 * tokens * 256 * 256 * 32,
        "mix_back",
    )
    token = early.advance([gu])
    gp, gx1, gf1, ln2 = call(
        mix_end_kernel,
        (rows,),
        [
            row(end), row(u), row(bt), row(te), row(se), row(gu), row(gb), row(gc), row(gg),
            every(ssm_in), row(a2), row(r2), g2, row(gx2), (token, anywhere()),
        ],
        [rows_of(PROJ, BF16), rows_of(D), rows_of(D, BF16), line],
        [full],
        2 * tokens * D * PROJ,
        "mix_end",
    )
    token = early.advance([gf1])
    kept, sent = weight_sums(
        [(flatten(a2), flatten(gp)), (flatten(s1), flatten(gf1))], share, core, None, [token]
    )
    middle = Sum(bits, [(0, PROJ, False), (PROJ, FF, True)])
    middle.begin(kept, sent, PROJ)
    gh1, gxr, features_grad, ln1 = call(
        front_back_kernel,
        (rows,),
        [
            row(gx1), row(gf1), every(ffn1_out), row(d1), every(ffn1_in), row(a1), row(r1), g1,
            every(sub_wide), tk, fk, (sent, anywhere()),
        ],
        [rows_of(FF, BF16), rows_of(D, BF16), ((rows, frame_count, mels), F32, "row"), line],
        (),
        2 * tokens * D * (WIDE + 2 * FF),
        "front_back",
    )
    small = jnp.concatenate(
        [ln1, ln2, ln3, ln4, ln5, taps_grad[:KERNEL], jnp.zeros((WIDE - SUB * mels - 20, D), F32)],
        axis=0,
    )
    small = jnp.pad(small.T, ((0, 0), (SUB * mels, 0)))
    token = middle.advance([ln1])
    while early.steps[0][0] == "chips":
        token = early.advance([token])
    early.parts = [[(group_a, None, 0, group_a.shape[1])]] + early.parts
    token = early.advance([token])
    last = Sum(bits, [(0, FF, False), (FF, SUB * mels, False), (FF + SUB * mels, 24, False)])
    kept, sent = weight_sums(
        [(flatten(a1), flatten(gh1)), (flatten(gxr), flatten(flat))], share, core, small, [token]
    )
    last.begin(kept, sent, 2 * D)
    order = [early, middle, last, early, middle, last, middle, last, early, middle, last, early, middle, last]
    order += [middle, last]
    token = sent
    while any(group.steps for group in (early, middle, last)):
        group = order.pop(0) if order else next(g for g in (early, middle, last) if g.steps)
        if group.steps:
            token = group.advance([token])
    ffn2_in_grad, ffn2_out_grad, conv_out_grad, conv_in_grad, ssm_out_grad = early.done
    ssm_in_grad, ffn1_out_grad = middle.done
    ffn1_in_grad, w_sub_grad, gains = last.done

    start_row = place * share
    return (
        out,
        features_grad,
        w_sub_grad,
        gains[:, 0],
        ffn1_in_grad,
        ffn1_out_grad,
        gains[:, 1],
        ssm_in_grad,
        ssm_out_grad,
        gains[:, 2],
        conv_in_grad,
        gains[:, 5 : 5 + KERNEL],
        lax.dynamic_slice_in_dim(back[0], start_row, share),
        lax.dynamic_slice_in_dim(back[1], start_row, share),
        conv_out_grad,
        gains[:, 3],
        ffn2_in_grad,
        ffn2_out_grad,
        gains[:, 4],
    )


def solution(mesh):
    block = P("rec", "seq", None)
    rows_of_seq, line = P("seq", None), P("seq")
    return jax.shard_map(
        local,
        mesh=mesh,
        in_specs=(block, P("rec", "seq"), P("rec", None), P("rec", None), P("rec", None, "seq"))
        + (P(),) * 17
        + (block,),
        out_specs=(
            block, block, rows_of_seq, line, rows_of_seq, rows_of_seq, line, rows_of_seq, rows_of_seq,
            line, rows_of_seq, rows_of_seq, line, line, rows_of_seq, line, rows_of_seq, rows_of_seq, line,
        ),
        check_vma=False,
    )
```

time: 958 us -> 435 us (0.45)
  waiting for transfers between devices: 432 us -> 128 us
  matrix products: 185 us -> 0 us
  Pallas kernels: 0 us -> 178 us
  blocking collectives: 141 us -> 16.3 us
  local copies, waits for them, and re-layouts: 97.3 us -> 33.9 us
  other arithmetic: 64.3 us -> 10.1 us
  starting transfers between devices: 10 us -> 52 us
    reduce_scatter x9 -> x1, waiting for transfers between devices: 325 us -> 0.01 us  [scatter_sum(): return lax.psum_scatter(value, 'seq', scatter_dimension=0, tiled=True)]
    dot_general x39 -> x0, matrix products: 185 us -> none  [the longest x12 84.1 us: contract(): return jnp.einsum(formula, tensor_a, tensor_b, precision=highest)]
    pallas_call x0 -> x35, Pallas kernels: none -> 178 us  [the longest x14 159 us: call(): pl.pallas_call(kernel, grid=grid, in_specs=[held_spec(a.shape) if kind ==...]
    ppermute x4 -> x37, waiting for transfers between devices: 1.01 us -> 120 us  [the longest x27 98.8 us: swap(): return lax.ppermute(value, axis, flip_pairs(lax.axis_size(axis), 1 << bit))]
    psum x3 -> x0, blocking collectives: 106 us -> none  [the longest x1 43.9 us: local(): lax.psum((jnp.sum(depth_out, axis=(0, 1)), jnp.sum(depth_out * depth_out,...]
    psum x1 -> x0, waiting for transfers between devices: 72.3 us -> none  [local(): lax.psum((shares[0], shares[1], shares[2], shares[3], shares[4], shares[5...]
    ppermute x4 -> x37, starting transfers between devices: 8.65 us -> 49.4 us  [the longest x27 33.2 us: swap(): return lax.ppermute(value, axis, flip_pairs(lax.axis_size(axis), 1 << bit))]
    unnamed x14 -> x1, waiting for transfers between devices: 33.5 us -> 0.02 us
  transfers between devices with their start and end apart: 17 -> 39, of which waited for: 11 -> 18; matrix products, arithmetic and copies ran while one was open for 19% -> 3% of each run, Pallas kernels for 0% -> 22%
where the time goes in v2:
time: 435 us; the launch traced here: 433 us
  Pallas kernels  178 us (41%)
  waiting for transfers between devices  128 us (29%)
  starting transfers between devices  52 us (12%)
  local copies, waits for them, and re-layouts  33.9 us (8%)
  blocking collectives  16.3 us (4%)
  between operations  14.9 us (3%)
  other arithmetic  10.1 us (2%)
    pallas_call x14, Pallas kernels, call(): pl.pallas_call(kernel, grid=grid, in_specs=[held_spec(a.shape) if kind ==...  159 us
    ppermute x27, waiting for transfers between devices, swap(): return lax.ppermute(value, axis, flip_pairs(lax.axis_size(axis), 1 << bit))  98.8 us
    ppermute x27, starting transfers between devices, swap(): return lax.ppermute(value, axis, flip_pairs(lax.axis_size(axis), 1 << bit))  33.2 us
    unnamed x77, local copies, waits for them, and re-layouts  21.1 us
    pallas_call x21, Pallas kernels, in_vmem(): pl.pallas_call(kernel, in_specs=[scalars()] + [vmem] * len(ins) + [anywhe...  18.7 us
    ppermute x6, waiting for transfers between devices, entering(): other = lax.ppermute(value, 'seq', flip_pairs(count, mask))  18 us
    all_to_all x1, blocking collectives, sum_over_all(): return jnp.sum(lax.all_to_all(copies, ('rec', 'seq'), 0, 0), axis=0)  16.3 us
    ppermute x6, starting transfers between devices, entering(): other = lax.ppermute(value, 'seq', flip_pairs(count, mask))  9.98 us
  transfers between devices with their start and end apart: 39, of which 18 were waited for; matrix products, arithmetic and copies ran while one was open for 3% of the time, Pallas kernels for 22%

profile of v2, /device:TPU:0, one launch (start us, length us, event | category | flops | bytes accessed | tf_op | source)
XLA Modules:
  0.0 433.3 jit_solution(17777007584306646322)
XLA Ops:
  16.1 20.4 %front.1 = (bf16[4,256,512]{2,1,0:T(8,128)(2,1)}, f32[4,256,512]{2,1,0:T(8,128)}, bf16[4,256,512]{2,1,0:T(8,128)(2,1)}, f32[4,256,1]{2,1,0:T(8,128)}, bf16[4,256...) custom-call(bf16[4,1024,80]{2,1,0:T(8,128)(2,1)} %copy.80.feat, ...), custom_call_target="tpu_custom_call" | custom-call | flops 21849999360 | tf_op jit(solution)/shard_map/front/pallas_call | solution.py:594
  43.5 7.9 %collective-permute-done.1 = f32[4,4,40,128]{3,2,1,0:T(8,128)S(1)} collective-permute-done((f32[4,4,40,128]{3,2,1,0:T(8,128)S(1)}, f32[4,4,40,128]{3,2,1,0:T(8,128)S(1)}, u32[]{:S(2)}, u32[]{:S(2)}) %collective-permute-start.1) | collective-permute-done | bytes 327712 | tf_op jit(solution)/shard_map/ppermute | solution.py:629
  53.4 7.3 %mix.1 = (f32[4,256,512]{2,1,0:T(8,128)}, bf16[4,8,256,256]{3,2,1,0:T(8,128)(2,1)}, bf16[4,8,256,256]{3,2,1,0:T(8,128)(2,1)}) custom-call(bf16[4,256,512]{2,1,0:T(8,128)(2,1)} %get-tuple-element.139.u, bf16[4,256,256]{2,1,0:T(8,128)(2,1)} %get-tuple-element.140.bs, bf16[4,256,256]{2,1,0:T(8,128)(2,1)} %get-tuple-element.141.c, ...), custom_call_target="tpu_custom_call" | custom-call | flops 6899999744 | tf_op jit(solution)/shard_map/mix/pallas_call | solution.py:594
  61.8 9.1 %lift.1 = (bf16[4,256,512]{2,1,0:T(8,128)(2,1)}, bf16[4,256,512]{2,1,0:T(8,128)(2,1)}, bf16[4,256,512]{2,1,0:T(8,128)(2,1)}, f32[4,256,512]{2,1,0:T(8,128)}, bf1...) custom-call(f32[4,256,512]{2,1,0:T(8,128)} %get-tuple-element.144.mi, ...), custom_call_target="tpu_custom_call" | custom-call | flops 9200000000 | tf_op jit(solution)/shard_map/lift/pallas_call | solution.py:594
  77.9 5.6 %depth.1 = (f32[4,256,512]{2,1,0:T(8,128)}, f32[2,512]{1,0:T(2,128)}) custom-call(f32[4,256,512]{2,1,0:T(8,128)} %get-tuple-element.149.v, f32[4,8,512]{2,1,0:T(8,128)} %copy-done.32, f32[4,8,512]{2,1,0:T(8,128)} %copy-done.33, f32[2,4]{1,0:T(2,128)} %pad_maximum_fusion.keep, f32[16,512]{1,0:T(8,128)} %pad.14.taps), custom_call_target="tpu_custom_call" | custom-call | flops 6899999744 | tf_op jit(solution)/shard_map/depth/pallas_call | solution.py:594
  84.2 16.3 %all_to_all.10 = f32[32,2,512]{2,1,0:T(2,128)S(1)} all-to-all(f32[32,2,512]{2,1,0:T(2,128)S(1)} %broadcast_in_dim.11), channel_id=1, replica_groups=mesh['seq'=8,'rec'=4] {'rec','seq'}, dimensions={0} | all-to-all | bytes 262144 | tf_op jit(solution)/shard_map/all_to_all | solution.py:649
  101.1 23.8 %late.1 = (bf16[4,256,512]{2,1,0:T(8,128)(2,1)}, bf16[4,256,512]{2,1,0:T(8,128)(2,1)}, bf16[4,256,512]{2,1,0:T(8,128)(2,1)}, bf16[4,256,2048]{2,1,0:T(8,128)(2,1...) custom-call(f32[4,256,512]{2,1,0:T(8,128)} %get-tuple-element.152.dc, ...), custom_call_target="tpu_custom_call" | custom-call | flops 25300000768 | tf_op jit(solution)/shard_map/late/pallas_call | solution.py:594
  124.9 11.4 %late_weights.1._ = f32[512,4608]{1,0:T(8,128)} custom-call(bf16[1024,512]{1,0:T(8,128)(2,1)} %bitcast.125, bf16[1024,512]{1,0:T(8,128)(2,1)} %bitcast.124, bf16[1024,2048]{1,0:T(8,128)(2,1)} %bitcast.113, bf16[1024,2048]{1,0:T(8,128)(2,1)} %bitcast.114, bf16[1024,512]{1,0:T(8,128)(2,1)} %bitcast.127, bf16[1024,512]{1,0:T(8,128)(2,1)} %bitcast.126), custom_call_target="tpu_custom_call" | custom-call | flops 11500000256 | tf_op jit(solution)/shard_map/late_weights/pallas_call | solution.py:594
  140.3 8.2 %all-to-all-done.1 = f32[32,2,512]{2,1,0:T(2,128)S(1)} async-done(((f32[32,2,512]{2,1,0:T(2,128)}), f32[32,2,512]{2,1,0:T(2,128)S(1)}, u32[]{:S(2)}, u32[]{:S(2)}) %all-to-all-start.1) | async-done | bytes 131104 | tf_op jit(solution)/shard_map/all_to_all | solution.py:649
  153.3 6.7 %depth_grad.1 = (f32[4,256,512]{2,1,0:T(8,128)}, f32[16,512]{1,0:T(8,128)}) custom-call(f32[4,256,512]{2,1,0:T(8,128)} %get-tuple-element.156.gbn, f32[4,256,512]{2,1,0:T(8,128)} %get-tuple-element.152.dc, f32[2,512]{1,0:T(2,128)} %reduce_sum.18.stats, f32[2,512]{1,0:T(2,128)} %copy-done.23, f32[1,512]{1,0:T(1,128)} %bitcast.99, ...), custom_call_target="tpu_custom_call" | custom-call | flops 8049999872 | tf_op jit(solution)/shard_map/depth_grad/pallas_call | solution.py:594
  160.7 11.4 %conv_back.1 = (bf16[4,256,1024]{2,1,0:T(8,128)(2,1)}, f32[4,256,512]{2,1,0:T(8,128)}, bf16[4,256,512]{2,1,0:T(8,128)(2,1)}, bf16[4,256,512]{2,1,0:T(8,128)(2,1)...) custom-call(f32[4,256,512]{2,1,0:T(8,128)} %get-tuple-element.164.gd, ...), custom_call_target="tpu_custom_call" | custom-call | flops 12650000384 | tf_op jit(solution)/shard_map/conv_back/pallas_call | solution.py:594
  178.7 6.4 %weights.3 = (f32[256,1536]{1,0:T(8,128)}, f32[256,1536]{1,0:T(8,128)}) custom-call(s32[1]{0:T(128)} %bitcast.34.core_ref, bf16[1024,512]{1,0:T(8,128)(2,1)} %bitcast.121, bf16[1024,512]{1,0:T(8,128)(2,1)} %bitcast.120, bf16[1024,1024]{1,0:T(8,128)(2,1)} %bitcast.116, bf16[1024,512]{1,0:T(8,128)(2,1)} %bitcast.122), custom_call_target="tpu_custom_call" | custom-call | flops 10350000128 | tf_op jit(solution)/shard_map/weights/pallas_call | solution.py:594
  185.2 9.0 %collective-permute-done.8 = f32[4,4,40,128]{3,2,1,0:T(8,128)S(1)} collective-permute-done((f32[4,4,40,128]{3,2,1,0:T(8,128)S(1)}, f32[4,4,40,128]{3,2,1,0:T(8,128)S(1)}, u32[]{:S(2)}, u32[]{:S(2)}) %collective-permute-start.8) | collective-permute-done | bytes 327712 | tf_op jit(solution)/shard_map/ppermute | solution.py:629
  195.9 12.2 %mix_back.1 = (f32[4,256,512]{2,1,0:T(8,128)}, f32[4,256,256]{2,1,0:T(8,128)}, bf16[4,256,256]{2,1,0:T(8,128)(2,1)}) custom-call(bf16[4,256,512]{2,1,0:T(8,128)(2,1)} %get-tuple-element.139.u, bf16[4,256,256]{2,1,0:T(8,128)(2,1)} %get-tuple-element.140.bs, bf16[4,256,256]{2,1,0:T(8,128)(2,1)} %get-tuple-element.141.c, ...), custom_call_target="tpu_custom_call" | custom-call | flops 12650000384 | tf_op jit(solution)/shard_map/mix_back/pallas_call | solution.py:594
  212.3 9.7 %mix_end.1 = (bf16[4,256,1536]{2,1,0:T(8,128)(2,1)}, f32[4,256,512]{2,1,0:T(8,128)}, bf16[4,256,512]{2,1,0:T(8,128)(2,1)}, f32[1,512]{1,0:T(1,128)}) custom-call(f32[4,4,40,128]{3,2,1,0:T(8,128)} %maximum_select_fusion.7.end, bf16[4,256,512]{2,1,0:T(8,128)(2,1)} %get-tuple-element.139.u, bf16[4,256,256]{2,1,0:T(8,128)(2,1)} %get-tuple-element.173.bt, ...), custom_call_target="tpu_custom_call" | custom-call | flops 9200000000 | tf_op jit(solution)/shard_map/mix_end/pallas_call | solution.py:594
  222.0 5.7 %collective-permute-done.12.refs_3_ = f32[128,1024]{1,0:T(8,128)S(1)} collective-permute-done((f32[128,1024]{1,0:T(8,128)S(1)}, f32[128,1024]{1,0:T(8,128)S(1)}, u32[]{:S(2)}, u32[]{:S(2)}) %collective-permute-start.12) | collective-permute-done | bytes 524320 | tf_op jit(solution)/shard_map/ppermute | solution.py:762
  230.9 12.0 %weights.4 = (f32[256,3584]{1,0:T(8,128)}, f32[256,3584]{1,0:T(8,128)}) custom-call(s32[1]{0:T(128)} %bitcast.34.core_ref, bf16[1024,512]{1,0:T(8,128)(2,1)} %bitcast.119, bf16[1024,2048]{1,0:T(8,128)(2,1)} %bitcast.111, bf16[1024,1536]{1,0:T(8,128)(2,1)} %bitcast.115, bf16[1024,512]{1,0:T(8,128)(2,1)} %bitcast.61, f32[64,512]{1,0:T(8,128)} %copy-done.13), custom_call_target="tpu_custom_call" | custom-call | flops 10350000128 | tf_op jit(solution)/shard_map/weights/pallas_call | solution.py:594
  246.0 14.0 %front_back.1 = (bf16[4,256,2048]{2,1,0:T(8,128)(2,1)}, bf16[4,256,512]{2,1,0:T(8,128)(2,1)}, f32[4,1024,80]{2,1,0:T(8,128)}, f32[1,512]{1,0:T(1,128)}) custom-call(f32[4,256,512]{2,1,0:T(8,128)} %get-tuple-element.193.gx1, bf16[4,256,512]{2,1,0:T(8,128)(2,1)} %get-tuple-element.194.refs_4_.gf, bf16[2048,512]{1,0:T(8,128)(2,1)} %w2.3, ...), custom_call_target="tpu_custom_call" | custom-call | flops 14949999616 | tf_op jit(solution)/shard_map/front_back/pallas_call | solution.py:594
  271.3 9.3 %weights.5 = (f32[256,2560]{1,0:T(8,128)}, f32[256,2560]{1,0:T(8,128)}) custom-call(s32[1]{0:T(128)} %bitcast.34.core_ref, bf16[1024,512]{1,0:T(8,128)(2,1)} %bitcast.118, bf16[1024,512]{1,0:T(8,128)(2,1)} %bitcast.123, bf16[1024,2048]{1,0:T(8,128)(2,1)} %bitcast.112, bf16[1024,512]{1,0:T(8,128)(2,1)} %bitcast.117, f32[512,512]{1,0:T(8,128)} %pad.15.refs_4_, ...), custom_call_target="tpu_custom_call" | custom-call | flops 10350000128 | tf_op jit(solution)/shard_map/weights/pallas_call | solution.py:594
  283.9 16.9 %collective-permute-done.19.refs_1_ = f32[32,6144]{1,0:T(8,128)S(1)} collective-permute-done((f32[32,6144]{1,0:T(8,128)S(1)}, f32[32,6144]{1,0:T(8,128)S(1)}, u32[]{:S(2)}, u32[]{:S(2)}) %collective-permute-start.19) | collective-permute-done | bytes 786464 | tf_op jit(solution)/shard_map/ppermute | solution.py:762
  313.4 16.2 %collective-permute-done.24.b = f32[16,6144]{1,0:T(8,128)S(1)} collective-permute-done((f32[16,6144]{1,0:T(8,128)S(1)}, f32[16,6144]{1,0:T(8,128)S(1)}, u32[]{:S(2)}, u32[]{:S(2)}) %collective-permute-start.24) | collective-permute-done | bytes 393248 | tf_op jit(solution)/shard_map/ppermute | solution.py:762
  341.9 12.1 %collective-permute-done.27.refs_1_ = f32[32,3584]{1,0:T(8,128)S(1)} collective-permute-done((f32[32,3584]{1,0:T(8,128)S(1)}, f32[32,3584]{1,0:T(8,128)S(1)}, u32[]{:S(2)}, u32[]{:S(2)}) %collective-permute-start.27) | collective-permute-done | bytes 458784 | tf_op jit(solution)/shard_map/ppermute | solution.py:762
  361.3 20.8 %collective-permute-done.29.b = f32[16,3584]{1,0:T(8,128)S(1)} collective-permute-done((f32[16,3584]{1,0:T(8,128)S(1)}, f32[16,3584]{1,0:T(8,128)S(1)}, u32[]{:S(2)}, u32[]{:S(2)}) %collective-permute-start.29) | collective-permute-done | bytes 229408 | tf_op jit(solution)/shard_map/ppermute | solution.py:762
  398.2 7.6 %collective-permute-done.31.b = f32[16,2560]{1,0:T(8,128)S(1)} collective-permute-done((f32[16,2560]{1,0:T(8,128)S(1)}, f32[16,2560]{1,0:T(8,128)S(1)}, u32[]{:S(2)}, u32[]{:S(2)}) %collective-permute-start.31) | collective-permute-done | bytes 163872 | tf_op jit(solution)/shard_map/ppermute | solution.py:762
  (236 shorter events, 138.4 us)
Async XLA Ops:
  7.2 261.2 %reduce-scatter.2.cloned.1.call-start = ((), (), s32[]{:S(2)}) async-start(), calls=%async_computation.3 | async-start | bytes 10616832 | tf_op jit(solution)/shard_map/reduce_scatter | solution.py:653
  176.9 17.2 %collective-permute-start.8 = (f32[4,4,40,128]{3,2,1,0:T(8,128)S(1)}, f32[4,4,40,128]{3,2,1,0:T(8,128)S(1)}, u32[]{:S(2)}, u32[]{:S(2)}) collective-permute-start(f32[4,4,40,128]{3,2,1,0:T(8,128)S(1)} %maximum_select_fusion.4), channel_id=1, source_target_pairs={{0,8},{4,12},{8,0},{12,4},{16,24},{20,28},{24,16},{28,20},{1,9},{5... | collective-permute-start | bytes 983048 | tf_op jit(solution)/shard_map/ppermute | solution.py:629
  185.0 24.1 %collective-permute-start.10 = (f32[256,1536]{1,0:T(8,128)}, f32[256,1536]{1,0:T(8,128)S(1)}, u32[]{:S(2)}, u32[]{:S(2)}) collective-permute-start(f32[256,1536]{1,0:T(8,128)} %get-tuple-element.183._), channel_id=1, source_target_pairs={{0,4},{4,0},{8,12},{12,8},{16,20},{20,16},{24,28},{28,24},{1,5},{5... | collective-permute-start | bytes 4718600 | tf_op jit(solution)/shard_map/ppermute | solution.py:762
  194.3 14.0 %collective-permute-start.9 = (f32[4,4,40,128]{3,2,1,0:T(8,128)S(1)}, f32[4,4,40,128]{3,2,1,0:T(8,128)S(1)}, u32[]{:S(2)}, u32[]{:S(2)}) collective-permute-start(f32[4,4,40,128]{3,2,1,0:T(8,128)S(1)} %maximum_select_fusion.6), channel_id=1, source_target_pairs={{0,16},{4,20},{8,24},{12,28},{16,0},{20,4},{24,8},{28,12},{1,17},{... | collective-permute-start | bytes 983048 | tf_op jit(solution)/shard_map/ppermute | solution.py:629
  211.4 16.3 %collective-permute-start.12 = (f32[128,1024]{1,0:T(8,128)S(1)}, f32[128,1024]{1,0:T(8,128)S(1)}, u32[]{:S(2)}, u32[]{:S(2)}) collective-permute-start(f32[128,1024]{1,0:T(8,128)S(1)} %get-tuple-element.202), channel_id=1, source_target_pairs={{0,16},{4,20},{8,24},{12,28},{16,0},{20,4},{24,8},{28,12},{1,17},{... | collective-permute-start | bytes 1572872 | tf_op jit(solution)/shard_map/ppermute | solution.py:762
  242.9 20.1 %collective-permute-start.15 = (f32[256,3584]{1,0:T(8,128)}, f32[256,3584]{1,0:T(8,128)}, u32[]{:S(2)}, u32[]{:S(2)}) collective-permute-start(f32[256,3584]{1,0:T(8,128)} %get-tuple-element.204._), channel_id=1, source_target_pairs={{0,4},{4,0},{8,12},{12,8},{16,20},{20,16},{24,28},{28,24},{1,5},{5... | collective-permute-start | bytes 11010056 | tf_op jit(solution)/shard_map/ppermute | solution.py:762
  243.7 24.8 %collective-permute-start.13 = (f32[64,512]{1,0:T(8,128)S(1)}, f32[64,512]{1,0:T(8,128)S(1)}, u32[]{:S(2)}, u32[]{:S(2)}) collective-permute-start(f32[64,512]{1,0:T(8,128)S(1)} %get-tuple-element.215), channel_id=1, source_target_pairs={{0,16},{4,20},{8,24},{12,28},{16,0},{20,4},{24,8},{28,12},{1,17},{... | collective-permute-start | bytes 393224 | tf_op jit(solution)/shard_map/ppermute | solution.py:762
  245.3 23.2 %collective-permute-start.14 = (f32[64,1024]{1,0:T(8,128)}, f32[64,1024]{1,0:T(8,128)S(1)}, u32[]{:S(2)}, u32[]{:S(2)}) collective-permute-start(f32[64,1024]{1,0:T(8,128)} %get-tuple-element.217), channel_id=1, source_target_pairs={{0,8},{4,12},{8,0},{12,4},{16,24},{20,28},{24,16},{28,20},{1,9},{5... | collective-permute-start | bytes 786440 | tf_op jit(solution)/shard_map/ppermute | solution.py:762
  280.6 26.4 %collective-permute-start.16 = (f32[256,2560]{1,0:T(8,128)}, f32[256,2560]{1,0:T(8,128)S(1)}, u32[]{:S(2)}, u32[]{:S(2)}) collective-permute-start(f32[256,2560]{1,0:T(8,128)} %get-tuple-element.222.refs_2_), channel_id=1, source_target_pairs={{0,4},{4,0},{8,12},{12,8},{16,20},{20,16},{24,28},{28,24},{1,5},{5... | collective-permute-start | bytes 7864328 | tf_op jit(solution)/shard_map/ppermute | solution.py:762
  280.6 25.6 %collective-permute-start.18 = (f32[128,2048]{1,0:T(8,128)S(1)}, f32[128,2048]{1,0:T(8,128)S(1)}, u32[]{:S(2)}, u32[]{:S(2)}) collective-permute-start(f32[128,2048]{1,0:T(8,128)S(1)} %copy-done.17), channel_id=1, source_target_pairs={{0,16},{4,20},{8,24},{12,28},{16,0},{20,4},{24,8},{28,12},{1,17},{... | collective-permute-start | bytes 3145736 | tf_op jit(solution)/shard_map/ppermute | solution.py:762
  281.2 19.6 %collective-permute-start.19 = (f32[32,6144]{1,0:T(8,128)S(1)}, f32[32,6144]{1,0:T(8,128)S(1)}, u32[]{:S(2)}, u32[]{:S(2)}) collective-permute-start(f32[32,6144]{1,0:T(8,128)S(1)} %get-tuple-element.226), channel_id=1, source_target_pairs={{0,1},{1,0},{2,3},{3,2},{4,5},{5,4},{6,7},{7,6},{8,9},{9,8},{10,11... | collective-permute-start | bytes 2359304 | tf_op jit(solution)/shard_map/ppermute | solution.py:762
  282.7 20.5 %collective-permute-start.17 = (f32[128,1536]{1,0:T(8,128)S(1)}, f32[128,1536]{1,0:T(8,128)S(1)}, u32[]{:S(2)}, u32[]{:S(2)}) collective-permute-start(f32[128,1536]{1,0:T(8,128)S(1)} %get-tuple-element.223), channel_id=1, source_target_pairs={{0,8},{4,12},{8,0},{12,4},{16,24},{20,28},{24,16},{28,20},{1,9},{5... | collective-permute-start | bytes 2359304 | tf_op jit(solution)/shard_map/ppermute | solution.py:762
  307.8 29.8 %collective-permute-start.21 = (f32[128,1536]{1,0:T(8,128)S(1)}, f32[128,1536]{1,0:T(8,128)S(1)}, u32[]{:S(2)}, u32[]{:S(2)}) collective-permute-start(f32[128,1536]{1,0:T(8,128)S(1)} %get-tuple-element.232), channel_id=1, source_target_pairs={{0,16},{4,20},{8,24},{12,28},{16,0},{20,4},{24,8},{28,12},{1,17},{... | collective-permute-start | bytes 2359304 | tf_op jit(solution)/shard_map/ppermute | solution.py:762
  308.4 27.0 %collective-permute-start.23 = (f32[64,2048]{1,0:T(8,128)S(1)}, f32[64,2048]{1,0:T(8,128)S(1)}, u32[]{:S(2)}, u32[]{:S(2)}) collective-permute-start(f32[64,2048]{1,0:T(8,128)S(1)} %get-tuple-element.235), channel_id=1, source_target_pairs={{0,8},{4,12},{8,0},{12,4},{16,24},{20,28},{24,16},{28,20},{1,9},{5... | collective-permute-start | bytes 1572872 | tf_op jit(solution)/shard_map/ppermute | solution.py:762
  309.7 27.9 %collective-permute-start.20 = (f32[128,1024]{1,0:T(8,128)S(1)}, f32[128,1024]{1,0:T(8,128)S(1)}, u32[]{:S(2)}, u32[]{:S(2)}) collective-permute-start(f32[128,1024]{1,0:T(8,128)S(1)} %get-tuple-element.230), channel_id=1, source_target_pairs={{0,8},{4,12},{8,0},{12,4},{16,24},{20,28},{24,16},{28,20},{1,9},{5... | collective-permute-start | bytes 1572872 | tf_op jit(solution)/shard_map/ppermute | solution.py:762
  310.4 19.2 %collective-permute-start.24 = (f32[16,6144]{1,0:T(8,128)S(1)}, f32[16,6144]{1,0:T(8,128)S(1)}, u32[]{:S(2)}, u32[]{:S(2)}) collective-permute-start(f32[16,6144]{1,0:T(8,128)S(1)} %get-tuple-element.236), channel_id=1, source_target_pairs={{0,2},{1,3},{2,0},{3,1},{4,6},{5,7},{6,4},{7,5},{8,10},{9,11},{10,... | collective-permute-start | bytes 1179656 | tf_op jit(solution)/shard_map/ppermute | solution.py:762
  312.8 22.5 %collective-permute-start.22 = (f32[64,1536]{1,0:T(8,128)S(1)}, f32[64,1536]{1,0:T(8,128)S(1)}, u32[]{:S(2)}, u32[]{:S(2)}) collective-permute-start(f32[64,1536]{1,0:T(8,128)S(1)} %get-tuple-element.233), channel_id=1, source_target_pairs={{0,16},{4,20},{8,24},{12,28},{16,0},{20,4},{24,8},{28,12},{1,17},{... | collective-permute-start | bytes 1179656 | tf_op jit(solution)/shard_map/ppermute | solution.py:762
  336.0 18.0 %collective-permute-start.27 = (f32[32,3584]{1,0:T(8,128)S(1)}, f32[32,3584]{1,0:T(8,128)S(1)}, u32[]{:S(2)}, u32[]{:S(2)}) collective-permute-start(f32[32,3584]{1,0:T(8,128)S(1)} %get-tuple-element.242), channel_id=1, source_target_pairs={{0,1},{1,0},{2,3},{3,2},{4,5},{5,4},{6,7},{7,6},{8,9},{9,8},{10,11... | collective-permute-start | bytes 1376264 | tf_op jit(solution)/shard_map/ppermute | solution.py:762
  338.3 16.4 %collective-permute-start.26 = (f32[64,1536]{1,0:T(8,128)S(1)}, f32[64,1536]{1,0:T(8,128)S(1)}, u32[]{:S(2)}, u32[]{:S(2)}) collective-permute-start(f32[64,1536]{1,0:T(8,128)S(1)} %get-tuple-element.241), channel_id=1, source_target_pairs={{0,8},{4,12},{8,0},{12,4},{16,24},{20,28},{24,16},{28,20},{1,9},{5... | collective-permute-start | bytes 1179656 | tf_op jit(solution)/shard_map/ppermute | solution.py:762
  339.8 18.7 %collective-permute-start.30 = (f32[16,6144]{1,0:T(8,128)S(1)}, f32[16,6144]{1,0:T(8,128)S(1)}, u32[]{:S(2)}, u32[]{:S(2)}) collective-permute-start(f32[16,6144]{1,0:T(8,128)S(1)} %add_pair.3.refs_4_.mine_ref), channel_id=1, source_target_pairs={{0,2},{1,3},{2,0},{3,1},{4,6},{5,7},{6,4},{7,5},{8,10},{9,11},{10,... | collective-permute-start | bytes 1179656 | tf_op jit(solution)/shard_map/ppermute | solution.py:762
  359.1 32.7 %collective-permute-start.33 = (f32[32,6144]{1,0:T(8,128)S(1)}, f32[32,6144]{1,0:T(8,128)S(1)}, u32[]{:S(2)}, u32[]{:S(2)}) collective-permute-start(f32[32,6144]{1,0:T(8,128)S(1)} %join.6.rest_0_.mine_ref), channel_id=1, source_target_pairs={{0,1},{1,0},{2,3},{3,2},{4,5},{5,4},{6,7},{7,6},{8,9},{9,8},{10,11... | collective-permute-start | bytes 2359304 | tf_op jit(solution)/shard_map/ppermute | solution.py:762
  359.2 23.0 %collective-permute-start.29 = (f32[16,3584]{1,0:T(8,128)S(1)}, f32[16,3584]{1,0:T(8,128)S(1)}, u32[]{:S(2)}, u32[]{:S(2)}) collective-permute-start(f32[16,3584]{1,0:T(8,128)S(1)} %get-tuple-element.246), channel_id=1, source_target_pairs={{0,2},{1,3},{2,0},{3,1},{4,6},{5,7},{6,4},{7,5},{8,10},{9,11},{10,... | collective-permute-start | bytes 688136 | tf_op jit(solution)/shard_map/ppermute | solution.py:762
  361.3 30.0 %collective-permute-start.28 = (f32[32,2560]{1,0:T(8,128)S(1)}, f32[32,2560]{1,0:T(8,128)S(1)}, u32[]{:S(2)}, u32[]{:S(2)}) collective-permute-start(f32[32,2560]{1,0:T(8,128)S(1)} %get-tuple-element.245), channel_id=1, source_target_pairs={{0,1},{1,0},{2,3},{3,2},{4,5},{5,4},{6,7},{7,6},{8,9},{9,8},{10,11... | collective-permute-start | bytes 983048 | tf_op jit(solution)/shard_map/ppermute | solution.py:762
  395.2 14.7 %collective-permute-start.35 = (f32[32,3584]{1,0:T(8,128)S(1)}, f32[32,3584]{1,0:T(8,128)S(1)}, u32[]{:S(2)}, u32[]{:S(2)}) collective-permute-start(f32[32,3584]{1,0:T(8,128)S(1)} %join.8.rest_0_.mine_ref), channel_id=1, source_target_pairs={{0,1},{1,0},{2,3},{3,2},{4,5},{5,4},{6,7},{7,6},{8,9},{9,8},{10,11... | collective-permute-start | bytes 1376264 | tf_op jit(solution)/shard_map/ppermute | solution.py:762
  (51 other events, 326.0 us)
Sparse Core Ops, SparseCore 0:
  136.5 83.8 reduce-scatter.1

commit v3 on v2

--- a/solution.py
+++ b/solution.py
@@ -17,7 +17,7 @@
 EPS = 1e-05
 F32 = jnp.float32
 BF16 = jnp.bfloat16
-LIMIT = 56
+LIMIT = 32
 READ_SCALE = STATE ** (-0.5)
 
 
@@ -92,7 +92,7 @@
     lane = iota((STATE, 128), 1)
     full[...] = jnp.zeros_like(full)
     for a in range(4):
-        pair = ref[0, a, :STATE, :]
+        pair = ref[0, STATE * a : STATE * (a + 1), :]
         full[64 * a : 64 * a + 32, 128 * a : 128 * a + 128] = jnp.where(
             lane < HEADP, pair, 0.0
         ).astype(BF16)
@@ -126,7 +126,7 @@
     parts.append(jnp.zeros((steps, WIDE - SUB * parts[0].shape[1]), F32))
     stacked = jnp.concatenate(parts, axis=1).astype(BF16)
     flat[0] = stacked
-    x0 = dot(stacked, w_sub[...])
+    x0 = dot_t(stacked[:, : w_sub.shape[1]], w_sub[...])
     low, scale = norm(x0, g1[...])
     a1[0] = low
     r1[0] = scale
@@ -177,8 +177,9 @@
     block = sum(dot(part, spread_values) for part in split_three(head[steps - 8 :, :]))
     block = block[7:8, :] * keep[0, pl.program_id(0)]
     for a, pair in enumerate(pack_state(t_dot(tailed, u_low))):
-        state[0, a, :STATE, :] = pair
-        state[0, a, STATE:, :] = jnp.broadcast_to(block[:, 128 * a : 128 * a + 128], (8, 128))
+        state[0, STATE * a : STATE * (a + 1), :] = pair
+    lines = [block[:, 128 * a : 128 * a + 128] for a in range(4)]
+    state[0, 4 * STATE :, :] = jnp.concatenate(lines + lines, axis=0)
 
 
 def mix_kernel(u, bs, c, cum, cum_t, mixed, pairs, decay_pairs):
@@ -375,11 +376,11 @@
     gy[0] = read_grad
     row = pl.program_id(0)
     for a, pair in enumerate(pack_state(t_dot(ce[0], read_grad))):
-        pulled[0, a, :STATE, :] = pair * keep[0, row]
-        pulled[0, a, STATE:, :] = block[0, a, STATE:, :]
-
-
-def mix_back_kernel(u, bs, c, ee, gy, start, pairs, decay_pairs, _, gu, gb, gc, full):
+        pulled[0, STATE * a : STATE * (a + 1), :] = pair * keep[0, row]
+    pulled[0, 4 * STATE :, :] = block[0, 4 * STATE :, :]
+
+
+def mix_back_kernel(u, bs, c, ee, gy, start, pairs, decay_pairs, _, __, gu, gb, gc, full):
     steps = u.shape[1]
     unpack_state(start, full)
     reads_grad = dot_t(gy[0], full[...]) * ee[0].astype(F32)
@@ -486,19 +487,24 @@
             place[pl.ds(to, share), :] = rows[share * piece : share * (piece + 1), :]
 
 
-def weights_kernel(pairs, share, waits):
+def weights_kernel(pairs, share, waits, cuts):
     has_small = pairs[-1] == (1, 0)
 
     def kernel(core_ref, *refs):
         count = len(pairs)
         lefts, rights = refs[:count], refs[count : 2 * count]
-        extra = refs[2 * count] if has_small else None
-        kept, sent = refs[2 * count + has_small + waits :][:2]
-        places = refs[2 * count + has_small + waits + 2 :]
+        lines = refs[2 * count : 2 * count + 6 * has_small]
+        kept, *sents = refs[2 * count + 6 * has_small + waits :][: len(cuts)]
+        places = refs[2 * count + 6 * has_small + waits + len(cuts) :]
+
+        def send(change):
+            for sent, low, high in zip(sents, cuts, cuts[1:]):
+                pl.when((step >= low) & (step < high))(lambda sent=sent: change(sent))
+
         step = pl.program_id(0)
         core = core_ref[0]
         start = 0
-        for (wide, long), left, right, place in zip(pairs, lefts, rights, places):
+        for (wide, long), left, right, place in zip(pairs, lefts, rights, places[:count]):
             steps = max(wide, long)
 
             @pl.when(step == start)
@@ -516,22 +522,28 @@
                     rows = place[pl.ds(pl.multiple_of((step - start) * D, D), D), :]
                 block = dot(rows, right[...])
                 kept[...] = block[: D // 2, :]
-                sent[...] = block[D // 2 :, :]
+
+                def put(sent):
+                    sent[...] = block[D // 2 :, :]
+
+                send(put)
 
             start += steps
         if has_small:
 
             @pl.when(step == start - 1)
             def _():
+                stacked = jnp.concatenate([line[...] for line in lines] + [jnp.zeros((107, D), F32)], axis=0)
+                places[-1][...] = stacked.T
                 for s in range(D // share // 2):
-                    for out, side in ((kept, core), (sent, 1 - core)):
+                    for out, side in ((kept, core), (sents[-1], 1 - core)):
                         at = pl.multiple_of((2 * s + side) * share, 8)
-                        out[s * share : (s + 1) * share, :] += extra[pl.ds(at, share), :]
+                        out[s * share : (s + 1) * share, D - 128 :] = places[-1][pl.ds(at, share), :]
 
     return kernel
 
 
-def weight_sums(pairs, share, core, small=None, after=()):
+def weight_sums(pairs, share, core, small=None, after=(), pieces=1):
     tokens = pairs[0][0].shape[0]
     sizes = [(l.shape[1] // D, r.shape[1] // D) for l, r in pairs]
     if small is not None:
@@ -547,17 +559,24 @@
             rights.append((right, "all"))
         start += steps
     columns = start * D
-    extra = [] if small is None else [(small, "all")]
-    half = ((D // 2, columns), F32, pl.BlockSpec((D // 2, D), lambda j: (0, j)))
-    return call(
-        weights_kernel(sizes, share, len(after)),
+    extra = [] if small is None else [(line, "all") for line in small]
+    cuts = [start * i // pieces for i in range(pieces + 1)]
+
+    def half(low, high):
+        index = lambda j: (0, jnp.clip(j - low, 0, high - low - 1))
+        return ((D // 2, D * (high - low)), F32, pl.BlockSpec((D // 2, D), index))
+
+    kept, *sent, token = call(
+        weights_kernel(sizes, share, len(after), cuts),
         (start,),
         [(core, scalars())] + lefts + rights + extra + [(a, anywhere()) for a in after],
-        [half, half],
-        [pltpu.VMEM((D * wide, tokens), BF16) for wide, _ in sizes],
+        [half(0, start)] + [half(low, high) for low, high in zip(cuts, cuts[1:])],
+        [pltpu.VMEM((D * wide, tokens), BF16) for wide, _ in sizes]
+        + [pltpu.VMEM((D, 128), F32)] * (small is not None),
         2 * tokens * D * columns,
         "weights",
     )
+    return kept, sent, token
 
 
 def row_spec(shape):
@@ -581,57 +600,104 @@
     return pl.BlockSpec(memory_space=pl.ANY)
 
 
-TIMES = {'front': 19, 'mix': 6, 'lift': 8, 'depth': 6, 'late': 22, 'late_weights': 10, 'depth_grad': 7, 'conv_back': 11, 'mix_back': 11, 'mix_end': 8, 'front_back': 13, 'weights': 9}
-
-
-def call(kernel, grid, ins, outs, scratch=(), flops=0, name=None, room=LIMIT):
+ROOM = {'front': 44, 'mix': 24, 'lift': 28, 'depth': 20, 'late': 44, 'late_weights': 36, 'depth_grad': 20, 'conv_back': 28, 'mix_back': 28, 'mix_end': 24, 'front_back': 32, 'weights': 28}
+TIMES = {'front': 60.0, 'mix': 21.0, 'lift': 27.0, 'depth': 18.0, 'late': 69.0, 'late_weights': 33.0, 'depth_grad': 21.0, 'conv_back': 33.0, 'mix_back': 36.0, 'mix_end': 30.0, 'front_back': 42.0, 'weights': 30.0}
+
+
+def call(kernel, grid, ins, outs, scratch=(), flops=0, name=None):
+    def placed(array, kind):
+        if kind not in ("row", "all") and kind.memory_space is not None:
+            return array
+        return pltpu.with_memory_space_constraint(array, pltpu.HBM)
+
     def made(kind, shape):
         if kind == "row":
             return row_spec(shape)
         return whole_spec(shape) if kind == "all" else kind
 
     moved = sum(a.size * a.dtype.itemsize for a, _ in ins)
-    return pl.pallas_call(
-        kernel,
+    inner = len(ins) + len(outs)
+
+    def with_token(*refs):
+        kernel(*refs[:inner], *refs[inner + 1 :])
+        refs[inner][...] = jnp.zeros((8, 128), F32)
+
+    *made_arrays, token = pl.pallas_call(
+        with_token,
         grid=grid,
         in_specs=[held_spec(a.shape) if kind == "all" else made(kind, a.shape) for a, kind in ins],
-        out_specs=[made(kind, shape) for shape, _, kind in outs],
-        out_shape=[jax.ShapeDtypeStruct(shape, kind) for shape, kind, _ in outs],
+        out_specs=[made(kind, shape) for shape, _, kind in outs] + [whole_spec((8, 128))],
+        out_shape=[pltpu.HBM(shape, kind) for shape, kind, _ in outs] + [pltpu.HBM((8, 128), F32)],
         scratch_shapes=list(scratch),
         compiler_params=pltpu.CompilerParams(
-            dimension_semantics=("arbitrary",), vmem_limit_bytes=room * 2**20
+            dimension_semantics=("arbitrary",), vmem_limit_bytes=ROOM[name] * 2**20
         ),
         cost_estimate=pl.CostEstimate(
             flops=int(TIMES[name] * 1.15e9), bytes_accessed=0, transcendentals=0
         ),
         name=name,
-    )(*[a for a, _ in ins])
+    )(*[placed(a, kind) for a, kind in ins])
+    return (*made_arrays, token)
 
 
 def flip_pairs(count, mask):
     return [(i, i ^ mask) for i in range(count)]
 
 
-def entering(value, backward):
-    count, mine = lax.axis_size("seq"), lax.axis_index("seq")
-
-    def link(earlier, later):
-        decay = later[:, :, STATE : STATE + 1, :]
-        state = decay * earlier[:, :, :STATE, :] + later[:, :, :STATE, :]
-        return jnp.concatenate([state, decay * earlier[:, :, STATE:, :]], axis=2)
-
-    shape = value.shape[:2] + (STATE, value.shape[3])
-    before = jnp.concatenate(
-        [jnp.zeros(shape, F32), jnp.ones(value.shape[:2] + (8, value.shape[3]), F32)], axis=2
-    )
-    mask = 1
-    while mask < count:
-        other = lax.ppermute(value, "seq", flip_pairs(count, mask))
-        second = ((mine & mask) != 0) != backward
-        before = jnp.where(second, link(other, before), before)
-        value = jnp.where(second, link(other, value), link(value, other))
-        mask *= 2
-    return before
+def hop_kernel(backward, first, keep_state):
+    def kernel(keep, second_ref, value, other, *refs):
+        before, (out, out_before, token) = (None, refs) if first else (refs[0], refs[1:])
+        token[...] = jnp.zeros((8, 128), F32)
+        second = (second_ref[0] != 0) != backward
+        rows = value.shape[0]
+        decay_rows = slice(4 * STATE, 4 * STATE + 8)
+        for r in range(rows):
+            here, there = value[r, decay_rows, :], other[r, decay_rows, :]
+            out[r, decay_rows, :] = here * there
+            if first:
+                entered = jnp.where(second, there, 1.0)
+            else:
+                entered = before[r, decay_rows, :]
+                entered = jnp.where(second, entered * there, entered)
+            out_before[r, decay_rows, :] = entered
+            for a in range(4):
+                at = slice(STATE * a, STATE * (a + 1))
+                mine, others = value[r, at, :], other[r, at, :]
+                mine_decay, other_decay = here[a : a + 1, :], there[a : a + 1, :]
+                out[r, at, :] = jnp.where(
+                    second, mine_decay * others + mine, other_decay * mine + others
+                )
+                if first:
+                    entered = jnp.where(second, others, 0.0)
+                else:
+                    entered = before[r, at, :]
+                    own = before[r, 4 * STATE + a : 4 * STATE + a + 1, :]
+                    entered = jnp.where(second, own * others + entered, entered)
+                out_before[r, at, :] = entered * keep[0, r] if keep_state else entered
+
+    return kernel
+
+
+def entering(value, backward, keep):
+    count, place = lax.axis_size("seq"), lax.axis_index("seq")
+    vmem = pl.BlockSpec(memory_space=pltpu.VMEM)
+    shape = jax.ShapeDtypeStruct(value.shape, F32)
+    before, tokens = [], []
+    for bit in range(count.bit_length() - 1):
+        other = lax.ppermute(value, "seq", flip_pairs(count, 1 << bit))
+        last = (2 << bit) == count
+        value, entered, token = pl.pallas_call(
+            hop_kernel(backward, bit == 0, last and not backward),
+            in_specs=[scalars(), scalars()] + [vmem] * (2 + len(before)),
+            out_specs=[vmem] * 3,
+            out_shape=[shape, shape, jax.ShapeDtypeStruct((8, 128), F32)],
+            compiler_params=pltpu.CompilerParams(vmem_limit_bytes=8 * 2**20),
+            cost_estimate=pl.CostEstimate(flops=0, bytes_accessed=0, transcendentals=0),
+            name="hop",
+        )(keep, ((place >> bit) & 1).reshape(1), value, other, *before)
+        before = [entered]
+        tokens.append(token)
+    return before[0], tokens
 
 
 def halos(top, bottom):
@@ -653,16 +719,16 @@
     return lax.psum_scatter(value, "seq", scatter_dimension=0, tiled=True)
 
 
-def in_vmem(kernel, scalars_in, ins, outs, after, name):
+def in_vmem(kernel, scalars_in, ins, outs, after, name, cost=0):
     vmem = pl.BlockSpec(memory_space=pltpu.VMEM)
     return pl.pallas_call(
         kernel,
         in_specs=[scalars()] + [vmem] * len(ins) + [anywhere()] * len(after),
-        out_specs=[vmem] * len(outs),
-        out_shape=[jax.ShapeDtypeStruct(shape, F32) for shape in outs],
-        compiler_params=pltpu.CompilerParams(vmem_limit_bytes=32 * 2**20),
+        out_specs=[vmem] * len(outs) + [vmem],
+        out_shape=[jax.ShapeDtypeStruct(shape, F32) for shape in outs + [(8, 128)]],
+        compiler_params=pltpu.CompilerParams(vmem_limit_bytes=8 * 2**20),
         cost_estimate=pl.CostEstimate(
-            flops=0, bytes_accessed=0, transcendentals=0
+            flops=int(cost * 1.15e9), bytes_accessed=0, transcendentals=0
         ),
         name=name,
     )(scalars_in, *ins, *after)
@@ -676,7 +742,7 @@
     return ref[pl.ds(pl.multiple_of((2 * group + side) * chunk, 8), chunk), columns]
 
 
-def add_and_split(bits, groups, after):
+def split_task(groups):
     arrays, outs, plan = [], [], []
 
     def known(array):
@@ -689,82 +755,96 @@
     for items, chunk, bit in groups:
         rows = items[0][0].shape[0]
         placed, at = [], 0
-        for kept, received, first, columns in items:
-            placed.append(
-                (known(kept), None if received is None else known(received), first, columns, at)
-            )
+        for kept, first, received, other_first, columns in items:
+            there = None if received is None else known(received)
+            placed.append((known(kept), first, there, other_first, columns, at))
             at += columns
         plan.append((placed, rows, chunk, bit, len(outs)))
         outs += [(rows // 2, at)] * 2
-    count = len(arrays) + len(after)
-
-    def kernel(bit_ref, *refs):
+
+    def body(bit_ref, ins, made):
         for placed, rows, chunk, bit, out in plan:
             mine = bit_ref[bit]
-            for kept, received, first, columns, at in placed:
-                for target, side in ((refs[count + out], mine), (refs[count + out + 1], 1 - mine)):
+            for kept, first, received, other_first, columns, at in placed:
+                mine_at = slice(first, first + columns)
+                other_at = slice(other_first, other_first + columns)
+                for target, side in ((made[out], mine), (made[out + 1], 1 - mine)):
                     for group in range(rows // chunk // 2):
-                        value = part_rows(refs[kept], group, chunk, side, slice(first, first + columns))
+                        value = part_rows(ins[kept], group, chunk, side, mine_at)
                         if received is not None:
-                            value = value + part_rows(
-                                refs[received], group, chunk, side, slice(first, first + columns)
-                            )
+                            value = value + part_rows(ins[received], group, chunk, side, other_at)
                         target[group * chunk : (group + 1) * chunk, at : at + columns] = value
 
-    made = in_vmem(kernel, bits, arrays, outs, after, "add_and_split")
-    return [(made[i], made[i + 1]) for i in range(0, len(made), 2)]
-
-
-def add_pair(bits, kept, received, after):
-    def kernel(_, a, b, *rest):
-        rest[-1][...] = a[...] + b[...]
-
-    return in_vmem(kernel, bits, [kept, received], [kept.shape], after, "add_pair")[0]
-
-
-def join(bits, mine, other, bit, after, pieces=None):
+    return arrays, outs, body
+
+
+def add_task(kept, received):
+    def body(_, ins, made):
+        made[0][...] = ins[0][...] + ins[1][...]
+
+    return [kept, received], [kept.shape], body
+
+
+def join_task(mine, other, bit, pieces=None):
     rows, columns = mine.shape
-    outs = [(2 * rows, columns)]
-    if pieces is not None:
-        outs = [(8 * rows, D) if spread else (2 * rows, wide) for _, wide, spread in pieces]
     cuts = [(0, columns, False)] if pieces is None else pieces
-
-    def kernel(bit_ref, mine_ref, other_ref, *rest):
+    outs = [(8 * rows, D) if spread else (2 * rows, wide) for _, wide, spread in cuts]
+
+    def body(bit_ref, ins, made):
         first = bit_ref[bit] == 0
-        targets = rest[len(after) :]
-        for target, (at, wide, spread) in zip(targets, cuts):
+        for target, (at, wide, spread) in zip(made, cuts):
             for k in range(4 if spread else 1):
                 width = D if spread else wide
-                left = mine_ref[:, at + D * k : at + D * k + width]
-                right = other_ref[:, at + D * k : at + D * k + width]
+                left = ins[0][:, at + D * k : at + D * k + width]
+                right = ins[1][:, at + D * k : at + D * k + width]
                 start = 2 * rows * k
                 target[start : start + rows, :] = jnp.where(first, left, right)
                 target[start + rows : start + 2 * rows, :] = jnp.where(first, right, left)
 
-    made = in_vmem(kernel, bits, [mine, other], outs, after, "join")
-    return made[0] if pieces is None else made
+    return [mine, other], outs, body
+
+
+def together(bits, sums, after, cost=0):
+    tasks = [one.step() for one in sums]
+    arrays = [array for ins, _, _, _ in tasks for array in ins]
+    outs = [shape for _, shapes, _, _ in tasks for shape in shapes]
+    count = len(arrays) + len(after)
+
+    def kernel(bit_ref, *refs):
+        at, out = 0, count
+        for ins, shapes, body, _ in tasks:
+            body(bit_ref, refs[at : at + len(ins)], refs[out : out + len(shapes)])
+            at, out = at + len(ins), out + len(shapes)
+        refs[-1][...] = jnp.zeros((8, 128), F32)
+
+    *made, token = in_vmem(kernel, bits, arrays, outs, after, "together", cost)
+    for _, shapes, _, commit in tasks:
+        commit(made[: len(shapes)])
+        made = made[len(shapes) :]
+    return token
 
 
 class Sum:
-    def __init__(self, bits, pieces):
-        self.bits = bits
+    def __init__(self, pieces):
         self.pieces = pieces
-        self.seq = lax.axis_size("seq")
-        self.rec = lax.axis_size("rec")
-        self.chip_bits = self.seq.bit_length() - 2
-        self.rec_bits = self.rec.bit_length() - 1
-        self.parts = []
-        self.left = []
-        self.steps = []
+        self.chip_bits = lax.axis_size("seq").bit_length() - 2
+        self.rec_bits = lax.axis_size("rec").bit_length() - 1
+        self.parts, self.left, self.steps, self.beside = [], [], [], []
         self.done = None
 
     def swap(self, value, axis, bit):
         return lax.ppermute(value, axis, flip_pairs(lax.axis_size(axis), 1 << bit))
 
     def begin(self, kept, sent, first):
-        columns = kept.shape[1]
-        received = self.swap(sent, "seq", 0)
-        self.parts = [[(kept, received, 0, first)], [(kept, received, first, columns - first)]]
+        self.parts = [[], []]
+        at = 0
+        for piece in sent:
+            received = self.swap(piece, "seq", 0)
+            end = at + piece.shape[1]
+            for part, low, high in ((0, at, min(end, first)), (1, max(at, first), end)):
+                if low < high:
+                    self.parts[part].append((kept, low, received, low - at, high - low))
+            at = end
         turn = 1 + self.chip_bits // 2
         orders = (
             list(range(1, self.chip_bits + 1)),
@@ -772,45 +852,53 @@
         )
         self.left = [list(range(self.chip_bits, 0, -1)) for _ in orders]
         self.steps += [("chips", now) for now in zip(*orders)]
-        self.finish_steps()
-
-    def finish_steps(self):
         self.steps += [("rec", bit) for bit in range(self.rec_bits)] + [("turn", self.rec_bits - 1)]
         self.steps += [("join", bit) for bit in reversed(range(self.rec_bits))]
 
-    def advance(self, after):
+    def step(self):
         kind, now = self.steps.pop(0)
         if kind == "chips":
             groups = []
             for items, bit, left in zip(self.parts, now, self.left):
-                rows = items[0][0].shape[0]
-                chunk = rows >> (left.index(bit) + 1)
+                chunk = items[0][0].shape[0] >> (left.index(bit) + 1)
                 left.remove(bit)
                 groups.append((items, chunk, bit))
-            made = add_and_split(self.bits, groups, after)
-            self.parts = [
-                [(kept, self.swap(sent, "seq", bit), 0, kept.shape[1])]
-                for (kept, sent), bit in zip(made, now)
-            ]
-            return made[0][0]
+
+            def commit(made):
+                self.parts = [
+                    [(made[2 * i], 0, self.swap(made[2 * i + 1], "seq", bit), 0, made[2 * i].shape[1])]
+                    for i, bit in enumerate(now)
+                ]
+
+            return *split_task(groups), commit
         if kind == "rec":
-            items = [item for part in self.parts for item in part]
-            groups = [(items, items[0][0].shape[0] // 2, self.chip_bits + 1 + now)]
-            [(kept, sent)] = add_and_split(self.bits, groups, after)
-            self.parts = [[(kept, self.swap(sent, "rec", now), 0, kept.shape[1])]]
-            return kept
+            items = [item for part in self.beside + self.parts for item in part]
+            self.beside = []
+
+            def commit(made):
+                kept, sent = made
+                self.parts = [[(kept, 0, self.swap(sent, "rec", now), 0, kept.shape[1])]]
+
+            chunk = items[0][0].shape[0] // 2
+            return *split_task([(items, chunk, self.chip_bits + 1 + now)]), commit
         if kind == "turn":
-            [[(kept, received, _, _)]] = self.parts
-            self.mine = add_pair(self.bits, kept, received, after)
-            self.other = self.swap(self.mine, "rec", now)
-            return self.mine
-        bit = self.chip_bits + 1 + now
-        if now == 0:
-            self.done = join(self.bits, self.mine, self.other, bit, after, self.pieces)
-            return self.done[0]
-        self.mine = join(self.bits, self.mine, self.other, bit, after)
-        self.other = self.swap(self.mine, "rec", now - 1)
-        return self.mine
+            [[(kept, _, received, _, _)]] = self.parts
+
+            def commit(made):
+                [self.mine] = made
+                self.other = self.swap(self.mine, "rec", now)
+
+            return *add_task(kept, received), commit
+
+        def commit(made):
+            if now == 0:
+                self.done = made
+                return
+            [self.mine] = made
+            self.other = self.swap(self.mine, "rec", now - 1)
+
+        pieces = self.pieces if now == 0 else None
+        return *join_task(self.mine, self.other, self.chip_bits + 1 + now, pieces), commit
 
 
 def local(
@@ -834,7 +922,6 @@
     keep = (jnp.stack([keep_here, keep_next]), scalars())
     tk = (time_keep.reshape(rows, steps, SUB).astype(F32), "row")
     fk = (freq_keep[:, None, :].astype(F32), "row")
-    sub_wide = jnp.pad(w_sub, ((0, 0), (0, WIDE - SUB * mels)))
     g1, g2, g3, g4, g5, bg, bb = (
         (gain.reshape(1, D), "all")
         for gain in (ln1_gain, ln2_gain, ln3_gain, ln4_gain, ln5_gain, bn_gain, bn_shift)
@@ -844,7 +931,8 @@
     def rows_of(width, kind=F32):
         return ((rows, steps, width), kind, "row")
 
-    per_state = ((rows, 4, STATE + 8, 128), F32, "row")
+
+    per_state = ((rows, 4 * STATE + 8, 128), F32, "row")
     edge = ((rows, 8, D), F32, "row")
     line = ((1, D), F32, "all")
     two_lines = ((2, D), F32, "all")
@@ -857,12 +945,12 @@
     def every(value):
         return (value, "all")
 
-    (flat, x1, a1, r1, s1, d1, a2, r2, u, g, bs, c, ce, bt, se, ee, te, cum, cum_t, state) = call(
+    (flat, x1, a1, r1, s1, d1, a2, r2, u, g, bs, c, ce, bt, se, ee, te, cum, cum_t, state, _) = call(
         front_kernel,
         (rows,),
         [
             row(features), tk, fk, row(decays), row(decays.transpose(0, 2, 1)), keep,
-            every(sub_wide.T), g1, every(ffn1_in), every(ffn1_out), g2, every(ssm_in),
+            every(w_sub), g1, every(ffn1_in), every(ffn1_out), g2, every(ssm_in),
         ],
         [
             rows_of(WIDE, BF16), rows_of(D), rows_of(D, BF16), rows_of(1), rows_of(FF, BF16),
@@ -875,10 +963,9 @@
         2 * tokens * D * (WIDE + 2 * FF + PROJ),
         "front",
     )
-    before = entering(state, False)
-    start = before * keep_here[:, None, None, None]
+    start, _ = entering(state, False, keep[0])
     pair_shape = ((rows, HEADS, steps, steps), BF16, "row")
-    mixed, pairs, decay_pairs = call(
+    mixed, pairs, decay_pairs, _ = call(
         mix_kernel,
         (rows,),
         [row(u), row(bs), row(c), row(cum), row(cum_t)],
@@ -887,7 +974,7 @@
         2 * tokens * 256 * 256 * 16,
         "mix",
     )
-    z, gs, yd, x2, a3, r3, v, sq, cq, top, bottom = call(
+    z, gs, yd, x2, a3, r3, v, sq, cq, top, bottom, _ = call(
         lift_kernel,
         (rows,),
         [row(mixed), row(ce), row(start), row(g), row(x1), every(ssm_out), g3, every(conv_in)],
@@ -900,7 +987,7 @@
         "lift",
     )
     v_before, v_after = halos(top, bottom)
-    dc, sums = call(
+    dc, sums, _ = call(
         depth_kernel,
         (rows,),
         [row(v), row(v_before), row(v_after), keep, taps],
@@ -910,7 +997,7 @@
         "depth",
     )
     stats = sum_over_all(sums)
-    out, e, a4, s4, gf4, gh4, ge, gx3, gbn, back_sums, ln4, ln5 = call(
+    out, e, a4, s4, gf4, gh4, ge, gx3, gbn, back_sums, ln4, ln5, _ = call(
         late_kernel(count),
         (rows,),
         [
@@ -936,7 +1023,7 @@
     def row_block(columns):
         return ((D, columns), F32, pl.BlockSpec((256, columns), lambda i: (i, 0)))
 
-    (late_grads,) = call(
+    late_grads, late_token = call(
         late_weights_kernel(share),
         (2,),
         [
@@ -948,7 +1035,7 @@
         2 * tokens * D * (2 * FF + D),
         "late_weights",
     )
-    group_a = scatter_sum(late_grads)
+    scattered_a = scatter_sum(late_grads)
 
     def edge_grad(at):
         return batch_back(
@@ -958,19 +1045,19 @@
         )
 
     gd_before, gd_after = halos(edge_grad(0), edge_grad(steps - 8))
-    gd, taps_grad = call(
+    gd, taps_grad, _ = call(
         depth_grad_kernel(count),
         (rows,),
         [
             row(gbn), row(dc), every(stats), every(back), bg, row(v), row(v_before), row(v_after), keep,
-            (late_grads, anywhere()),
+            (late_token, anywhere()),
         ],
         [rows_of(D), ((16, D), F32, "all")],
         [padded],
         2 * tokens * D * 64,
         "depth_grad",
     )
-    gq, gx2, gz, gy, gg, pulled, ln3 = call(
+    gq, gx2, gz, gy, gg, pulled, ln3, _ = call(
         conv_back_kernel,
         (rows,),
         [
@@ -985,35 +1072,36 @@
         2 * tokens * D * 4 * D,
         "conv_back",
     )
-    end = entering(pulled, True)
+    end, hops = entering(pulled, True, keep[0])
     core = (place % 2).reshape(1)
-    kept, sent = weight_sums([(flatten(a3), flatten(gq)), (flatten(z), flatten(gz))], share, core)
+    kept, sent, weights_token = weight_sums(
+        [(flatten(a3), flatten(gq)), (flatten(z), flatten(gz))], share, core, None, hops[:-2]
+    )
     bits = jnp.stack(
         [(place >> k) & 1 for k in range(blocks.bit_length() - 1)]
         + [(lax.axis_index("rec") >> k) & 1 for k in range(lax.axis_size("rec").bit_length() - 1)]
     )
     early = Sum(
-        bits,
         [
             (0, FF, False), (FF, FF, True), (2 * FF, D, False), (2 * FF + D, 2 * D, False),
             (2 * FF + 3 * D, D, False),
         ],
     )
     early.begin(kept, sent, D)
-    gu, gb, gc = call(
+    gu, gb, gc, mixed_token = call(
         mix_back_kernel,
         (rows,),
         [
             row(u), row(bs), row(c), row(ee), row(gy), row(start), row(pairs), row(decay_pairs),
-            (sent, anywhere()),
+            (weights_token, anywhere()), (hops[-2], anywhere()),
         ],
         [rows_of(D), rows_of(256), rows_of(256, BF16)],
         [full],
         2 * tokens * 256 * 256 * 32,
         "mix_back",
     )
-    token = early.advance([gu])
-    gp, gx1, gf1, ln2 = call(
+    token = together(bits, [early], [mixed_token])
+    gp, gx1, gf1, ln2, end_token = call(
         mix_end_kernel,
         (rows,),
         [
@@ -1025,46 +1113,44 @@
         2 * tokens * D * PROJ,
         "mix_end",
     )
-    token = early.advance([gf1])
-    kept, sent = weight_sums(
+    token = together(bits, [early], [end_token])
+    kept, sent, weights_token = weight_sums(
         [(flatten(a2), flatten(gp)), (flatten(s1), flatten(gf1))], share, core, None, [token]
     )
-    middle = Sum(bits, [(0, PROJ, False), (PROJ, FF, True)])
+    middle = Sum([(0, PROJ, False), (PROJ, FF, True)])
     middle.begin(kept, sent, PROJ)
-    gh1, gxr, features_grad, ln1 = call(
+    token = weights_token
+    while early.steps[0][0] == "chips":
+        token = together(bits, [early], [token])
+    early.parts = [[(scattered_a, 0, None, 0, scattered_a.shape[1])]] + early.parts
+    token = together(bits, [early], [token])
+    gh1, gxr, features_grad, ln1, back_token = call(
         front_back_kernel,
         (rows,),
         [
             row(gx1), row(gf1), every(ffn1_out), row(d1), every(ffn1_in), row(a1), row(r1), g1,
-            every(sub_wide), tk, fk, (sent, anywhere()),
+            every(w_sub), tk, fk, (token, anywhere()),
         ],
         [rows_of(FF, BF16), rows_of(D, BF16), ((rows, frame_count, mels), F32, "row"), line],
         (),
         2 * tokens * D * (WIDE + 2 * FF),
         "front_back",
     )
-    small = jnp.concatenate(
-        [ln1, ln2, ln3, ln4, ln5, taps_grad[:KERNEL], jnp.zeros((WIDE - SUB * mels - 20, D), F32)],
-        axis=0,
-    )
-    small = jnp.pad(small.T, ((0, 0), (SUB * mels, 0)))
-    token = middle.advance([ln1])
-    while early.steps[0][0] == "chips":
-        token = early.advance([token])
-    early.parts = [[(group_a, None, 0, group_a.shape[1])]] + early.parts
-    token = early.advance([token])
-    last = Sum(bits, [(0, FF, False), (FF, SUB * mels, False), (FF + SUB * mels, 24, False)])
-    kept, sent = weight_sums(
-        [(flatten(a1), flatten(gh1)), (flatten(gxr), flatten(flat))], share, core, small, [token]
+    small = [taps_grad, ln1, ln2, ln3, ln4, ln5]
+    token = together(bits, [early, middle], [back_token])
+    last = Sum([(0, FF, False), (FF, SUB * mels, False), (FF + D - 128, 128, False)])
+    kept, sent, weights_token = weight_sums(
+        [(flatten(a1), flatten(gh1)), (flatten(gxr), flatten(flat))], share, core, small, [token], 1
     )
     last.begin(kept, sent, 2 * D)
-    order = [early, middle, last, early, middle, last, middle, last, early, middle, last, early, middle, last]
-    order += [middle, last]
-    token = sent
-    while any(group.steps for group in (early, middle, last)):
-        group = order.pop(0) if order else next(g for g in (early, middle, last) if g.steps)
-        if group.steps:
-            token = group.advance([token])
+    token = weights_token
+    token = together(bits, [early, middle], [token], 60.0)
+    rounds = [(last,), (early, middle, last), (middle, last)]
+    while early.steps or middle.steps or last.steps:
+        now = rounds.pop(0) if rounds else (early, middle, last)
+        now = [one for one in now if one.steps]
+        if now:
+            token = together(bits, now, [token])
     ffn2_in_grad, ffn2_out_grad, conv_out_grad, conv_in_grad, ssm_out_grad = early.done
     ssm_in_grad, ffn1_out_grad = middle.done
     ffn1_in_grad, w_sub_grad, gains = last.done
@@ -1074,22 +1160,22 @@
         out,
         features_grad,
         w_sub_grad,
-        gains[:, 0],
+        gains[:, 16],
         ffn1_in_grad,
         ffn1_out_grad,
-        gains[:, 1],
+        gains[:, 17],
         ssm_in_grad,
         ssm_out_grad,
-        gains[:, 2],
+        gains[:, 18],
         conv_in_grad,
-        gains[:, 5 : 5 + KERNEL],
+        gains[:, :KERNEL],
         lax.dynamic_slice_in_dim(back[0], start_row, share),
         lax.dynamic_slice_in_dim(back[1], start_row, share),
         conv_out_grad,
-        gains[:, 3],
+        gains[:, 19],
         ffn2_in_grad,
         ffn2_out_grad,
-        gains[:, 4],
+        gains[:, 20],
     )
 
 

time: 435 us -> 422 us (0.970)
  local copies, waits for them, and re-layouts: 33.9 us -> 23.5 us
  waiting for transfers between devices: 128 us -> 136 us
  other arithmetic: 10.1 us -> 3.22 us
  starting transfers between devices: 52 us -> 47.1 us
    ppermute x27, waiting for transfers between devices: 98.8 us -> 116 us  [swap(): return lax.ppermute(value, axis, flip_pairs(lax.axis_size(axis), 1 << bit))]
    all_to_all x1, waiting for transfers between devices: 8.19 us -> 0.01 us  [sum_over_all(): return jnp.sum(lax.all_to_all(copies, ('rec', 'seq'), 0, 0), axis=0)]
    pallas_call x14 -> x20, Pallas kernels: 159 us -> 167 us  [the longest x14 161 us: call(): pl.pallas_call(with_token, grid=grid, in_specs=[held_spec(a.shape) if kin...]
    ppermute x27, starting transfers between devices: 33.2 us -> 26.4 us  [swap(): return lax.ppermute(value, axis, flip_pairs(lax.axis_size(axis), 1 << bit))]
    pallas_call x21 -> x12, Pallas kernels: 18.7 us -> 13 us  [in_vmem(): pl.pallas_call(kernel, in_specs=[scalars()] + [vmem] * len(ins) + [anywhe...]
    unnamed x77 -> x65, local copies, waits for them, and re-layouts: 21.1 us -> 17.4 us
  transfers between devices with their start and end apart: 39 -> 39, of which waited for: 18 -> 21; matrix products, arithmetic and copies ran while one was open for 3% -> 1% of each run, Pallas kernels for 22% -> 26%
where the time goes in v3:
time: 422 us; the launch traced here: 420 us
  Pallas kernels  180 us (43%)
  waiting for transfers between devices  136 us (32%)
  starting transfers between devices  47.1 us (11%)
  local copies, waits for them, and re-layouts  23.5 us (6%)
  blocking collectives  15.4 us (4%)
  between operations  14.6 us (3%)
    pallas_call x14, Pallas kernels, call(): pl.pallas_call(with_token, grid=grid, in_specs=[held_spec(a.shape) if kin...  161 us
    ppermute x27, waiting for transfers between devices, swap(): return lax.ppermute(value, axis, flip_pairs(lax.axis_size(axis), 1 << bit))  116 us
    ppermute x27, starting transfers between devices, swap(): return lax.ppermute(value, axis, flip_pairs(lax.axis_size(axis), 1 << bit))  26.4 us
    unnamed x65, local copies, waits for them, and re-layouts  17.4 us
    ppermute x6, waiting for transfers between devices, entering(): other = lax.ppermute(value, 'seq', flip_pairs(count, 1 << bit))  16.5 us
    all_to_all x1, blocking collectives, sum_over_all(): return jnp.sum(lax.all_to_all(copies, ('rec', 'seq'), 0, 0), axis=0)  15.4 us
    pallas_call x12, Pallas kernels, in_vmem(): pl.pallas_call(kernel, in_specs=[scalars()] + [vmem] * len(ins) + [anywhe...  13 us
    ppermute x6, starting transfers between devices, entering(): other = lax.ppermute(value, 'seq', flip_pairs(count, 1 << bit))  12 us
  transfers between devices with their start and end apart: 39, of which 21 were waited for; matrix products, arithmetic and copies ran while one was open for 1% of the time, Pallas kernels for 26%

profile of v3, /device:TPU:0, one launch (start us, length us, event | category | flops | bytes accessed | tf_op | source)
XLA Modules:
  0.0 420.1 jit_solution(2690672287329817588)
XLA Ops:
  14.3 20.4 %front.1 = (bf16[4,256,512]{2,1,0:T(8,128)(2,1)}, f32[4,256,512]{2,1,0:T(8,128)}, bf16[4,256,512]{2,1,0:T(8,128)(2,1)}, f32[4,256,1]{2,1,0:T(8,128)}, bf16[4,256...) custom-call(bf16[4,1024,80]{2,1,0:T(8,128)(2,1)} %copy.61.refs_0_, ...), custom_call_target="tpu_custom_call" | custom-call | flops 69000003584 | tf_op jit(solution)/shard_map/front/pallas_call | solution.py:625
  41.6 7.0 %collective-permute-done.1.other = f32[4,136,128]{2,1,0:T(8,128)S(1)} collective-permute-done((f32[4,136,128]{2,1,0:T(8,128)S(1)}, f32[4,136,128]{2,1,0:T(8,128)S(1)}, u32[]{:S(2)}, u32[]{:S(2)}) %collective-permute-start.1) | collective-permute-done | bytes 278560 | tf_op jit(solution)/shard_map/ppermute | solution.py:687
  51.4 7.3 %mix.1 = (f32[4,256,512]{2,1,0:T(8,128)}, bf16[4,8,256,256]{3,2,1,0:T(8,128)(2,1)}, bf16[4,8,256,256]{3,2,1,0:T(8,128)(2,1)}, f32[8,128]{1,0:T(8,128)}) custom-call(bf16[4,256,512]{2,1,0:T(8,128)(2,1)} %get-tuple-element.176.refs_0_.refs_1_, bf16[4,256,256]{2,1,0:T(8,128)(2,1)} %get-tuple-element.177.refs_1_, ...), custom_call_target="tpu_custom_call" | custom-call | flops 24149999616 | tf_op jit(solution)/shard_map/mix/pallas_call | solution.py:625
  60.8 9.1 %lift.1 = (bf16[4,256,512]{2,1,0:T(8,128)(2,1)}, bf16[4,256,512]{2,1,0:T(8,128)(2,1)}, bf16[4,256,512]{2,1,0:T(8,128)(2,1)}, f32[4,256,512]{2,1,0:T(8,128)}, bf1...) custom-call(f32[4,256,512]{2,1,0:T(8,128)} %get-tuple-element.181.re, ...), custom_call_target="tpu_custom_call" | custom-call | flops 31050000384 | tf_op jit(solution)/shard_map/lift/pallas_call | solution.py:625
  83.2 15.4 %all_to_all.10 = f32[32,2,512]{2,1,0:T(2,128)S(1)} all-to-all(f32[32,2,512]{2,1,0:T(2,128)S(1)} %broadcast_in_dim.9), channel_id=1, replica_groups=mesh['seq'=8,'rec'=4] {'rec','seq'}, dimensions={0} | all-to-all | bytes 262144 | tf_op jit(solution)/shard_map/all_to_all | solution.py:715
  99.3 23.9 %late.1 = (bf16[4,256,512]{2,1,0:T(8,128)(2,1)}, bf16[4,256,512]{2,1,0:T(8,128)(2,1)}, bf16[4,256,512]{2,1,0:T(8,128)(2,1)}, bf16[4,256,2048]{2,1,0:T(8,128)(2,1...) custom-call(f32[4,256,512]{2,1,0:T(8,128)} %get-tuple-element.194.re, ...), custom_call_target="tpu_custom_call" | custom-call | flops 79349997568 | tf_op jit(solution)/shard_map/late/pallas_call | solution.py:625
  127.3 11.4 %late_weights.1 = (f32[512,4608]{1,0:T(8,128)}, f32[8,128]{1,0:T(8,128)}) custom-call(bf16[1024,512]{1,0:T(8,128)(2,1)} %bitcast.85, bf16[1024,512]{1,0:T(8,128)(2,1)} %bitcast.84, bf16[1024,2048]{1,0:T(8,128)(2,1)} %bitcast.72, bf16[1024,2048]{1,0:T(8,128)(2,1)} %bitcast.73, bf16[1024,512]{1,0:T(8,128)(2,1)} %bitcast.87, bf16[1024,512]{1,0:T(8,128)(2,1)} %bitcast.86), custom_call_target="tpu_custom_call" | custom-call | flops 37950001152 | tf_op jit(solution)/shard_map/late_weights/pallas_call | solution.py:625
  143.8 7.2 %depth_grad.1 = (f32[4,256,512]{2,1,0:T(8,128)}, f32[16,512]{1,0:T(8,128)}, f32[8,128]{1,0:T(8,128)}) custom-call(f32[4,256,512]{2,1,0:T(8,128)} %get-tuple-element.198.refs_0_, f32[4,256,512]{2,1,0:T(8,128)} %get-tuple-element.194.refs_0_.refs_1_, f32[2,512]{1,0:T(2,128)} %reduce_sum.18.refs_3_.refs_2_, f32[2,512]{1,0:T(2,128)} %copy-done.20, ...), custom_call_target="tpu_custom_call" | custom-call | flops 24149999616 | tf_op jit(solution)/shard_map/depth_grad/pallas_call | solution.py:625
  151.6 12.4 %conv_back.1 = (bf16[4,256,1024]{2,1,0:T(8,128)(2,1)}, f32[4,256,512]{2,1,0:T(8,128)}, bf16[4,256,512]{2,1,0:T(8,128)(2,1)}, bf16[4,256,512]{2,1,0:T(8,128)(2,1)...) custom-call(f32[4,256,512]{2,1,0:T(8,128)} %get-tuple-element.207.refs_0_, ...), custom_call_target="tpu_custom_call" | custom-call | flops 37950001152 | tf_op jit(solution)/shard_map/conv_back/pallas_call | solution.py:625
  171.1 6.5 %weights.3 = (f32[256,1536]{1,0:T(8,128)}, f32[256,1536]{1,0:T(8,128)}, f32[8,128]{1,0:T(8,128)}) custom-call(s32[1]{0:T(128)} %bitcast.24.refs_0_, bf16[1024,512]{1,0:T(8,128)(2,1)} %bitcast.80, bf16[1024,512]{1,0:T(8,128)(2,1)} %bitcast.79, bf16[1024,1024]{1,0:T(8,128)(2,1)} %bitcast.75, bf16[1024,512]{1,0:T(8,128)(2,1)} %bitcast.82, ...), custom_call_target="tpu_custom_call" | custom-call | flops 34500001792 | tf_op jit(solution)/shard_map/weights/pallas_call | solution.py:625
  177.6 6.8 %collective-permute-done.8.other = f32[4,136,128]{2,1,0:T(8,128)S(1)} collective-permute-done((f32[4,136,128]{2,1,0:T(8,128)S(1)}, f32[4,136,128]{2,1,0:T(8,128)S(1)}, u32[]{:S(2)}, u32[]{:S(2)}) %collective-permute-start.8) | collective-permute-done | bytes 278560 | tf_op jit(solution)/shard_map/ppermute | solution.py:687
  188.6 11.8 %mix_back.1 = (f32[4,256,512]{2,1,0:T(8,128)}, f32[4,256,256]{2,1,0:T(8,128)}, bf16[4,256,256]{2,1,0:T(8,128)(2,1)}, f32[8,128]{1,0:T(8,128)}) custom-call(bf16[4,256,512]{2,1,0:T(8,128)(2,1)} %get-tuple-element.176.refs_0_.refs_1_, bf16[4,256,256]{2,1,0:T(8,128)(2,1)} %get-tuple-element.177.refs_1_, bf16[4,256,256]{2,1,0:T(8,128)(2,1)} %get-tuple-element.178.refs_2_, ...), custom_call_target="tpu_custom_call" | custom-call | flops 41400000512 | tf_op jit(solution)/shard_map/mix_back/pallas_call | solution.py:625
  204.6 10.4 %mix_end.1 = (bf16[4,256,1536]{2,1,0:T(8,128)(2,1)}, f32[4,256,512]{2,1,0:T(8,128)}, bf16[4,256,512]{2,1,0:T(8,128)(2,1)}, f32[1,512]{1,0:T(1,128)}, f32[8,128]{1,0:T(8,128)}) custom-call(f32[4,136,128]{2,1,0:T(8,128)} %copy-done.11, bf16[4,256,512]{2,1,0:T(8,128)(2,1)} %get-tuple-element.176.refs_0_.refs_1_, ...), custom_call_target="tpu_custom_call" | custom-call | flops 34500001792 | tf_op jit(solution)/shard_map/mix_end/pallas_call | solution.py:625
  215.0 12.8 %collective-permute-done.12.refs_2_ = f32[128,1024]{1,0:T(8,128)S(1)} collective-permute-done((f32[128,1024]{1,0:T(8,128)S(1)}, f32[128,1024]{1,0:T(8,128)S(1)}, u32[]{:S(2)}, u32[]{:S(2)}) %collective-permute-start.12) | collective-permute-done | bytes 524320 | tf_op jit(solution)/shard_map/ppermute | solution.py:836
  230.9 12.2 %weights.4 = (f32[256,3584]{1,0:T(8,128)}, f32[256,3584]{1,0:T(8,128)}, f32[8,128]{1,0:T(8,128)}) custom-call(s32[1]{0:T(128)} %bitcast.24.refs_0_, bf16[1024,512]{1,0:T(8,128)(2,1)} %bitcast.78, bf16[1024,2048]{1,0:T(8,128)(2,1)} %bitcast.70, bf16[1024,1536]{1,0:T(8,128)(2,1)} %bitcast.74, bf16[1024,512]{1,0:T(8,128)(2,1)} %bitcast.81, ...), custom_call_target="tpu_custom_call" | custom-call | flops 34500001792 | tf_op jit(solution)/shard_map/weights/pallas_call | solution.py:625
  247.3 14.0 %front_back.1 = (bf16[4,256,2048]{2,1,0:T(8,128)(2,1)}, bf16[4,256,512]{2,1,0:T(8,128)(2,1)}, f32[4,1024,80]{2,1,0:T(8,128)}, f32[1,512]{1,0:T(1,128)}, f32[8,128]{1,0:T(8,128)}) custom-call(f32[4,256,512]{2,1,0:T(8,128)} %get-tuple-element.245.refs_0_, bf16[4,256,512]{2,1,0:T(8,128)(2,1)} %get-tuple-element.246.refs_1_, bf16[2048,512]{1,0:T(8,128)(2,1)} %refs_2_.3, ...), custom_call_target="tpu_custom_call" | custom-call | flops 48299999232 | tf_op jit(solution)/shard_map/front_back/pallas_call | solution.py:625
  273.9 9.1 %weights.5 = (f32[256,2560]{1,0:T(8,128)}, f32[256,2560]{1,0:T(8,128)}, f32[8,128]{1,0:T(8,128)}) custom-call(s32[1]{0:T(128)} %bitcast.24.refs_0_, bf16[1024,512]{1,0:T(8,128)(2,1)} %bitcast.77, bf16[1024,512]{1,0:T(8,128)(2,1)} %bitcast.83, bf16[1024,2048]{1,0:T(8,128)(2,1)} %bitcast.71, bf16[1024,512]{1,0:T(8,128)(2,1)} %bitcast.76, ...), custom_call_target="tpu_custom_call" | custom-call | flops 34500001792 | tf_op jit(solution)/shard_map/weights/pallas_call | solution.py:625
  283.0 6.0 %collective-permute-done.17.refs_1_ = f32[16,6144]{1,0:T(8,128)S(1)} collective-permute-done((f32[16,6144]{1,0:T(8,128)S(1)}, f32[16,6144]{1,0:T(8,128)S(1)}, u32[]{:S(2)}, u32[]{:S(2)}) %collective-permute-start.17) | collective-permute-done | bytes 393248 | tf_op jit(solution)/shard_map/ppermute | solution.py:836
  290.3 6.7 %collective-permute-done.19.refs_4_ = f32[128,2048]{1,0:T(8,128)S(1)} collective-permute-done((f32[128,2048]{1,0:T(8,128)S(1)}, f32[128,2048]{1,0:T(8,128)S(1)}, u32[]{:S(2)}, u32[]{:S(2)}) %collective-permute-start.19) | collective-permute-done | bytes 1048608 | tf_op jit(solution)/shard_map/ppermute | solution.py:836
  305.1 16.1 %collective-permute-done.20.refs_1_ = f32[16,6144]{1,0:T(8,128)S(1)} collective-permute-done((f32[16,6144]{1,0:T(8,128)S(1)}, f32[16,6144]{1,0:T(8,128)S(1)}, u32[]{:S(2)}, u32[]{:S(2)}) %collective-permute-start.20) | collective-permute-done | bytes 393248 | tf_op jit(solution)/shard_map/ppermute | solution.py:836
  337.1 6.1 %collective-permute-done.27.refs_0_ = f32[32,3584]{1,0:T(8,128)S(1)} collective-permute-done((f32[32,3584]{1,0:T(8,128)S(1)}, f32[32,3584]{1,0:T(8,128)S(1)}, u32[]{:S(2)}, u32[]{:S(2)}) %collective-permute-start.27) | collective-permute-done | bytes 458784 | tf_op jit(solution)/shard_map/ppermute | solution.py:836
  345.9 19.0 %collective-permute-done.30.refs_3_ = f32[16,3584]{1,0:T(8,128)S(1)} collective-permute-done((f32[16,3584]{1,0:T(8,128)S(1)}, f32[16,3584]{1,0:T(8,128)S(1)}, u32[]{:S(2)}, u32[]{:S(2)}) %collective-permute-start.30) | collective-permute-done | bytes 229408 | tf_op jit(solution)/shard_map/ppermute | solution.py:836
  370.5 13.6 %collective-permute-done.33.refs_3_ = f32[16,2560]{1,0:T(8,128)S(1)} collective-permute-done((f32[16,2560]{1,0:T(8,128)S(1)}, f32[16,2560]{1,0:T(8,128)S(1)}, u32[]{:S(2)}, u32[]{:S(2)}) %collective-permute-start.33) | collective-permute-done | bytes 163872 | tf_op jit(solution)/shard_map/ppermute | solution.py:836
  387.2 10.9 %collective-permute-done.35.refs_3_ = f32[16,2560]{1,0:T(8,128)S(1)} collective-permute-done((f32[16,2560]{1,0:T(8,128)S(1)}, f32[16,2560]{1,0:T(8,128)S(1)}, u32[]{:S(2)}, u32[]{:S(2)}) %collective-permute-start.35) | collective-permute-done | bytes 163872 | tf_op jit(solution)/shard_map/ppermute | solution.py:836
  (169 shorter events, 129.7 us)
Async XLA Ops:
  124.5 14.9 %all-to-all-start.1 = ((f32[32,2,512]{2,1,0:T(2,128)}), f32[32,2,512]{2,1,0:T(2,128)S(1)}, u32[]{:S(2)}, u32[]{:S(2)}) async-start(f32[32,2,512]{2,1,0:T(2,128)} %broadcast_in_dim.10), calls=%async_computation.1 | async-start | bytes 262144 | tf_op jit(solution)/shard_map/all_to_all | solution.py:715
  127.0 116.1 %reduce-scatter.2.cloned.1.call-start = ((), (), s32[]{:S(2)}) async-start(), calls=%async_computation.3 | async-start | bytes 10616832 | tf_op jit(solution)/shard_map/reduce_scatter | solution.py:719
  169.1 15.3 %collective-permute-start.8 = (f32[4,136,128]{2,1,0:T(8,128)S(1)}, f32[4,136,128]{2,1,0:T(8,128)S(1)}, u32[]{:S(2)}, u32[]{:S(2)}) collective-permute-start(f32[4,136,128]{2,1,0:T(8,128)S(1)} %get-tuple-element.216.value), channel_id=1, source_target_pairs={{0,8},{4,12},{8,0},{12,4},{16,24},{20,28},{24,16},{28,20},{1,9},{5... | collective-permute-start | bytes 835592 | tf_op jit(solution)/shard_map/ppermute | solution.py:687
  177.6 24.2 %collective-permute-start.10 = (f32[256,1536]{1,0:T(8,128)}, f32[256,1536]{1,0:T(8,128)S(1)}, u32[]{:S(2)}, u32[]{:S(2)}) collective-permute-start(f32[256,1536]{1,0:T(8,128)} %get-tuple-element.241), channel_id=1, source_target_pairs={{0,4},{4,0},{8,12},{12,8},{16,20},{20,16},{24,28},{28,24},{1,5},{5... | collective-permute-start | bytes 4718600 | tf_op jit(solution)/shard_map/ppermute | solution.py:836
  185.1 15.4 %collective-permute-start.9 = (f32[4,136,128]{2,1,0:T(8,128)S(1)}, f32[4,136,128]{2,1,0:T(8,128)S(1)}, u32[]{:S(2)}, u32[]{:S(2)}) collective-permute-start(f32[4,136,128]{2,1,0:T(8,128)S(1)} %get-tuple-element.218.value), channel_id=1, source_target_pairs={{0,16},{4,20},{8,24},{12,28},{16,0},{20,4},{24,8},{28,12},{1,17},{... | collective-permute-start | bytes 835592 | tf_op jit(solution)/shard_map/ppermute | solution.py:687
  203.8 24.0 %collective-permute-start.12 = (f32[128,1024]{1,0:T(8,128)S(1)}, f32[128,1024]{1,0:T(8,128)S(1)}, u32[]{:S(2)}, u32[]{:S(2)}) collective-permute-start(f32[128,1024]{1,0:T(8,128)S(1)} %get-tuple-element.253), channel_id=1, source_target_pairs={{0,16},{4,20},{8,24},{12,28},{16,0},{20,4},{24,8},{28,12},{1,17},{... | collective-permute-start | bytes 1572872 | tf_op jit(solution)/shard_map/ppermute | solution.py:836
  243.1 18.2 %collective-permute-start.16 = (f32[256,3584]{1,0:T(8,128)}, f32[256,3584]{1,0:T(8,128)}, u32[]{:S(2)}, u32[]{:S(2)}) collective-permute-start(f32[256,3584]{1,0:T(8,128)} %get-tuple-element.268), channel_id=1, source_target_pairs={{0,4},{4,0},{8,12},{12,8},{16,20},{20,16},{24,28},{28,24},{1,5},{5... | collective-permute-start | bytes 11010056 | tf_op jit(solution)/shard_map/ppermute | solution.py:836
  245.8 20.0 %collective-permute-start.15 = (f32[32,6144]{1,0:T(8,128)S(1)}, f32[32,6144]{1,0:T(8,128)S(1)}, u32[]{:S(2)}, u32[]{:S(2)}) collective-permute-start(f32[32,6144]{1,0:T(8,128)S(1)} %get-tuple-element.266), channel_id=1, source_target_pairs={{0,1},{1,0},{2,3},{3,2},{4,5},{5,4},{6,7},{7,6},{8,9},{9,8},{10,11... | collective-permute-start | bytes 2359304 | tf_op jit(solution)/shard_map/ppermute | solution.py:836
  268.9 20.1 %collective-permute-start.17 = (f32[16,6144]{1,0:T(8,128)S(1)}, f32[16,6144]{1,0:T(8,128)S(1)}, u32[]{:S(2)}, u32[]{:S(2)}) collective-permute-start(f32[16,6144]{1,0:T(8,128)S(1)} %get-tuple-element.272), channel_id=1, source_target_pairs={{0,2},{1,3},{2,0},{3,1},{4,6},{5,7},{6,4},{7,5},{8,10},{9,11},{10,... | collective-permute-start | bytes 1179656 | tf_op jit(solution)/shard_map/ppermute | solution.py:836
  271.5 18.8 %collective-permute-start.18 = (f32[128,1536]{1,0:T(8,128)S(1)}, f32[128,1536]{1,0:T(8,128)S(1)}, u32[]{:S(2)}, u32[]{:S(2)}) collective-permute-start(f32[128,1536]{1,0:T(8,128)S(1)} %get-tuple-element.273), channel_id=1, source_target_pairs={{0,8},{4,12},{8,0},{12,4},{16,24},{20,28},{24,16},{28,20},{1,9},{5... | collective-permute-start | bytes 2359304 | tf_op jit(solution)/shard_map/ppermute | solution.py:836
  272.8 24.2 %collective-permute-start.19 = (f32[128,2048]{1,0:T(8,128)S(1)}, f32[128,2048]{1,0:T(8,128)S(1)}, u32[]{:S(2)}, u32[]{:S(2)}) collective-permute-start(f32[128,2048]{1,0:T(8,128)S(1)} %get-tuple-element.275), channel_id=1, source_target_pairs={{0,16},{4,20},{8,24},{12,28},{16,0},{20,4},{24,8},{28,12},{1,17},{... | collective-permute-start | bytes 3145736 | tf_op jit(solution)/shard_map/ppermute | solution.py:836
  283.0 15.4 %collective-permute-start.23 = (f32[256,2560]{1,0:T(8,128)}, f32[256,2560]{1,0:T(8,128)S(1)}, u32[]{:S(2)}, u32[]{:S(2)}) collective-permute-start(f32[256,2560]{1,0:T(8,128)} %get-tuple-element.293), channel_id=1, source_target_pairs={{0,4},{4,0},{8,12},{12,8},{16,20},{20,16},{24,28},{28,24},{1,5},{5... | collective-permute-start | bytes 7864328 | tf_op jit(solution)/shard_map/ppermute | solution.py:836
  300.2 26.1 %collective-permute-start.25 = (f32[128,1536]{1,0:T(8,128)S(1)}, f32[128,1536]{1,0:T(8,128)S(1)}, u32[]{:S(2)}, u32[]{:S(2)}) collective-permute-start(f32[128,1536]{1,0:T(8,128)S(1)} %get-tuple-element.298), channel_id=1, source_target_pairs={{0,16},{4,20},{8,24},{12,28},{16,0},{20,4},{24,8},{28,12},{1,17},{... | collective-permute-start | bytes 2359304 | tf_op jit(solution)/shard_map/ppermute | solution.py:836
  301.4 24.9 %collective-permute-start.22 = (f32[64,2048]{1,0:T(8,128)S(1)}, f32[64,2048]{1,0:T(8,128)S(1)}, u32[]{:S(2)}, u32[]{:S(2)}) collective-permute-start(f32[64,2048]{1,0:T(8,128)S(1)} %get-tuple-element.291), channel_id=1, source_target_pairs={{0,8},{4,12},{8,0},{12,4},{16,24},{20,28},{24,16},{28,20},{1,9},{5... | collective-permute-start | bytes 1572872 | tf_op jit(solution)/shard_map/ppermute | solution.py:836
  302.7 23.6 %collective-permute-start.24 = (f32[128,1024]{1,0:T(8,128)S(1)}, f32[128,1024]{1,0:T(8,128)S(1)}, u32[]{:S(2)}, u32[]{:S(2)}) collective-permute-start(f32[128,1024]{1,0:T(8,128)S(1)} %get-tuple-element.296), channel_id=1, source_target_pairs={{0,8},{4,12},{8,0},{12,4},{16,24},{20,28},{24,16},{28,20},{1,9},{5... | collective-permute-start | bytes 1572872 | tf_op jit(solution)/shard_map/ppermute | solution.py:836
  303.5 17.7 %collective-permute-start.20 = (f32[16,6144]{1,0:T(8,128)S(1)}, f32[16,6144]{1,0:T(8,128)S(1)}, u32[]{:S(2)}, u32[]{:S(2)}) collective-permute-start(f32[16,6144]{1,0:T(8,128)S(1)} %get-tuple-element.288.refs_0_), channel_id=1, source_target_pairs={{0,2},{1,3},{2,0},{3,1},{4,6},{5,7},{6,4},{7,5},{8,10},{9,11},{10,... | collective-permute-start | bytes 1179656 | tf_op jit(solution)/shard_map/ppermute | solution.py:836
  303.8 22.5 %collective-permute-start.21 = (f32[64,1536]{1,0:T(8,128)S(1)}, f32[64,1536]{1,0:T(8,128)S(1)}, u32[]{:S(2)}, u32[]{:S(2)}) collective-permute-start(f32[64,1536]{1,0:T(8,128)S(1)} %get-tuple-element.289), channel_id=1, source_target_pairs={{0,16},{4,20},{8,24},{12,28},{16,0},{20,4},{24,8},{28,12},{1,17},{... | collective-permute-start | bytes 1179656 | tf_op jit(solution)/shard_map/ppermute | solution.py:836
  327.2 16.0 %collective-permute-start.27 = (f32[32,3584]{1,0:T(8,128)S(1)}, f32[32,3584]{1,0:T(8,128)S(1)}, u32[]{:S(2)}, u32[]{:S(2)}) collective-permute-start(f32[32,3584]{1,0:T(8,128)S(1)} %get-tuple-element.302), channel_id=1, source_target_pairs={{0,1},{1,0},{2,3},{3,2},{4,5},{5,4},{6,7},{7,6},{8,9},{9,8},{10,11... | collective-permute-start | bytes 1376264 | tf_op jit(solution)/shard_map/ppermute | solution.py:836
  328.9 36.9 %collective-permute-start.26 = (f32[32,6144]{1,0:T(8,128)S(1)}, f32[32,6144]{1,0:T(8,128)S(1)}, u32[]{:S(2)}, u32[]{:S(2)}) collective-permute-start(f32[32,6144]{1,0:T(8,128)S(1)} %get-tuple-element.301.refs_0_), channel_id=1, source_target_pairs={{0,1},{1,0},{2,3},{3,2},{4,5},{5,4},{6,7},{7,6},{8,9},{9,8},{10,11... | collective-permute-start | bytes 2359304 | tf_op jit(solution)/shard_map/ppermute | solution.py:836
  343.9 21.9 %collective-permute-start.31 = (f32[32,2560]{1,0:T(8,128)S(1)}, f32[32,2560]{1,0:T(8,128)S(1)}, u32[]{:S(2)}, u32[]{:S(2)}) collective-permute-start(f32[32,2560]{1,0:T(8,128)S(1)} %get-tuple-element.311), channel_id=1, source_target_pairs={{0,1},{1,0},{2,3},{3,2},{4,5},{5,4},{6,7},{7,6},{8,9},{9,8},{10,11... | collective-permute-start | bytes 983048 | tf_op jit(solution)/shard_map/ppermute | solution.py:836
  344.0 20.9 %collective-permute-start.30 = (f32[16,3584]{1,0:T(8,128)S(1)}, f32[16,3584]{1,0:T(8,128)S(1)}, u32[]{:S(2)}, u32[]{:S(2)}) collective-permute-start(f32[16,3584]{1,0:T(8,128)S(1)} %get-tuple-element.310), channel_id=1, source_target_pairs={{0,2},{1,3},{2,0},{3,1},{4,6},{5,7},{6,4},{7,5},{8,10},{9,11},{10,... | collective-permute-start | bytes 688136 | tf_op jit(solution)/shard_map/ppermute | solution.py:836
  367.6 16.6 %collective-permute-start.32 = (f32[16,3584]{1,0:T(8,128)S(1)}, f32[16,3584]{1,0:T(8,128)S(1)}, u32[]{:S(2)}, u32[]{:S(2)}) collective-permute-start(f32[16,3584]{1,0:T(8,128)S(1)} %get-tuple-element.314.refs_0_), channel_id=1, source_target_pairs={{0,2},{1,3},{2,0},{3,1},{4,6},{5,7},{6,4},{7,5},{8,10},{9,11},{10,... | collective-permute-start | bytes 688136 | tf_op jit(solution)/shard_map/ppermute | solution.py:836
  370.1 14.1 %collective-permute-start.33 = (f32[16,2560]{1,0:T(8,128)S(1)}, f32[16,2560]{1,0:T(8,128)S(1)}, u32[]{:S(2)}, u32[]{:S(2)}) collective-permute-start(f32[16,2560]{1,0:T(8,128)S(1)} %get-tuple-element.316), channel_id=1, source_target_pairs={{0,2},{1,3},{2,0},{3,1},{4,6},{5,7},{6,4},{7,5},{8,10},{9,11},{10,... | collective-permute-start | bytes 491528 | tf_op jit(solution)/shard_map/ppermute | solution.py:836
  384.8 15.5 %collective-permute-start.34 = (f32[32,3584]{1,0:T(8,128)S(1)}, f32[32,3584]{1,0:T(8,128)S(1)}, u32[]{:S(2)}, u32[]{:S(2)}) collective-permute-start(f32[32,3584]{1,0:T(8,128)S(1)} %get-tuple-element.318.refs_0_), channel_id=1, source_target_pairs={{0,1},{1,0},{2,3},{3,2},{4,5},{5,4},{6,7},{7,6},{8,9},{9,8},{10,11... | collective-permute-start | bytes 1376264 | tf_op jit(solution)/shard_map/ppermute | solution.py:836
  (45 other events, 280.2 us)
Sparse Core Ops, SparseCore 0:
  138.8 93.5 reduce-scatter.1

commit v4 on v3

--- a/solution.py
+++ b/solution.py
@@ -114,19 +114,19 @@
 
 
 def front_kernel(
-    feat, tk, fk, dec, dec_t, keep, w_sub, g1, w1, w2, g2, w_in,
+    feat, tk, fk, dec, keep, w_sub, g1, w1, w2, g2, w_in,
     flat, x1, a1, r1, s1, d1, a2, r2, u, g, bs, c, ce, bt, se, ee, te, cum, cum_t, state,
     frames,
 ):
     steps = x1.shape[1]
-    frames[...] = feat[0].astype(F32)
-    parts = [
-        frames[pl.ds(j, steps, stride=SUB), :] * (tk[0][:, j : j + 1] * fk[0]) for j in range(SUB)
-    ]
+    here = pl.ds(pl.program_id(0), 1)
+    kept = feat[0].astype(F32) * tk[here, :].astype(F32)
+    frames[...] = kept.T * fk[here, :].astype(F32)
+    parts = [frames[pl.ds(j, steps, stride=SUB), :] for j in range(SUB)]
     parts.append(jnp.zeros((steps, WIDE - SUB * parts[0].shape[1]), F32))
     stacked = jnp.concatenate(parts, axis=1).astype(BF16)
     flat[0] = stacked
-    x0 = dot_t(stacked[:, : w_sub.shape[1]], w_sub[...])
+    x0 = dot(stacked[:, : w_sub.shape[0]], w_sub[...])
     low, scale = norm(x0, g1[...])
     a1[0] = low
     r1[0] = scale
@@ -149,10 +149,11 @@
     g[0] = dot(low, w_in[:, D : 2 * D]).astype(BF16)
     keys = dot(low, w_in[:, 2 * D : 2 * D + 256])
     reads = dot(low, w_in[:, 2 * D + 256 :])
-    log_decay = jnp.log(dec_t[0])
+    log_rows = jnp.log(dec[0])
+    log_decay = log_rows.T
     lower = jnp.where(iota((steps, steps), 0) >= iota((steps, steps), 1), 1.0, 0.0).astype(BF16)
     running = sum(dot(lower, part) for part in split_three(log_decay))
-    running_t = sum(dot_t(part, lower) for part in split_three(jnp.log(dec[0])))
+    running_t = sum(dot_t(part, lower) for part in split_three(log_rows))
     cum[0] = running
     cum_t[0] = running_t
     spread = jnp.where(iota((HEADS, 256), 1) // STATE == iota((HEADS, 256), 0), 1.0, 0.0).astype(BF16)
@@ -380,7 +381,7 @@
     pulled[0, 4 * STATE :, :] = block[0, 4 * STATE :, :]
 
 
-def mix_back_kernel(u, bs, c, ee, gy, start, pairs, decay_pairs, _, __, gu, gb, gc, full):
+def mix_back_kernel(u, bs, c, ee, gy, start, pairs, decay_pairs, _, gu, gb, gc, full):
     steps = u.shape[1]
     unpack_state(start, full)
     reads_grad = dot_t(gy[0], full[...]) * ee[0].astype(F32)
@@ -425,6 +426,7 @@
 def front_back_kernel(
     gx1, gf, w2, d1, w1, a1, r1, g1, w_sub, tk, fk, _,
     gh, gxr, fg, ln1,
+    mel_rows,
 ):
     steps = gx1.shape[1]
     low = gf[0]
@@ -437,12 +439,13 @@
     accumulate(ln1, gain)
     low = (gx1[0] + back).astype(BF16)
     gxr[0] = low
-    frames = dot(low, w_sub[...])
-    mels = fk.shape[2]
+    frames = dot_t(low, w_sub[...])
+    mels = fk.shape[1]
+    here = pl.ds(pl.program_id(0), 1)
+    keep_mels = fk[here, :].astype(F32)
     for j in range(SUB):
-        fg[0, pl.ds(j, steps, stride=SUB), :] = frames[:, mels * j : mels * (j + 1)] * (
-            tk[0][:, j : j + 1] * fk[0]
-        )
+        mel_rows[pl.ds(j, steps, stride=SUB), :] = frames[:, mels * j : mels * (j + 1)] * keep_mels
+    fg[0] = mel_rows[...].T * tk[here, :].astype(F32)
 
 
 def by_share_store(out, at, share, start, block):
@@ -476,15 +479,15 @@
         place[pl.ds(at, share), :] = rows[s * share : (s + 1) * share, :]
 
 
-def turned_by_share(place, share, core, block):
-    for at in range(0, block.shape[1], 256):
+def turned_by_share(place, share, core, block, at_block):
+    for at in range(0, D, 256):
         rows = block[:, at : at + 256].T
         for piece in range(256 // share):
-            row = at + share * piece
-            s, k = row // (4 * share), row % (4 * share) // share
-            side = core if s % 2 == 0 else 1 - core
-            to = pl.multiple_of(side * (D // 2) + D * k + s // 2 * share, 16)
-            place[pl.ds(to, share), :] = rows[share * piece : share * (piece + 1), :]
+            here = at + share * piece
+            first, k = here // (4 * share), here % (4 * share) // share
+            side = core if first % 2 == 0 else 1 - core
+            to = side * (D // 2) + D * k + (at_block * (D // (8 * share)) + first // 2) * share
+            place[pl.ds(pl.multiple_of(to, 16), share), :] = rows[share * piece : share * (piece + 1), :]
 
 
 def weights_kernel(pairs, share, waits, cuts):
@@ -507,12 +510,17 @@
         for (wide, long), left, right, place in zip(pairs, lefts, rights, places[:count]):
             steps = max(wide, long)
 
-            @pl.when(step == start)
-            def _(left=left, place=place, wide=wide):
-                if wide == 1:
+            if wide == 1:
+
+                @pl.when(step == start)
+                def _(left=left, place=place):
                     turned(place, share, core, left[...])
-                else:
-                    turned_by_share(place, share, core, left)
+
+            else:
+
+                @pl.when((step > start - wide) & (step <= start))
+                def _(left=left, place=place, before=start - wide + 1):
+                    turned_by_share(place, share, core, left, step - before)
 
             @pl.when((step >= start) & (step < start + steps))
             def _(right=right, place=place, wide=wide, start=start):
@@ -551,7 +559,11 @@
     lefts, rights, start = [], [], 0
     for (left, right), (wide, long) in zip(pairs, sizes):
         steps = max(wide, long)
-        lefts.append((left, "all"))
+        if wide == 1:
+            lefts.append((left, "all"))
+        else:
+            index = lambda j, first=start - wide + 1, last=wide - 1: (0, jnp.clip(j - first, 0, last))
+            lefts.append((left, pl.BlockSpec((tokens, D), index)))
         if wide == 1 and long > 1:
             index = lambda j, start=start, last=steps - 1: (0, jnp.clip(j - start, 0, last))
             rights.append((right, pl.BlockSpec((tokens, D), index)))
@@ -601,7 +613,8 @@
 
 
 ROOM = {'front': 44, 'mix': 24, 'lift': 28, 'depth': 20, 'late': 44, 'late_weights': 36, 'depth_grad': 20, 'conv_back': 28, 'mix_back': 28, 'mix_end': 24, 'front_back': 32, 'weights': 28}
-TIMES = {'front': 60.0, 'mix': 21.0, 'lift': 27.0, 'depth': 18.0, 'late': 69.0, 'late_weights': 33.0, 'depth_grad': 21.0, 'conv_back': 33.0, 'mix_back': 36.0, 'mix_end': 30.0, 'front_back': 42.0, 'weights': 30.0}
+HOP_COST = 30e9
+TIMES = {'front': 40.0, 'mix': 14.0, 'lift': 18.0, 'depth': 12.0, 'late': 46.0, 'late_weights': 22.0, 'depth_grad': 10.0, 'conv_back': 4, 'mix_back': 24.0, 'mix_end': 20.0, 'front_back': 60, 'weights': 20.0}
 
 
 def call(kernel, grid, ins, outs, scratch=(), flops=0, name=None):
@@ -644,8 +657,9 @@
     return [(i, i ^ mask) for i in range(count)]
 
 
-def hop_kernel(backward, first, keep_state):
+def hop_kernel(backward, first, keep_state, waits):
     def kernel(keep, second_ref, value, other, *refs):
+        refs = refs[waits:]
         before, (out, out_before, token) = (None, refs) if first else (refs[0], refs[1:])
         token[...] = jnp.zeros((8, 128), F32)
         second = (second_ref[0] != 0) != backward
@@ -678,7 +692,7 @@
     return kernel
 
 
-def entering(value, backward, keep):
+def entering(value, backward, keep, meanwhile=lambda tokens: []):
     count, place = lax.axis_size("seq"), lax.axis_index("seq")
     vmem = pl.BlockSpec(memory_space=pltpu.VMEM)
     shape = jax.ShapeDtypeStruct(value.shape, F32)
@@ -686,18 +700,21 @@
     for bit in range(count.bit_length() - 1):
         other = lax.ppermute(value, "seq", flip_pairs(count, 1 << bit))
         last = (2 << bit) == count
+        after = meanwhile(tokens) if last else []
         value, entered, token = pl.pallas_call(
-            hop_kernel(backward, bit == 0, last and not backward),
-            in_specs=[scalars(), scalars()] + [vmem] * (2 + len(before)),
+            hop_kernel(backward, bit == 0, last and not backward, len(after)),
+            in_specs=[scalars()] * 2 + [vmem] * 2 + [anywhere()] * len(after) + [vmem] * len(before),
             out_specs=[vmem] * 3,
             out_shape=[shape, shape, jax.ShapeDtypeStruct((8, 128), F32)],
             compiler_params=pltpu.CompilerParams(vmem_limit_bytes=8 * 2**20),
-            cost_estimate=pl.CostEstimate(flops=0, bytes_accessed=0, transcendentals=0),
+            cost_estimate=pl.CostEstimate(
+                flops=int(HOP_COST) if backward and bit == 1 else 0, bytes_accessed=0, transcendentals=0
+            ),
             name="hop",
-        )(keep, ((place >> bit) & 1).reshape(1), value, other, *before)
+        )(keep, ((place >> bit) & 1).reshape(1), value, other, *after, *before)
         before = [entered]
         tokens.append(token)
-    return before[0], tokens
+    return before[0]
 
 
 def halos(top, bottom):
@@ -920,8 +937,8 @@
     keep_here = (1 - here).astype(F32)
     keep_next = jnp.where(place + 1 < blocks, 1 - after, 0).astype(F32)
     keep = (jnp.stack([keep_here, keep_next]), scalars())
-    tk = (time_keep.reshape(rows, steps, SUB).astype(F32), "row")
-    fk = (freq_keep[:, None, :].astype(F32), "row")
+    tk = (time_keep, "all")
+    fk = (freq_keep, "all")
     g1, g2, g3, g4, g5, bg, bb = (
         (gain.reshape(1, D), "all")
         for gain in (ln1_gain, ln2_gain, ln3_gain, ln4_gain, ln5_gain, bn_gain, bn_shift)
@@ -949,8 +966,8 @@
         front_kernel,
         (rows,),
         [
-            row(features), tk, fk, row(decays), row(decays.transpose(0, 2, 1)), keep,
-            every(w_sub), g1, every(ffn1_in), every(ffn1_out), g2, every(ssm_in),
+            row(features.transpose(0, 2, 1)), tk, fk, row(decays), keep,
+            every(w_sub.T), g1, every(ffn1_in), every(ffn1_out), g2, every(ssm_in),
         ],
         [
             rows_of(WIDE, BF16), rows_of(D), rows_of(D, BF16), rows_of(1), rows_of(FF, BF16),
@@ -963,7 +980,7 @@
         2 * tokens * D * (WIDE + 2 * FF + PROJ),
         "front",
     )
-    start, _ = entering(state, False, keep[0])
+    start = entering(state, False, keep[0])
     pair_shape = ((rows, HEADS, steps, steps), BF16, "row")
     mixed, pairs, decay_pairs, _ = call(
         mix_kernel,
@@ -1072,11 +1089,7 @@
         2 * tokens * D * 4 * D,
         "conv_back",
     )
-    end, hops = entering(pulled, True, keep[0])
     core = (place % 2).reshape(1)
-    kept, sent, weights_token = weight_sums(
-        [(flatten(a3), flatten(gq)), (flatten(z), flatten(gz))], share, core, None, hops[:-2]
-    )
     bits = jnp.stack(
         [(place >> k) & 1 for k in range(blocks.bit_length() - 1)]
         + [(lax.axis_index("rec") >> k) & 1 for k in range(lax.axis_size("rec").bit_length() - 1)]
@@ -1087,19 +1100,31 @@
             (2 * FF + 3 * D, D, False),
         ],
     )
-    early.begin(kept, sent, D)
-    gu, gb, gc, mixed_token = call(
-        mix_back_kernel,
-        (rows,),
-        [
-            row(u), row(bs), row(c), row(ee), row(gy), row(start), row(pairs), row(decay_pairs),
-            (weights_token, anywhere()), (hops[-2], anywhere()),
-        ],
-        [rows_of(D), rows_of(256), rows_of(256, BF16)],
-        [full],
-        2 * tokens * 256 * 256 * 32,
-        "mix_back",
-    )
+    found = {}
+
+    def beside(hops):
+        kept, sent, weights_token = weight_sums(
+            [(flatten(a3), flatten(gq)), (flatten(z), flatten(gz))], share, core, None, hops[-2:-1]
+        )
+        early.begin(kept, sent, D)
+        token = together(bits, [early], [weights_token, hops[-1]])
+        gu, gb, gc, mixed_token = call(
+            mix_back_kernel,
+            (rows,),
+            [
+                row(u), row(bs), row(c), row(ee), row(gy), row(start), row(pairs), row(decay_pairs),
+                (token, anywhere()),
+            ],
+            [rows_of(D), rows_of(256), rows_of(256, BF16)],
+            [full],
+            2 * tokens * 256 * 256 * 32,
+            "mix_back",
+        )
+        found["mixed"] = (gu, gb, gc, mixed_token)
+        return [mixed_token]
+
+    end = entering(pulled, True, keep[0], beside)
+    gu, gb, gc, mixed_token = found["mixed"]
     token = together(bits, [early], [mixed_token])
     gp, gx1, gf1, ln2, end_token = call(
         mix_end_kernel,
@@ -1113,9 +1138,8 @@
         2 * tokens * D * PROJ,
         "mix_end",
     )
-    token = together(bits, [early], [end_token])
     kept, sent, weights_token = weight_sums(
-        [(flatten(a2), flatten(gp)), (flatten(s1), flatten(gf1))], share, core, None, [token]
+        [(flatten(a2), flatten(gp)), (flatten(s1), flatten(gf1))], share, core, None, [end_token]
     )
     middle = Sum([(0, PROJ, False), (PROJ, FF, True)])
     middle.begin(kept, sent, PROJ)
@@ -1129,10 +1153,10 @@
         (rows,),
         [
             row(gx1), row(gf1), every(ffn1_out), row(d1), every(ffn1_in), row(a1), row(r1), g1,
-            every(w_sub), tk, fk, (token, anywhere()),
+            every(w_sub.T), tk, fk, (token, anywhere()),
         ],
-        [rows_of(FF, BF16), rows_of(D, BF16), ((rows, frame_count, mels), F32, "row"), line],
-        (),
+        [rows_of(FF, BF16), rows_of(D, BF16), ((rows, mels, frame_count), F32, "row"), line],
+        [pltpu.VMEM((frame_count, mels), F32)],
         2 * tokens * D * (WIDE + 2 * FF),
         "front_back",
     )
@@ -1158,7 +1182,7 @@
     start_row = place * share
     return (
         out,
-        features_grad,
+        features_grad.transpose(0, 2, 1),
         w_sub_grad,
         gains[:, 16],
         ffn1_in_grad,

time: 422 us -> 406 us (0.962)
  local copies, waits for them, and re-layouts: 23.5 us -> 15.7 us
  waiting for transfers between devices: 136 us -> 130 us
    unnamed x65 -> x51, local copies, waits for them, and re-layouts: 17.4 us -> 10.9 us
    ppermute x27, waiting for transfers between devices: 116 us -> 111 us  [swap(): return lax.ppermute(value, axis, flip_pairs(lax.axis_size(axis), 1 << bit))]
  transfers between devices with their start and end apart: 39 -> 39, of which waited for: 21 -> 20; matrix products, arithmetic and copies ran while one was open for 1% -> 1% of each run, Pallas kernels for 26% -> 26%
where the time goes in v4:
time: 406 us; the launch traced here: 404 us
  Pallas kernels  179 us (44%)
  waiting for transfers between devices  130 us (32%)
  starting transfers between devices  47.1 us (12%)
  local copies, waits for them, and re-layouts  15.7 us (4%)
  blocking collectives  15.4 us (4%)
  between operations  14.5 us (4%)
    pallas_call x14, Pallas kernels, call(): pl.pallas_call(with_token, grid=grid, in_specs=[held_spec(a.shape) if kin...  160 us
    ppermute x27, waiting for transfers between devices, swap(): return lax.ppermute(value, axis, flip_pairs(lax.axis_size(axis), 1 << bit))  111 us
    ppermute x27, starting transfers between devices, swap(): return lax.ppermute(value, axis, flip_pairs(lax.axis_size(axis), 1 << bit))  26.7 us
    ppermute x6, waiting for transfers between devices, entering(): other = lax.ppermute(value, 'seq', flip_pairs(count, 1 << bit))  16.4 us
    all_to_all x1, blocking collectives, sum_over_all(): return jnp.sum(lax.all_to_all(copies, ('rec', 'seq'), 0, 0), axis=0)  15.4 us
    pallas_call x12, Pallas kernels, in_vmem(): pl.pallas_call(kernel, in_specs=[scalars()] + [vmem] * len(ins) + [anywhe...  13 us
    ppermute x6, starting transfers between devices, entering(): other = lax.ppermute(value, 'seq', flip_pairs(count, 1 << bit))  11.8 us
    unnamed x51, local copies, waits for them, and re-layouts  10.9 us
  transfers between devices with their start and end apart: 39, of which 20 were waited for; matrix products, arithmetic and copies ran while one was open for 1% of the time, Pallas kernels for 26%

profile of v4, /device:TPU:0, one launch (start us, length us, event | category | flops | bytes accessed | tf_op | source)
XLA Modules:
  0.0 404.4 jit_solution(2321910832401142854)
XLA Ops:
  8.2 20.5 %front.1 = (bf16[4,256,512]{2,1,0:T(8,128)(2,1)}, f32[4,256,512]{2,1,0:T(8,128)}, bf16[4,256,512]{2,1,0:T(8,128)(2,1)}, f32[4,256,1]{2,1,0:T(8,128)}, bf16[4,256...) custom-call(bf16[4,80,1024]{2,1,0:T(8,128)(2,1)} %bitcast.59, ...), custom_call_target="tpu_custom_call" | custom-call | flops 46000001024 | tf_op jit(solution)/shard_map/front/pallas_call | solution.py:638
  35.5 7.0 %collective-permute-done.1.other = f32[4,136,128]{2,1,0:T(8,128)S(1)} collective-permute-done((f32[4,136,128]{2,1,0:T(8,128)S(1)}, f32[4,136,128]{2,1,0:T(8,128)S(1)}, u32[]{:S(2)}, u32[]{:S(2)}) %collective-permute-start.1) | collective-permute-done | bytes 278560 | tf_op jit(solution)/shard_map/ppermute | solution.py:701
  45.4 7.3 %mix.1 = (f32[4,256,512]{2,1,0:T(8,128)}, bf16[4,8,256,256]{3,2,1,0:T(8,128)(2,1)}, bf16[4,8,256,256]{3,2,1,0:T(8,128)(2,1)}, f32[8,128]{1,0:T(8,128)}) custom-call(bf16[4,256,512]{2,1,0:T(8,128)(2,1)} %get-tuple-element.176.refs_0_.refs_1_, bf16[4,256,256]{2,1,0:T(8,128)(2,1)} %get-tuple-element.177.refs_1_, ...), custom_call_target="tpu_custom_call" | custom-call | flops 16099999744 | tf_op jit(solution)/shard_map/mix/pallas_call | solution.py:638
  54.8 9.1 %lift.1 = (bf16[4,256,512]{2,1,0:T(8,128)(2,1)}, bf16[4,256,512]{2,1,0:T(8,128)(2,1)}, bf16[4,256,512]{2,1,0:T(8,128)(2,1)}, f32[4,256,512]{2,1,0:T(8,128)}, bf1...) custom-call(f32[4,256,512]{2,1,0:T(8,128)} %get-tuple-element.181.re, ...), custom_call_target="tpu_custom_call" | custom-call | flops 20700000256 | tf_op jit(solution)/shard_map/lift/pallas_call | solution.py:638
  77.2 15.4 %all_to_all.10 = f32[32,2,512]{2,1,0:T(2,128)S(1)} all-to-all(f32[32,2,512]{2,1,0:T(2,128)S(1)} %broadcast_in_dim.9), channel_id=1, replica_groups=mesh['seq'=8,'rec'=4] {'rec','seq'}, dimensions={0} | all-to-all | bytes 262144 | tf_op jit(solution)/shard_map/all_to_all | solution.py:732
  93.2 23.9 %late.1 = (bf16[4,256,512]{2,1,0:T(8,128)(2,1)}, bf16[4,256,512]{2,1,0:T(8,128)(2,1)}, bf16[4,256,512]{2,1,0:T(8,128)(2,1)}, bf16[4,256,2048]{2,1,0:T(8,128)(2,1...) custom-call(f32[4,256,512]{2,1,0:T(8,128)} %get-tuple-element.194.re, ...), custom_call_target="tpu_custom_call" | custom-call | flops 52899999744 | tf_op jit(solution)/shard_map/late/pallas_call | solution.py:638
  121.1 11.4 %late_weights.1 = (f32[512,4608]{1,0:T(8,128)}, f32[8,128]{1,0:T(8,128)}) custom-call(bf16[1024,512]{1,0:T(8,128)(2,1)} %bitcast.87, bf16[1024,512]{1,0:T(8,128)(2,1)} %bitcast.86, bf16[1024,2048]{1,0:T(8,128)(2,1)} %bitcast.73, bf16[1024,2048]{1,0:T(8,128)(2,1)} %bitcast.74, bf16[1024,512]{1,0:T(8,128)(2,1)} %bitcast.89, bf16[1024,512]{1,0:T(8,128)(2,1)} %bitcast.88), custom_call_target="tpu_custom_call" | custom-call | flops 25300000768 | tf_op jit(solution)/shard_map/late_weights/pallas_call | solution.py:638
  137.6 7.5 %depth_grad.1 = (f32[4,256,512]{2,1,0:T(8,128)}, f32[16,512]{1,0:T(8,128)}, f32[8,128]{1,0:T(8,128)}) custom-call(f32[4,256,512]{2,1,0:T(8,128)} %get-tuple-element.198.refs_0_, f32[4,256,512]{2,1,0:T(8,128)} %get-tuple-element.194.refs_0_.refs_1_, f32[2,512]{1,0:T(2,128)} %reduce_sum.18.refs_3_.refs_2_, f32[2,512]{1,0:T(2,128)} %copy-done.17, ...), custom_call_target="tpu_custom_call" | custom-call | flops 11500000256 | tf_op jit(solution)/shard_map/depth_grad/pallas_call | solution.py:638
  145.8 12.5 %conv_back.1 = (bf16[4,256,1024]{2,1,0:T(8,128)(2,1)}, f32[4,256,512]{2,1,0:T(8,128)}, bf16[4,256,512]{2,1,0:T(8,128)(2,1)}, bf16[4,256,512]{2,1,0:T(8,128)(2,1)...) custom-call(f32[4,256,512]{2,1,0:T(8,128)} %get-tuple-element.207.refs_0_, ...), custom_call_target="tpu_custom_call" | custom-call | flops 4600000000 | tf_op jit(solution)/shard_map/conv_back/pallas_call | solution.py:638
  165.0 6.6 %weights.3 = (f32[256,1536]{1,0:T(8,128)}, f32[256,1536]{1,0:T(8,128)}, f32[8,128]{1,0:T(8,128)}) custom-call(s32[1]{0:T(128)} %bitcast.26.refs_0_, bf16[1024,512]{1,0:T(8,128)(2,1)} %bitcast.82, bf16[1024,512]{1,0:T(8,128)(2,1)} %bitcast.81, bf16[1024,1024]{1,0:T(8,128)(2,1)} %bitcast.76, bf16[1024,512]{1,0:T(8,128)(2,1)} %bitcast.83, ...), custom_call_target="tpu_custom_call" | custom-call | flops 23000000512 | tf_op jit(solution)/shard_map/weights/pallas_call | solution.py:638
  171.6 6.7 %collective-permute-done.8.other = f32[4,136,128]{2,1,0:T(8,128)S(1)} collective-permute-done((f32[4,136,128]{2,1,0:T(8,128)S(1)}, f32[4,136,128]{2,1,0:T(8,128)S(1)}, u32[]{:S(2)}, u32[]{:S(2)}) %collective-permute-start.8) | collective-permute-done | bytes 278560 | tf_op jit(solution)/shard_map/ppermute | solution.py:701
  183.9 11.8 %mix_back.1 = (f32[4,256,512]{2,1,0:T(8,128)}, f32[4,256,256]{2,1,0:T(8,128)}, bf16[4,256,256]{2,1,0:T(8,128)(2,1)}, f32[8,128]{1,0:T(8,128)}) custom-call(bf16[4,256,512]{2,1,0:T(8,128)(2,1)} %get-tuple-element.176.refs_0_.refs_1_, bf16[4,256,256]{2,1,0:T(8,128)(2,1)} %get-tuple-element.177.refs_1_, bf16[4,256,256]{2,1,0:T(8,128)(2,1)} %get-tuple-element.178.refs_2_, ...), custom_call_target="tpu_custom_call" | custom-call | flops 27599998976 | tf_op jit(solution)/shard_map/mix_back/pallas_call | solution.py:638
  197.7 6.6 %collective-permute-done.12.refs_2_ = f32[128,1024]{1,0:T(8,128)S(1)} collective-permute-done((f32[128,1024]{1,0:T(8,128)S(1)}, f32[128,1024]{1,0:T(8,128)S(1)}, u32[]{:S(2)}, u32[]{:S(2)}) %collective-permute-start.12) | collective-permute-done | bytes 524320 | tf_op jit(solution)/shard_map/ppermute | solution.py:853
  207.1 9.6 %mix_end.1 = (bf16[4,256,1536]{2,1,0:T(8,128)(2,1)}, f32[4,256,512]{2,1,0:T(8,128)}, bf16[4,256,512]{2,1,0:T(8,128)(2,1)}, f32[1,512]{1,0:T(1,128)}, f32[8,128]{1,0:T(8,128)}) custom-call(f32[4,136,128]{2,1,0:T(8,128)} %copy-done.11, bf16[4,256,512]{2,1,0:T(8,128)(2,1)} %get-tuple-element.176.refs_0_.refs_1_, ...), custom_call_target="tpu_custom_call" | custom-call | flops 23000000512 | tf_op jit(solution)/shard_map/mix_end/pallas_call | solution.py:638
  217.4 11.3 %weights.4 = (f32[256,3584]{1,0:T(8,128)}, f32[256,3584]{1,0:T(8,128)}, f32[8,128]{1,0:T(8,128)}) custom-call(s32[1]{0:T(128)} %bitcast.26.refs_0_, bf16[1024,512]{1,0:T(8,128)(2,1)} %bitcast.80, bf16[1024,2048]{1,0:T(8,128)(2,1)} %bitcast.71, bf16[1024,1536]{1,0:T(8,128)(2,1)} %bitcast.75, bf16[1024,512]{1,0:T(8,128)(2,1)} %bitcast.84, f32[8,128]{1,0:T(8,128)S(1)} %copy-done.13), custom_call_target="tpu_custom_call" | custom-call | flops 23000000512 | tf_op jit(solution)/shard_map/weights/pallas_call | solution.py:638
  232.9 13.5 %front_back.1 = (bf16[4,256,2048]{2,1,0:T(8,128)(2,1)}, bf16[4,256,512]{2,1,0:T(8,128)(2,1)}, f32[4,80,1024]{2,1,0:T(8,128)}, f32[1,512]{1,0:T(1,128)}, f32[8,128]{1,0:T(8,128)}) custom-call(f32[4,256,512]{2,1,0:T(8,128)} %get-tuple-element.250.refs_0_, bf16[4,256,512]{2,1,0:T(8,128)(2,1)} %get-tuple-element.251.refs_1_, bf16[2048,512]{1,0:T(8,128)(2,1)} %refs_2_.5, ...), custom_call_target="tpu_custom_call" | custom-call | flops 69000003584 | tf_op jit(solution)/shard_map/front_back/pallas_call | solution.py:638
  259.1 9.1 %weights.5 = (f32[256,2560]{1,0:T(8,128)}, f32[256,2560]{1,0:T(8,128)}, f32[8,128]{1,0:T(8,128)}) custom-call(s32[1]{0:T(128)} %bitcast.26.refs_0_, bf16[1024,512]{1,0:T(8,128)(2,1)} %bitcast.79, bf16[1024,512]{1,0:T(8,128)(2,1)} %bitcast.85, bf16[1024,2048]{1,0:T(8,128)(2,1)} %bitcast.72, bf16[1024,512]{1,0:T(8,128)(2,1)} %bitcast.78, ...), custom_call_target="tpu_custom_call" | custom-call | flops 23000000512 | tf_op jit(solution)/shard_map/weights/pallas_call | solution.py:638
  268.1 6.5 %collective-permute-done.17.refs_1_ = f32[16,6144]{1,0:T(8,128)S(1)} collective-permute-done((f32[16,6144]{1,0:T(8,128)S(1)}, f32[16,6144]{1,0:T(8,128)S(1)}, u32[]{:S(2)}, u32[]{:S(2)}) %collective-permute-start.17) | collective-permute-done | bytes 393248 | tf_op jit(solution)/shard_map/ppermute | solution.py:853
  289.5 16.8 %collective-permute-done.20.refs_1_ = f32[16,6144]{1,0:T(8,128)S(1)} collective-permute-done((f32[16,6144]{1,0:T(8,128)S(1)}, f32[16,6144]{1,0:T(8,128)S(1)}, u32[]{:S(2)}, u32[]{:S(2)}) %collective-permute-start.20) | collective-permute-done | bytes 393248 | tf_op jit(solution)/shard_map/ppermute | solution.py:853
  321.9 6.1 %collective-permute-done.27.refs_0_ = f32[32,3584]{1,0:T(8,128)S(1)} collective-permute-done((f32[32,3584]{1,0:T(8,128)S(1)}, f32[32,3584]{1,0:T(8,128)S(1)}, u32[]{:S(2)}, u32[]{:S(2)}) %collective-permute-start.27) | collective-permute-done | bytes 458784 | tf_op jit(solution)/shard_map/ppermute | solution.py:853
  330.8 18.8 %collective-permute-done.30.refs_3_ = f32[16,3584]{1,0:T(8,128)S(1)} collective-permute-done((f32[16,3584]{1,0:T(8,128)S(1)}, f32[16,3584]{1,0:T(8,128)S(1)}, u32[]{:S(2)}, u32[]{:S(2)}) %collective-permute-start.30) | collective-permute-done | bytes 229408 | tf_op jit(solution)/shard_map/ppermute | solution.py:853
  355.3 13.4 %collective-permute-done.33.refs_3_ = f32[16,2560]{1,0:T(8,128)S(1)} collective-permute-done((f32[16,2560]{1,0:T(8,128)S(1)}, f32[16,2560]{1,0:T(8,128)S(1)}, u32[]{:S(2)}, u32[]{:S(2)}) %collective-permute-start.33) | collective-permute-done | bytes 163872 | tf_op jit(solution)/shard_map/ppermute | solution.py:853
  372.0 10.4 %collective-permute-done.35.refs_3_ = f32[16,2560]{1,0:T(8,128)S(1)} collective-permute-done((f32[16,2560]{1,0:T(8,128)S(1)}, f32[16,2560]{1,0:T(8,128)S(1)}, u32[]{:S(2)}, u32[]{:S(2)}) %collective-permute-start.35) | collective-permute-done | bytes 163872 | tf_op jit(solution)/shard_map/ppermute | solution.py:853
  387.6 7.2 %collective-permute-done.36.refs_1_ = f32[32,2560]{1,0:T(8,128)S(1)} collective-permute-done((f32[32,2560]{1,0:T(8,128)S(1)}, f32[32,2560]{1,0:T(8,128)S(1)}, u32[]{:S(2)}, u32[]{:S(2)}) %collective-permute-start.36) | collective-permute-done | bytes 327712 | tf_op jit(solution)/shard_map/ppermute | solution.py:853
  (152 shorter events, 121.1 us)
Async XLA Ops:
  121.0 107.7 %reduce-scatter.2.cloned.1.call-start = ((), (), s32[]{:S(2)}) async-start(), calls=%async_computation.3 | async-start | bytes 10616832 | tf_op jit(solution)/shard_map/reduce_scatter | solution.py:736
  163.0 15.3 %collective-permute-start.8 = (f32[4,136,128]{2,1,0:T(8,128)S(1)}, f32[4,136,128]{2,1,0:T(8,128)S(1)}, u32[]{:S(2)}, u32[]{:S(2)}) collective-permute-start(f32[4,136,128]{2,1,0:T(8,128)S(1)} %get-tuple-element.216.value), channel_id=1, source_target_pairs={{0,8},{4,12},{8,0},{12,4},{16,24},{20,28},{24,16},{28,20},{1,9},{5... | collective-permute-start | bytes 835592 | tf_op jit(solution)/shard_map/ppermute | solution.py:701
  179.0 16.8 %collective-permute-start.9 = (f32[4,136,128]{2,1,0:T(8,128)S(1)}, f32[4,136,128]{2,1,0:T(8,128)S(1)}, u32[]{:S(2)}, u32[]{:S(2)}) collective-permute-start(f32[4,136,128]{2,1,0:T(8,128)S(1)} %get-tuple-element.218.value), channel_id=1, source_target_pairs={{0,16},{4,20},{8,24},{12,28},{16,0},{20,4},{24,8},{28,12},{1,17},{... | collective-permute-start | bytes 835592 | tf_op jit(solution)/shard_map/ppermute | solution.py:701
  182.6 15.1 %collective-permute-start.11 = (f32[128,512]{1,0:T(8,128)S(1)}, f32[128,512]{1,0:T(8,128)S(1)}, u32[]{:S(2)}, u32[]{:S(2)}) collective-permute-start(f32[128,512]{1,0:T(8,128)S(1)} %get-tuple-element.245), channel_id=1, source_target_pairs={{0,8},{4,12},{8,0},{12,4},{16,24},{20,28},{24,16},{28,20},{1,9},{5... | collective-permute-start | bytes 786440 | tf_op jit(solution)/shard_map/ppermute | solution.py:853
  183.2 21.1 %collective-permute-start.12 = (f32[128,1024]{1,0:T(8,128)S(1)}, f32[128,1024]{1,0:T(8,128)S(1)}, u32[]{:S(2)}, u32[]{:S(2)}) collective-permute-start(f32[128,1024]{1,0:T(8,128)S(1)} %get-tuple-element.247), channel_id=1, source_target_pairs={{0,16},{4,20},{8,24},{12,28},{16,0},{20,4},{24,8},{28,12},{1,17},{... | collective-permute-start | bytes 1572872 | tf_op jit(solution)/shard_map/ppermute | solution.py:853
  205.0 23.7 %collective-permute-start.13 = (f32[64,512]{1,0:T(8,128)S(1)}, f32[64,512]{1,0:T(8,128)S(1)}, u32[]{:S(2)}, u32[]{:S(2)}) collective-permute-start(f32[64,512]{1,0:T(8,128)S(1)} %get-tuple-element.256), channel_id=1, source_target_pairs={{0,16},{4,20},{8,24},{12,28},{16,0},{20,4},{24,8},{28,12},{1,17},{... | collective-permute-start | bytes 393224 | tf_op jit(solution)/shard_map/ppermute | solution.py:853
  205.4 23.3 %collective-permute-start.14 = (f32[64,1024]{1,0:T(8,128)S(1)}, f32[64,1024]{1,0:T(8,128)S(1)}, u32[]{:S(2)}, u32[]{:S(2)}) collective-permute-start(f32[64,1024]{1,0:T(8,128)S(1)} %get-tuple-element.258), channel_id=1, source_target_pairs={{0,8},{4,12},{8,0},{12,4},{16,24},{20,28},{24,16},{28,20},{1,9},{5... | collective-permute-start | bytes 786440 | tf_op jit(solution)/shard_map/ppermute | solution.py:853
  228.7 17.8 %collective-permute-start.16 = (f32[256,3584]{1,0:T(8,128)}, f32[256,3584]{1,0:T(8,128)}, u32[]{:S(2)}, u32[]{:S(2)}) collective-permute-start(f32[256,3584]{1,0:T(8,128)} %get-tuple-element.268), channel_id=1, source_target_pairs={{0,4},{4,0},{8,12},{12,8},{16,20},{20,16},{24,28},{28,24},{1,5},{5... | collective-permute-start | bytes 11010056 | tf_op jit(solution)/shard_map/ppermute | solution.py:853
  231.4 20.0 %collective-permute-start.15 = (f32[32,6144]{1,0:T(8,128)S(1)}, f32[32,6144]{1,0:T(8,128)S(1)}, u32[]{:S(2)}, u32[]{:S(2)}) collective-permute-start(f32[32,6144]{1,0:T(8,128)S(1)} %get-tuple-element.266), channel_id=1, source_target_pairs={{0,1},{1,0},{2,3},{3,2},{4,5},{5,4},{6,7},{7,6},{8,9},{9,8},{10,11... | collective-permute-start | bytes 2359304 | tf_op jit(solution)/shard_map/ppermute | solution.py:853
  254.5 20.1 %collective-permute-start.17 = (f32[16,6144]{1,0:T(8,128)S(1)}, f32[16,6144]{1,0:T(8,128)S(1)}, u32[]{:S(2)}, u32[]{:S(2)}) collective-permute-start(f32[16,6144]{1,0:T(8,128)S(1)} %get-tuple-element.272), channel_id=1, source_target_pairs={{0,2},{1,3},{2,0},{3,1},{4,6},{5,7},{6,4},{7,5},{8,10},{9,11},{10,... | collective-permute-start | bytes 1179656 | tf_op jit(solution)/shard_map/ppermute | solution.py:853
  257.0 18.8 %collective-permute-start.18 = (f32[128,1536]{1,0:T(8,128)S(1)}, f32[128,1536]{1,0:T(8,128)S(1)}, u32[]{:S(2)}, u32[]{:S(2)}) collective-permute-start(f32[128,1536]{1,0:T(8,128)S(1)} %get-tuple-element.273), channel_id=1, source_target_pairs={{0,8},{4,12},{8,0},{12,4},{16,24},{20,28},{24,16},{28,20},{1,9},{5... | collective-permute-start | bytes 2359304 | tf_op jit(solution)/shard_map/ppermute | solution.py:853
  257.6 24.2 %collective-permute-start.19 = (f32[128,2048]{1,0:T(8,128)S(1)}, f32[128,2048]{1,0:T(8,128)S(1)}, u32[]{:S(2)}, u32[]{:S(2)}) collective-permute-start(f32[128,2048]{1,0:T(8,128)S(1)} %get-tuple-element.275), channel_id=1, source_target_pairs={{0,16},{4,20},{8,24},{12,28},{16,0},{20,4},{24,8},{28,12},{1,17},{... | collective-permute-start | bytes 3145736 | tf_op jit(solution)/shard_map/ppermute | solution.py:853
  268.1 15.1 %collective-permute-start.23 = (f32[256,2560]{1,0:T(8,128)}, f32[256,2560]{1,0:T(8,128)S(1)}, u32[]{:S(2)}, u32[]{:S(2)}) collective-permute-start(f32[256,2560]{1,0:T(8,128)} %get-tuple-element.293), channel_id=1, source_target_pairs={{0,4},{4,0},{8,12},{12,8},{16,20},{20,16},{24,28},{28,24},{1,5},{5... | collective-permute-start | bytes 7864328 | tf_op jit(solution)/shard_map/ppermute | solution.py:853
  285.0 26.1 %collective-permute-start.25 = (f32[128,1536]{1,0:T(8,128)S(1)}, f32[128,1536]{1,0:T(8,128)S(1)}, u32[]{:S(2)}, u32[]{:S(2)}) collective-permute-start(f32[128,1536]{1,0:T(8,128)S(1)} %get-tuple-element.298), channel_id=1, source_target_pairs={{0,16},{4,20},{8,24},{12,28},{16,0},{20,4},{24,8},{28,12},{1,17},{... | collective-permute-start | bytes 2359304 | tf_op jit(solution)/shard_map/ppermute | solution.py:853
  286.6 24.6 %collective-permute-start.22 = (f32[64,2048]{1,0:T(8,128)S(1)}, f32[64,2048]{1,0:T(8,128)S(1)}, u32[]{:S(2)}, u32[]{:S(2)}) collective-permute-start(f32[64,2048]{1,0:T(8,128)S(1)} %get-tuple-element.291), channel_id=1, source_target_pairs={{0,8},{4,12},{8,0},{12,4},{16,24},{20,28},{24,16},{28,20},{1,9},{5... | collective-permute-start | bytes 1572872 | tf_op jit(solution)/shard_map/ppermute | solution.py:853
  288.0 23.2 %collective-permute-start.24 = (f32[128,1024]{1,0:T(8,128)S(1)}, f32[128,1024]{1,0:T(8,128)S(1)}, u32[]{:S(2)}, u32[]{:S(2)}) collective-permute-start(f32[128,1024]{1,0:T(8,128)S(1)} %get-tuple-element.296), channel_id=1, source_target_pairs={{0,8},{4,12},{8,0},{12,4},{16,24},{20,28},{24,16},{28,20},{1,9},{5... | collective-permute-start | bytes 1572872 | tf_op jit(solution)/shard_map/ppermute | solution.py:853
  288.6 17.7 %collective-permute-start.20 = (f32[16,6144]{1,0:T(8,128)S(1)}, f32[16,6144]{1,0:T(8,128)S(1)}, u32[]{:S(2)}, u32[]{:S(2)}) collective-permute-start(f32[16,6144]{1,0:T(8,128)S(1)} %get-tuple-element.288.refs_0_), channel_id=1, source_target_pairs={{0,2},{1,3},{2,0},{3,1},{4,6},{5,7},{6,4},{7,5},{8,10},{9,11},{10,... | collective-permute-start | bytes 1179656 | tf_op jit(solution)/shard_map/ppermute | solution.py:853
  289.1 22.0 %collective-permute-start.21 = (f32[64,1536]{1,0:T(8,128)S(1)}, f32[64,1536]{1,0:T(8,128)S(1)}, u32[]{:S(2)}, u32[]{:S(2)}) collective-permute-start(f32[64,1536]{1,0:T(8,128)S(1)} %get-tuple-element.289), channel_id=1, source_target_pairs={{0,16},{4,20},{8,24},{12,28},{16,0},{20,4},{24,8},{28,12},{1,17},{... | collective-permute-start | bytes 1179656 | tf_op jit(solution)/shard_map/ppermute | solution.py:853
  312.0 16.0 %collective-permute-start.27 = (f32[32,3584]{1,0:T(8,128)S(1)}, f32[32,3584]{1,0:T(8,128)S(1)}, u32[]{:S(2)}, u32[]{:S(2)}) collective-permute-start(f32[32,3584]{1,0:T(8,128)S(1)} %get-tuple-element.302), channel_id=1, source_target_pairs={{0,1},{1,0},{2,3},{3,2},{4,5},{5,4},{6,7},{7,6},{8,9},{9,8},{10,11... | collective-permute-start | bytes 1376264 | tf_op jit(solution)/shard_map/ppermute | solution.py:853
  313.6 37.0 %collective-permute-start.26 = (f32[32,6144]{1,0:T(8,128)S(1)}, f32[32,6144]{1,0:T(8,128)S(1)}, u32[]{:S(2)}, u32[]{:S(2)}) collective-permute-start(f32[32,6144]{1,0:T(8,128)S(1)} %get-tuple-element.301.refs_0_), channel_id=1, source_target_pairs={{0,1},{1,0},{2,3},{3,2},{4,5},{5,4},{6,7},{7,6},{8,9},{9,8},{10,11... | collective-permute-start | bytes 2359304 | tf_op jit(solution)/shard_map/ppermute | solution.py:853
  328.7 21.9 %collective-permute-start.31 = (f32[32,2560]{1,0:T(8,128)S(1)}, f32[32,2560]{1,0:T(8,128)S(1)}, u32[]{:S(2)}, u32[]{:S(2)}) collective-permute-start(f32[32,2560]{1,0:T(8,128)S(1)} %get-tuple-element.311), channel_id=1, source_target_pairs={{0,1},{1,0},{2,3},{3,2},{4,5},{5,4},{6,7},{7,6},{8,9},{9,8},{10,11... | collective-permute-start | bytes 983048 | tf_op jit(solution)/shard_map/ppermute | solution.py:853
  328.8 20.8 %collective-permute-start.30 = (f32[16,3584]{1,0:T(8,128)S(1)}, f32[16,3584]{1,0:T(8,128)S(1)}, u32[]{:S(2)}, u32[]{:S(2)}) collective-permute-start(f32[16,3584]{1,0:T(8,128)S(1)} %get-tuple-element.310), channel_id=1, source_target_pairs={{0,2},{1,3},{2,0},{3,1},{4,6},{5,7},{6,4},{7,5},{8,10},{9,11},{10,... | collective-permute-start | bytes 688136 | tf_op jit(solution)/shard_map/ppermute | solution.py:853
  352.4 16.3 %collective-permute-start.32 = (f32[16,3584]{1,0:T(8,128)S(1)}, f32[16,3584]{1,0:T(8,128)S(1)}, u32[]{:S(2)}, u32[]{:S(2)}) collective-permute-start(f32[16,3584]{1,0:T(8,128)S(1)} %get-tuple-element.314.refs_0_), channel_id=1, source_target_pairs={{0,2},{1,3},{2,0},{3,1},{4,6},{5,7},{6,4},{7,5},{8,10},{9,11},{10,... | collective-permute-start | bytes 688136 | tf_op jit(solution)/shard_map/ppermute | solution.py:853
  369.3 15.3 %collective-permute-start.34 = (f32[32,3584]{1,0:T(8,128)S(1)}, f32[32,3584]{1,0:T(8,128)S(1)}, u32[]{:S(2)}, u32[]{:S(2)}) collective-permute-start(f32[32,3584]{1,0:T(8,128)S(1)} %get-tuple-element.318.refs_0_), channel_id=1, source_target_pairs={{0,1},{1,0},{2,3},{3,2},{4,5},{5,4},{6,7},{7,6},{8,9},{9,8},{10,11... | collective-permute-start | bytes 1376264 | tf_op jit(solution)/shard_map/ppermute | solution.py:853
  (40 other events, 220.2 us)
Sparse Core Ops, SparseCore 0:
  132.6 94.5 reduce-scatter.1

commit v5 on v4

--- a/solution.py
+++ b/solution.py
@@ -130,16 +130,13 @@
     low, scale = norm(x0, g1[...])
     a1[0] = low
     r1[0] = scale
-    total = jnp.zeros((steps, D), F32)
     for at in range(0, FF, D):
         hidden = dot(low, w1[:, at : at + D])
         gate = sigmoid(hidden)
         active = hidden * gate
         d1[0, :, at : at + D] = (gate * (1.0 + hidden - active)).astype(BF16)
-        active = active.astype(BF16)
-        s1[0, :, at : at + D] = active
-        total += dot(active, w2[at : at + D, :])
-    after = x0 + 0.5 * total
+        s1[0, :, at : at + D] = active.astype(BF16)
+    after = x0 + 0.5 * dot(s1[0], w2[...])
     x1[0] = after
     low, scale = norm(after, g2[...])
     a2[0] = low
@@ -279,16 +276,13 @@
         x3 = x2[0] + dot(active, w_conv[...])
         low, scale4 = norm(x3, g4[...])
         a4[0] = low
-        total = jnp.zeros_like(x3)
         for at in range(0, FF, D):
             hidden = dot(low, w3[:, at : at + D])
             gate = sigmoid(hidden)
             active = hidden * gate
             slope[:, at : at + D] = (gate * (1.0 + hidden - active)).astype(BF16)
-            active = active.astype(BF16)
-            s4[0, :, at : at + D] = active
-            total += dot(active, w4[at : at + D, :])
-        x4 = x3 + 0.5 * total
+            s4[0, :, at : at + D] = active.astype(BF16)
+        x4 = x3 + 0.5 * dot(s4[0], w4[...])
         centred = x4 - mean(x4)
         scale = lax.rsqrt(mean(centred * centred) + EPS)
         unit5 = centred * scale
@@ -300,12 +294,10 @@
         gx4 = scale * (inner - mean(inner) - unit5 * mean(inner * unit5))
         gf_low = (0.5 * gx4).astype(BF16)
         gf[0] = gf_low
-        back = jnp.zeros_like(x3)
         for at in range(0, FF, D):
             hidden = (dot_t(gf_low, w4[at : at + D, :]) * slope[:, at : at + D].astype(F32)).astype(BF16)
             gh[0, :, at : at + D] = hidden
-            back += dot_t(hidden, w3[:, at : at + D])
-        back, gain4 = norm_back(back, low, scale4, g4[...])
+        back, gain4 = norm_back(dot_t(gh[0], w3[...]), low, scale4, g4[...])
         accumulate(ln4, gain4)
         grad3 = gx4 + back
         gx3[0] = grad3
@@ -430,12 +422,10 @@
 ):
     steps = gx1.shape[1]
     low = gf[0]
-    back = jnp.zeros((steps, D), F32)
     for at in range(0, FF, D):
         hidden = (dot_t(low, w2[at : at + D, :]) * d1[0, :, at : at + D].astype(F32)).astype(BF16)
         gh[0, :, at : at + D] = hidden
-        back += dot_t(hidden, w1[:, at : at + D])
-    back, gain = norm_back(back, a1[0], r1[0], g1[...])
+    back, gain = norm_back(dot_t(gh[0], w1[...]), a1[0], r1[0], g1[...])
     accumulate(ln1, gain)
     low = (gx1[0] + back).astype(BF16)
     gxr[0] = low
@@ -1106,7 +1096,7 @@
         kept, sent, weights_token = weight_sums(
             [(flatten(a3), flatten(gq)), (flatten(z), flatten(gz))], share, core, None, hops[-2:-1]
         )
-        early.begin(kept, sent, D)
+        early.begin(kept, sent, 3 * D // 2)
         token = together(bits, [early], [weights_token, hops[-1]])
         gu, gb, gc, mixed_token = call(
             mix_back_kernel,
@@ -1142,7 +1132,7 @@
         [(flatten(a2), flatten(gp)), (flatten(s1), flatten(gf1))], share, core, None, [end_token]
     )
     middle = Sum([(0, PROJ, False), (PROJ, FF, True)])
-    middle.begin(kept, sent, PROJ)
+    middle.begin(kept, sent, (PROJ + FF) // 2)
     token = weights_token
     while early.steps[0][0] == "chips":
         token = together(bits, [early], [token])
@@ -1161,12 +1151,13 @@
         "front_back",
     )
     small = [taps_grad, ln1, ln2, ln3, ln4, ln5]
-    token = together(bits, [early, middle], [back_token])
+    token = together(bits, [middle], [back_token])
+    token = together(bits, [early], [token])
     last = Sum([(0, FF, False), (FF, SUB * mels, False), (FF + D - 128, 128, False)])
     kept, sent, weights_token = weight_sums(
         [(flatten(a1), flatten(gh1)), (flatten(gxr), flatten(flat))], share, core, small, [token], 1
     )
-    last.begin(kept, sent, 2 * D)
+    last.begin(kept, sent, (FF + WIDE) // 2)
     token = weights_token
     token = together(bits, [early, middle], [token], 60.0)
     rounds = [(last,), (early, middle, last), (middle, last)]

time: 406 us -> 397 us (0.978)
  waiting for transfers between devices: 130 us -> 115 us
  starting transfers between devices: 47.1 us -> 56.3 us
    ppermute x27, waiting for transfers between devices: 111 us -> 95.5 us  [swap(): return lax.ppermute(value, axis, flip_pairs(lax.axis_size(axis), 1 << bit))]
    ppermute x27, starting transfers between devices: 26.7 us -> 35.8 us  [swap(): return lax.ppermute(value, axis, flip_pairs(lax.axis_size(axis), 1 << bit))]
    pallas_call x12 -> x13, Pallas kernels: 13 us -> 13.6 us  [in_vmem(): pl.pallas_call(kernel, in_specs=[scalars()] + [vmem] * len(ins) + [anywhe...]
  transfers between devices with their start and end apart: 39 -> 39, of which waited for: 20 -> 20; matrix products, arithmetic and copies ran while one was open for 1% -> 1% of each run, Pallas kernels for 26% -> 27%
where the time goes in v5:
time: 397 us; the launch traced here: 396 us
  Pallas kernels  176 us (44%)
  waiting for transfers between devices  115 us (29%)
  starting transfers between devices  56.3 us (14%)
  local copies, waits for them, and re-layouts  15.7 us (4%)
  blocking collectives  15.3 us (4%)
  between operations  14.5 us (4%)
    pallas_call x14, Pallas kernels, call(): pl.pallas_call(with_token, grid=grid, in_specs=[held_spec(a.shape) if kin...  156 us
    ppermute x27, waiting for transfers between devices, swap(): return lax.ppermute(value, axis, flip_pairs(lax.axis_size(axis), 1 << bit))  95.5 us
    ppermute x27, starting transfers between devices, swap(): return lax.ppermute(value, axis, flip_pairs(lax.axis_size(axis), 1 << bit))  35.8 us
    ppermute x6, waiting for transfers between devices, entering(): other = lax.ppermute(value, 'seq', flip_pairs(count, 1 << bit))  16.5 us
    all_to_all x1, blocking collectives, sum_over_all(): return jnp.sum(lax.all_to_all(copies, ('rec', 'seq'), 0, 0), axis=0)  15.3 us
    pallas_call x13, Pallas kernels, in_vmem(): pl.pallas_call(kernel, in_specs=[scalars()] + [vmem] * len(ins) + [anywhe...  13.6 us
    ppermute x6, starting transfers between devices, entering(): other = lax.ppermute(value, 'seq', flip_pairs(count, 1 << bit))  11.8 us
    unnamed x51, local copies, waits for them, and re-layouts  10.9 us
  transfers between devices with their start and end apart: 39, of which 20 were waited for; matrix products, arithmetic and copies ran while one was open for 1% of the time, Pallas kernels for 27%

profile of v5, /device:TPU:0, one launch (start us, length us, event | category | flops | bytes accessed | tf_op | source)
XLA Modules:
  0.0 395.6 jit_solution(894535259270244433)
XLA Ops:
  8.2 20.0 %front.1 = (bf16[4,256,512]{2,1,0:T(8,128)(2,1)}, f32[4,256,512]{2,1,0:T(8,128)}, bf16[4,256,512]{2,1,0:T(8,128)(2,1)}, f32[4,256,1]{2,1,0:T(8,128)}, bf16[4,256...) custom-call(bf16[4,80,1024]{2,1,0:T(8,128)(2,1)} %bitcast.59, ...), custom_call_target="tpu_custom_call" | custom-call | flops 46000001024 | tf_op jit(solution)/shard_map/front/pallas_call | solution.py:628
  35.1 7.0 %collective-permute-done.1.other = f32[4,136,128]{2,1,0:T(8,128)S(1)} collective-permute-done((f32[4,136,128]{2,1,0:T(8,128)S(1)}, f32[4,136,128]{2,1,0:T(8,128)S(1)}, u32[]{:S(2)}, u32[]{:S(2)}) %collective-permute-start.1) | collective-permute-done | bytes 278560 | tf_op jit(solution)/shard_map/ppermute | solution.py:691
  45.0 7.3 %mix.1 = (f32[4,256,512]{2,1,0:T(8,128)}, bf16[4,8,256,256]{3,2,1,0:T(8,128)(2,1)}, bf16[4,8,256,256]{3,2,1,0:T(8,128)(2,1)}, f32[8,128]{1,0:T(8,128)}) custom-call(bf16[4,256,512]{2,1,0:T(8,128)(2,1)} %get-tuple-element.177.refs_0_.refs_1_, bf16[4,256,256]{2,1,0:T(8,128)(2,1)} %get-tuple-element.178.refs_1_, ...), custom_call_target="tpu_custom_call" | custom-call | flops 16099999744 | tf_op jit(solution)/shard_map/mix/pallas_call | solution.py:628
  54.3 9.1 %lift.1 = (bf16[4,256,512]{2,1,0:T(8,128)(2,1)}, bf16[4,256,512]{2,1,0:T(8,128)(2,1)}, bf16[4,256,512]{2,1,0:T(8,128)(2,1)}, f32[4,256,512]{2,1,0:T(8,128)}, bf1...) custom-call(f32[4,256,512]{2,1,0:T(8,128)} %get-tuple-element.182.re, ...), custom_call_target="tpu_custom_call" | custom-call | flops 20700000256 | tf_op jit(solution)/shard_map/lift/pallas_call | solution.py:628
  70.4 5.6 %depth.1 = (f32[4,256,512]{2,1,0:T(8,128)}, f32[2,512]{1,0:T(2,128)}, f32[8,128]{1,0:T(8,128)}) custom-call(f32[4,256,512]{2,1,0:T(8,128)} %get-tuple-element.192.refs_0_.refs_5_, f32[4,8,512]{2,1,0:T(8,128)} %copy-done.21, f32[4,8,512]{2,1,0:T(8,128)} %copy-done.22, f32[2,4]{1,0:T(2,128)S(1)} %pad_maximum_fusion.refs_4_.keep.refs_3_.refs_8_, ...), custom_call_target="tpu_custom_call" | custom-call | flops 13799999488 | tf_op jit(solution)/shard_map/depth/pallas_call | solution.py:628
  76.8 15.3 %all_to_all.10 = f32[32,2,512]{2,1,0:T(2,128)S(1)} all-to-all(f32[32,2,512]{2,1,0:T(2,128)S(1)} %broadcast_in_dim.9), channel_id=1, replica_groups=mesh['seq'=8,'rec'=4] {'rec','seq'}, dimensions={0} | all-to-all | bytes 262144 | tf_op jit(solution)/shard_map/all_to_all | solution.py:722
  92.7 21.9 %late.1 = (bf16[4,256,512]{2,1,0:T(8,128)(2,1)}, bf16[4,256,512]{2,1,0:T(8,128)(2,1)}, bf16[4,256,512]{2,1,0:T(8,128)(2,1)}, bf16[4,256,2048]{2,1,0:T(8,128)(2,1...) custom-call(f32[4,256,512]{2,1,0:T(8,128)} %get-tuple-element.195.re, ...), custom_call_target="tpu_custom_call" | custom-call | flops 52899999744 | tf_op jit(solution)/shard_map/late/pallas_call | solution.py:628
  118.7 11.4 %late_weights.1 = (f32[512,4608]{1,0:T(8,128)}, f32[8,128]{1,0:T(8,128)}) custom-call(bf16[1024,512]{1,0:T(8,128)(2,1)} %bitcast.87, bf16[1024,512]{1,0:T(8,128)(2,1)} %bitcast.86, bf16[1024,2048]{1,0:T(8,128)(2,1)} %bitcast.73, bf16[1024,2048]{1,0:T(8,128)(2,1)} %bitcast.74, bf16[1024,512]{1,0:T(8,128)(2,1)} %bitcast.89, bf16[1024,512]{1,0:T(8,128)(2,1)} %bitcast.88), custom_call_target="tpu_custom_call" | custom-call | flops 25300000768 | tf_op jit(solution)/shard_map/late_weights/pallas_call | solution.py:628
  135.4 7.3 %depth_grad.1 = (f32[4,256,512]{2,1,0:T(8,128)}, f32[16,512]{1,0:T(8,128)}, f32[8,128]{1,0:T(8,128)}) custom-call(f32[4,256,512]{2,1,0:T(8,128)} %get-tuple-element.199.refs_0_, f32[4,256,512]{2,1,0:T(8,128)} %get-tuple-element.195.refs_0_.refs_1_, f32[2,512]{1,0:T(2,128)} %reduce_sum.18.refs_3_.refs_2_, f32[2,512]{1,0:T(2,128)} %copy-done.17, ...), custom_call_target="tpu_custom_call" | custom-call | flops 11500000256 | tf_op jit(solution)/shard_map/depth_grad/pallas_call | solution.py:628
  143.4 12.5 %conv_back.1 = (bf16[4,256,1024]{2,1,0:T(8,128)(2,1)}, f32[4,256,512]{2,1,0:T(8,128)}, bf16[4,256,512]{2,1,0:T(8,128)(2,1)}, bf16[4,256,512]{2,1,0:T(8,128)(2,1)...) custom-call(f32[4,256,512]{2,1,0:T(8,128)} %get-tuple-element.208.refs_0_, ...), custom_call_target="tpu_custom_call" | custom-call | flops 4600000000 | tf_op jit(solution)/shard_map/conv_back/pallas_call | solution.py:628
  162.6 6.5 %weights.3 = (f32[256,1536]{1,0:T(8,128)}, f32[256,1536]{1,0:T(8,128)}, f32[8,128]{1,0:T(8,128)}) custom-call(s32[1]{0:T(128)} %bitcast.26.refs_0_, bf16[1024,512]{1,0:T(8,128)(2,1)} %bitcast.82, bf16[1024,512]{1,0:T(8,128)(2,1)} %bitcast.81, bf16[1024,1024]{1,0:T(8,128)(2,1)} %bitcast.76, bf16[1024,512]{1,0:T(8,128)(2,1)} %bitcast.83, ...), custom_call_target="tpu_custom_call" | custom-call | flops 23000000512 | tf_op jit(solution)/shard_map/weights/pallas_call | solution.py:628
  169.1 6.8 %collective-permute-done.8.other = f32[4,136,128]{2,1,0:T(8,128)S(1)} collective-permute-done((f32[4,136,128]{2,1,0:T(8,128)S(1)}, f32[4,136,128]{2,1,0:T(8,128)S(1)}, u32[]{:S(2)}, u32[]{:S(2)}) %collective-permute-start.8) | collective-permute-done | bytes 278560 | tf_op jit(solution)/shard_map/ppermute | solution.py:691
  181.5 11.8 %mix_back.1 = (f32[4,256,512]{2,1,0:T(8,128)}, f32[4,256,256]{2,1,0:T(8,128)}, bf16[4,256,256]{2,1,0:T(8,128)(2,1)}, f32[8,128]{1,0:T(8,128)}) custom-call(bf16[4,256,512]{2,1,0:T(8,128)(2,1)} %get-tuple-element.177.refs_0_.refs_1_, bf16[4,256,256]{2,1,0:T(8,128)(2,1)} %get-tuple-element.178.refs_1_, bf16[4,256,256]{2,1,0:T(8,128)(2,1)} %get-tuple-element.179.refs_2_, ...), custom_call_target="tpu_custom_call" | custom-call | flops 27599998976 | tf_op jit(solution)/shard_map/mix_back/pallas_call | solution.py:628
  201.9 9.7 %mix_end.1 = (bf16[4,256,1536]{2,1,0:T(8,128)(2,1)}, f32[4,256,512]{2,1,0:T(8,128)}, bf16[4,256,512]{2,1,0:T(8,128)(2,1)}, f32[1,512]{1,0:T(1,128)}, f32[8,128]{1,0:T(8,128)}) custom-call(f32[4,136,128]{2,1,0:T(8,128)} %copy-done.11, bf16[4,256,512]{2,1,0:T(8,128)(2,1)} %get-tuple-element.177.refs_0_.refs_1_, ...), custom_call_target="tpu_custom_call" | custom-call | flops 23000000512 | tf_op jit(solution)/shard_map/mix_end/pallas_call | solution.py:628
  212.3 11.4 %weights.4 = (f32[256,3584]{1,0:T(8,128)}, f32[256,3584]{1,0:T(8,128)}, f32[8,128]{1,0:T(8,128)}) custom-call(s32[1]{0:T(128)} %bitcast.26.refs_0_, bf16[1024,512]{1,0:T(8,128)(2,1)} %bitcast.80, bf16[1024,2048]{1,0:T(8,128)(2,1)} %bitcast.71, bf16[1024,1536]{1,0:T(8,128)(2,1)} %bitcast.75, bf16[1024,512]{1,0:T(8,128)(2,1)} %bitcast.85, f32[8,128]{1,0:T(8,128)S(1)} %copy-done.13), custom_call_target="tpu_custom_call" | custom-call | flops 23000000512 | tf_op jit(solution)/shard_map/weights/pallas_call | solution.py:628
  228.0 12.6 %front_back.1 = (bf16[4,256,2048]{2,1,0:T(8,128)(2,1)}, bf16[4,256,512]{2,1,0:T(8,128)(2,1)}, f32[4,80,1024]{2,1,0:T(8,128)}, f32[1,512]{1,0:T(1,128)}, f32[8,128]{1,0:T(8,128)}) custom-call(f32[4,256,512]{2,1,0:T(8,128)} %get-tuple-element.251.refs_0_, bf16[4,256,512]{2,1,0:T(8,128)(2,1)} %get-tuple-element.252.refs_1_, bf16[2048,512]{1,0:T(8,128)(2,1)} %refs_2_.5, ...), custom_call_target="tpu_custom_call" | custom-call | flops 69000003584 | tf_op jit(solution)/shard_map/front_back/pallas_call | solution.py:628
  249.5 9.1 %weights.5 = (f32[256,2560]{1,0:T(8,128)}, f32[256,2560]{1,0:T(8,128)}, f32[8,128]{1,0:T(8,128)}) custom-call(s32[1]{0:T(128)} %bitcast.26.refs_0_, bf16[1024,512]{1,0:T(8,128)(2,1)} %bitcast.79, bf16[1024,512]{1,0:T(8,128)(2,1)} %bitcast.84, bf16[1024,2048]{1,0:T(8,128)(2,1)} %bitcast.72, bf16[1024,512]{1,0:T(8,128)(2,1)} %bitcast.78, ...), custom_call_target="tpu_custom_call" | custom-call | flops 23000000512 | tf_op jit(solution)/shard_map/weights/pallas_call | solution.py:628
  258.6 7.6 %collective-permute-done.18.refs_2_ = f32[128,1792]{1,0:T(8,128)S(1)} collective-permute-done((f32[128,1792]{1,0:T(8,128)S(1)}, f32[128,1792]{1,0:T(8,128)S(1)}, u32[]{:S(2)}, u32[]{:S(2)}) %collective-permute-start.18) | collective-permute-done | bytes 917536 | tf_op jit(solution)/shard_map/ppermute | solution.py:843
  277.2 15.9 %collective-permute-done.20.refs_1_ = f32[16,6144]{1,0:T(8,128)S(1)} collective-permute-done((f32[16,6144]{1,0:T(8,128)S(1)}, f32[16,6144]{1,0:T(8,128)S(1)}, u32[]{:S(2)}, u32[]{:S(2)}) %collective-permute-start.20) | collective-permute-done | bytes 393248 | tf_op jit(solution)/shard_map/ppermute | solution.py:843
  302.2 5.7 %collective-permute-done.28.refs_2_ = f32[64,1280]{1,0:T(8,128)S(1)} collective-permute-done((f32[64,1280]{1,0:T(8,128)S(1)}, f32[64,1280]{1,0:T(8,128)S(1)}, u32[]{:S(2)}, u32[]{:S(2)}) %collective-permute-start.28) | collective-permute-done | bytes 327712 | tf_op jit(solution)/shard_map/ppermute | solution.py:843
  317.1 20.0 %collective-permute-done.30.refs_3_ = f32[16,3584]{1,0:T(8,128)S(1)} collective-permute-done((f32[16,3584]{1,0:T(8,128)S(1)}, f32[16,3584]{1,0:T(8,128)S(1)}, u32[]{:S(2)}, u32[]{:S(2)}) %collective-permute-start.30) | collective-permute-done | bytes 229408 | tf_op jit(solution)/shard_map/ppermute | solution.py:843
  342.6 15.3 %collective-permute-done.33.refs_3_ = f32[16,2560]{1,0:T(8,128)S(1)} collective-permute-done((f32[16,2560]{1,0:T(8,128)S(1)}, f32[16,2560]{1,0:T(8,128)S(1)}, u32[]{:S(2)}, u32[]{:S(2)}) %collective-permute-start.33) | collective-permute-done | bytes 163872 | tf_op jit(solution)/shard_map/ppermute | solution.py:843
  362.7 10.1 %collective-permute-done.35.refs_3_ = f32[16,2560]{1,0:T(8,128)S(1)} collective-permute-done((f32[16,2560]{1,0:T(8,128)S(1)}, f32[16,2560]{1,0:T(8,128)S(1)}, u32[]{:S(2)}, u32[]{:S(2)}) %collective-permute-start.35) | collective-permute-done | bytes 163872 | tf_op jit(solution)/shard_map/ppermute | solution.py:843
  379.7 6.2 %collective-permute-done.36.refs_1_ = f32[32,2560]{1,0:T(8,128)S(1)} collective-permute-done((f32[32,2560]{1,0:T(8,128)S(1)}, f32[32,2560]{1,0:T(8,128)S(1)}, u32[]{:S(2)}, u32[]{:S(2)}) %collective-permute-start.36) | collective-permute-done | bytes 327712 | tf_op jit(solution)/shard_map/ppermute | solution.py:843
  (153 shorter events, 115.1 us)
Async XLA Ops:
  116.1 14.7 %all-to-all-start.1 = ((f32[32,2,512]{2,1,0:T(2,128)}), f32[32,2,512]{2,1,0:T(2,128)S(1)}, u32[]{:S(2)}, u32[]{:S(2)}) async-start(f32[32,2,512]{2,1,0:T(2,128)} %broadcast_in_dim.10), calls=%async_computation.1 | async-start | bytes 262144 | tf_op jit(solution)/shard_map/all_to_all | solution.py:722
  118.6 105.1 %reduce-scatter.2.cloned.1.call-start = ((), (), s32[]{:S(2)}) async-start(), calls=%async_computation.3 | async-start | bytes 10616832 | tf_op jit(solution)/shard_map/reduce_scatter | solution.py:726
  160.6 15.3 %collective-permute-start.8 = (f32[4,136,128]{2,1,0:T(8,128)S(1)}, f32[4,136,128]{2,1,0:T(8,128)S(1)}, u32[]{:S(2)}, u32[]{:S(2)}) collective-permute-start(f32[4,136,128]{2,1,0:T(8,128)S(1)} %get-tuple-element.217.value), channel_id=1, source_target_pairs={{0,8},{4,12},{8,0},{12,4},{16,24},{20,28},{24,16},{28,20},{1,9},{5... | collective-permute-start | bytes 835592 | tf_op jit(solution)/shard_map/ppermute | solution.py:691
  176.6 16.7 %collective-permute-start.9 = (f32[4,136,128]{2,1,0:T(8,128)S(1)}, f32[4,136,128]{2,1,0:T(8,128)S(1)}, u32[]{:S(2)}, u32[]{:S(2)}) collective-permute-start(f32[4,136,128]{2,1,0:T(8,128)S(1)} %get-tuple-element.219.value), channel_id=1, source_target_pairs={{0,16},{4,20},{8,24},{12,28},{16,0},{20,4},{24,8},{28,12},{1,17},{... | collective-permute-start | bytes 835592 | tf_op jit(solution)/shard_map/ppermute | solution.py:691
  180.2 18.9 %collective-permute-start.11 = (f32[128,768]{1,0:T(8,128)S(1)}, f32[128,768]{1,0:T(8,128)S(1)}, u32[]{:S(2)}, u32[]{:S(2)}) collective-permute-start(f32[128,768]{1,0:T(8,128)S(1)} %get-tuple-element.246), channel_id=1, source_target_pairs={{0,8},{4,12},{8,0},{12,4},{16,24},{20,28},{24,16},{28,20},{1,9},{5... | collective-permute-start | bytes 1179656 | tf_op jit(solution)/shard_map/ppermute | solution.py:843
  180.8 18.3 %collective-permute-start.12 = (f32[128,768]{1,0:T(8,128)S(1)}, f32[128,768]{1,0:T(8,128)S(1)}, u32[]{:S(2)}, u32[]{:S(2)}) collective-permute-start(f32[128,768]{1,0:T(8,128)S(1)} %get-tuple-element.248), channel_id=1, source_target_pairs={{0,16},{4,20},{8,24},{12,28},{16,0},{20,4},{24,8},{28,12},{1,17},{... | collective-permute-start | bytes 1179656 | tf_op jit(solution)/shard_map/ppermute | solution.py:843
  199.8 23.9 %collective-permute-start.13 = (f32[64,768]{1,0:T(8,128)S(1)}, f32[64,768]{1,0:T(8,128)S(1)}, u32[]{:S(2)}, u32[]{:S(2)}) collective-permute-start(f32[64,768]{1,0:T(8,128)S(1)} %get-tuple-element.257), channel_id=1, source_target_pairs={{0,16},{4,20},{8,24},{12,28},{16,0},{20,4},{24,8},{28,12},{1,17},{... | collective-permute-start | bytes 589832 | tf_op jit(solution)/shard_map/ppermute | solution.py:843
  201.3 22.4 %collective-permute-start.14 = (f32[64,768]{1,0:T(8,128)S(1)}, f32[64,768]{1,0:T(8,128)S(1)}, u32[]{:S(2)}, u32[]{:S(2)}) collective-permute-start(f32[64,768]{1,0:T(8,128)S(1)} %get-tuple-element.259), channel_id=1, source_target_pairs={{0,8},{4,12},{8,0},{12,4},{16,24},{20,28},{24,16},{28,20},{1,9},{5... | collective-permute-start | bytes 589832 | tf_op jit(solution)/shard_map/ppermute | solution.py:843
  223.7 16.9 %collective-permute-start.16 = (f32[256,3584]{1,0:T(8,128)}, f32[256,3584]{1,0:T(8,128)}, u32[]{:S(2)}, u32[]{:S(2)}) collective-permute-start(f32[256,3584]{1,0:T(8,128)} %get-tuple-element.269), channel_id=1, source_target_pairs={{0,4},{4,0},{8,12},{12,8},{16,20},{20,16},{24,28},{28,24},{1,5},{5... | collective-permute-start | bytes 11010056 | tf_op jit(solution)/shard_map/ppermute | solution.py:843
  226.4 20.0 %collective-permute-start.15 = (f32[32,6144]{1,0:T(8,128)S(1)}, f32[32,6144]{1,0:T(8,128)S(1)}, u32[]{:S(2)}, u32[]{:S(2)}) collective-permute-start(f32[32,6144]{1,0:T(8,128)S(1)} %get-tuple-element.267), channel_id=1, source_target_pairs={{0,1},{1,0},{2,3},{3,2},{4,5},{5,4},{6,7},{7,6},{8,9},{9,8},{10,11... | collective-permute-start | bytes 2359304 | tf_op jit(solution)/shard_map/ppermute | solution.py:843
  243.7 22.5 %collective-permute-start.18 = (f32[128,1792]{1,0:T(8,128)S(1)}, f32[128,1792]{1,0:T(8,128)S(1)}, u32[]{:S(2)}, u32[]{:S(2)}) collective-permute-start(f32[128,1792]{1,0:T(8,128)S(1)} %get-tuple-element.275), channel_id=1, source_target_pairs={{0,8},{4,12},{8,0},{12,4},{16,24},{20,28},{24,16},{28,20},{1,9},{5... | collective-permute-start | bytes 2752520 | tf_op jit(solution)/shard_map/ppermute | solution.py:843
  245.3 22.2 %collective-permute-start.19 = (f32[128,1792]{1,0:T(8,128)S(1)}, f32[128,1792]{1,0:T(8,128)S(1)}, u32[]{:S(2)}, u32[]{:S(2)}) collective-permute-start(f32[128,1792]{1,0:T(8,128)S(1)} %get-tuple-element.277), channel_id=1, source_target_pairs={{0,16},{4,20},{8,24},{12,28},{16,0},{20,4},{24,8},{28,12},{1,17},{... | collective-permute-start | bytes 2752520 | tf_op jit(solution)/shard_map/ppermute | solution.py:843
  247.0 20.5 %collective-permute-start.17 = (f32[16,6144]{1,0:T(8,128)S(1)}, f32[16,6144]{1,0:T(8,128)S(1)}, u32[]{:S(2)}, u32[]{:S(2)}) collective-permute-start(f32[16,6144]{1,0:T(8,128)S(1)} %get-tuple-element.274), channel_id=1, source_target_pairs={{0,2},{1,3},{2,0},{3,1},{4,6},{5,7},{6,4},{7,5},{8,10},{9,11},{10,... | collective-permute-start | bytes 1179656 | tf_op jit(solution)/shard_map/ppermute | solution.py:843
  270.7 26.5 %collective-permute-start.24 = (f32[128,1280]{1,0:T(8,128)S(1)}, f32[128,1280]{1,0:T(8,128)S(1)}, u32[]{:S(2)}, u32[]{:S(2)}) collective-permute-start(f32[128,1280]{1,0:T(8,128)S(1)} %get-tuple-element.298), channel_id=1, source_target_pairs={{0,8},{4,12},{8,0},{12,4},{16,24},{20,28},{24,16},{28,20},{1,9},{5... | collective-permute-start | bytes 1966088 | tf_op jit(solution)/shard_map/ppermute | solution.py:843
  271.9 25.3 %collective-permute-start.25 = (f32[128,1280]{1,0:T(8,128)S(1)}, f32[128,1280]{1,0:T(8,128)S(1)}, u32[]{:S(2)}, u32[]{:S(2)}) collective-permute-start(f32[128,1280]{1,0:T(8,128)S(1)} %get-tuple-element.300), channel_id=1, source_target_pairs={{0,16},{4,20},{8,24},{12,28},{16,0},{20,4},{24,8},{28,12},{1,17},{... | collective-permute-start | bytes 1966088 | tf_op jit(solution)/shard_map/ppermute | solution.py:843
  272.8 24.4 %collective-permute-start.21 = (f32[64,1792]{1,0:T(8,128)S(1)}, f32[64,1792]{1,0:T(8,128)S(1)}, u32[]{:S(2)}, u32[]{:S(2)}) collective-permute-start(f32[64,1792]{1,0:T(8,128)S(1)} %get-tuple-element.291), channel_id=1, source_target_pairs={{0,16},{4,20},{8,24},{12,28},{16,0},{20,4},{24,8},{28,12},{1,17},{... | collective-permute-start | bytes 1376264 | tf_op jit(solution)/shard_map/ppermute | solution.py:843
  273.9 23.2 %collective-permute-start.22 = (f32[64,1792]{1,0:T(8,128)S(1)}, f32[64,1792]{1,0:T(8,128)S(1)}, u32[]{:S(2)}, u32[]{:S(2)}) collective-permute-start(f32[64,1792]{1,0:T(8,128)S(1)} %get-tuple-element.293), channel_id=1, source_target_pairs={{0,8},{4,12},{8,0},{12,4},{16,24},{20,28},{24,16},{28,20},{1,9},{5... | collective-permute-start | bytes 1376264 | tf_op jit(solution)/shard_map/ppermute | solution.py:843
  274.8 18.3 %collective-permute-start.20 = (f32[16,6144]{1,0:T(8,128)S(1)}, f32[16,6144]{1,0:T(8,128)S(1)}, u32[]{:S(2)}, u32[]{:S(2)}) collective-permute-start(f32[16,6144]{1,0:T(8,128)S(1)} %get-tuple-element.290.refs_0_), channel_id=1, source_target_pairs={{0,2},{1,3},{2,0},{3,1},{4,6},{5,7},{6,4},{7,5},{8,10},{9,11},{10,... | collective-permute-start | bytes 1179656 | tf_op jit(solution)/shard_map/ppermute | solution.py:843
  299.6 38.3 %collective-permute-start.26 = (f32[32,6144]{1,0:T(8,128)S(1)}, f32[32,6144]{1,0:T(8,128)S(1)}, u32[]{:S(2)}, u32[]{:S(2)}) collective-permute-start(f32[32,6144]{1,0:T(8,128)S(1)} %get-tuple-element.303.refs_0_), channel_id=1, source_target_pairs={{0,1},{1,0},{2,3},{3,2},{4,5},{5,4},{6,7},{7,6},{8,9},{9,8},{10,11... | collective-permute-start | bytes 2359304 | tf_op jit(solution)/shard_map/ppermute | solution.py:843
  312.3 25.6 %collective-permute-start.31 = (f32[32,2560]{1,0:T(8,128)S(1)}, f32[32,2560]{1,0:T(8,128)S(1)}, u32[]{:S(2)}, u32[]{:S(2)}) collective-permute-start(f32[32,2560]{1,0:T(8,128)S(1)} %get-tuple-element.313), channel_id=1, source_target_pairs={{0,1},{1,0},{2,3},{3,2},{4,5},{5,4},{6,7},{7,6},{8,9},{9,8},{10,11... | collective-permute-start | bytes 983048 | tf_op jit(solution)/shard_map/ppermute | solution.py:843
  313.8 23.4 %collective-permute-start.30 = (f32[16,3584]{1,0:T(8,128)S(1)}, f32[16,3584]{1,0:T(8,128)S(1)}, u32[]{:S(2)}, u32[]{:S(2)}) collective-permute-start(f32[16,3584]{1,0:T(8,128)S(1)} %get-tuple-element.312), channel_id=1, source_target_pairs={{0,2},{1,3},{2,0},{3,1},{4,6},{5,7},{6,4},{7,5},{8,10},{9,11},{10,... | collective-permute-start | bytes 688136 | tf_op jit(solution)/shard_map/ppermute | solution.py:843
  339.7 18.3 %collective-permute-start.32 = (f32[16,3584]{1,0:T(8,128)S(1)}, f32[16,3584]{1,0:T(8,128)S(1)}, u32[]{:S(2)}, u32[]{:S(2)}) collective-permute-start(f32[16,3584]{1,0:T(8,128)S(1)} %get-tuple-element.316.refs_0_), channel_id=1, source_target_pairs={{0,2},{1,3},{2,0},{3,1},{4,6},{5,7},{6,4},{7,5},{8,10},{9,11},{10,... | collective-permute-start | bytes 688136 | tf_op jit(solution)/shard_map/ppermute | solution.py:843
  342.3 15.6 %collective-permute-start.33 = (f32[16,2560]{1,0:T(8,128)S(1)}, f32[16,2560]{1,0:T(8,128)S(1)}, u32[]{:S(2)}, u32[]{:S(2)}) collective-permute-start(f32[16,2560]{1,0:T(8,128)S(1)} %get-tuple-element.318), channel_id=1, source_target_pairs={{0,2},{1,3},{2,0},{3,1},{4,6},{5,7},{6,4},{7,5},{8,10},{9,11},{10,... | collective-permute-start | bytes 491528 | tf_op jit(solution)/shard_map/ppermute | solution.py:843
  358.6 15.0 %collective-permute-start.34 = (f32[32,3584]{1,0:T(8,128)S(1)}, f32[32,3584]{1,0:T(8,128)S(1)}, u32[]{:S(2)}, u32[]{:S(2)}) collective-permute-start(f32[32,3584]{1,0:T(8,128)S(1)} %get-tuple-element.320.refs_0_), channel_id=1, source_target_pairs={{0,1},{1,0},{2,3},{3,2},{4,5},{5,4},{6,7},{7,6},{8,9},{9,8},{10,11... | collective-permute-start | bytes 1376264 | tf_op jit(solution)/shard_map/ppermute | solution.py:843
  (40 other events, 211.7 us)
Sparse Core Ops, SparseCore 0:
  130.2 91.9 reduce-scatter.1

commit v6 on v5

--- a/solution.py
+++ b/solution.py
@@ -197,7 +197,7 @@
             decay_pairs[0, h] = weights.astype(BF16)
             pairs[0, h] = scores
             total += dot(scores, values * lane_mask(256, HEADP, b))
-        mixed[0, :, 256 * q : 256 * q + 256] = total
+        mixed[0, :, 256 * q : 256 * q + 256] = total.astype(BF16)
 
 
 def lift_kernel(
@@ -207,7 +207,7 @@
 ):
     steps = x1.shape[1]
     unpack_state(start, full)
-    y = (mixed[0] + dot(ce[0], full[...])) * READ_SCALE
+    y = (mixed[0].astype(F32) + dot(ce[0], full[...])) * READ_SCALE
     gate = g[0].astype(F32)
     sig = sigmoid(gate)
     active = gate * sig
@@ -236,7 +236,7 @@
     for i in range(D // 128):
         columns = slice(128 * i, 128 * i + 128)
         padded[i, :8, :] = before[0, :, columns] * keep[0, row]
-        padded[i, 8 : 8 + steps, :] = body[0, :, columns]
+        padded[i, 8 : 8 + steps, :] = body[0, :, columns].astype(F32)
         padded[i, 8 + steps :, :] = after[0, :, columns] * keep[1, row]
 
 
@@ -304,7 +304,7 @@
         ge_low = grad3.astype(BF16)
         ge[0] = ge_low
         batch_grad = dot_t(ge_low, w_conv[...]) * conv_slope
-        gbn[0] = batch_grad
+        gbn[0] = batch_grad.astype(BF16)
         accumulate(
             sums,
             jnp.concatenate(
@@ -329,11 +329,11 @@
     def kernel(gbn, dc, stats, back, bn_gain, v, before, after, keep, _, gd, taps_grad, padded):
         steps = v.shape[1]
         fill_padded(padded, v, before, after, keep)
-        grad = batch_back(gbn[0], dc[0], stats, back, bn_gain[...], count)
-        gd[0] = grad
+        grad = batch_back(gbn[0].astype(F32), dc[0], stats, back, bn_gain[...], count)
+        gd[0] = grad.astype(BF16)
         columns = []
         for at in range(0, D, 128):
-            piece = gd[0, :, at : at + 128]
+            piece = grad[:, at : at + 128]
             rows = [
                 jnp.sum(padded[at // 128, k + 1 : k + 1 + steps, :] * piece, axis=0, keepdims=True)
                 for k in range(KERNEL)
@@ -373,28 +373,36 @@
     pulled[0, 4 * STATE :, :] = block[0, 4 * STATE :, :]
 
 
-def mix_back_kernel(u, bs, c, ee, gy, start, pairs, decay_pairs, _, gu, gb, gc, full):
+def mix_back_kernel(
+    u, bs, c, ee, gy, start, pairs, decay_pairs, _,
+    gu, gb, gc,
+    full, grads_by, keys_by, reads_by, scores_rows, scores_lanes,
+):
     steps = u.shape[1]
     unpack_state(start, full)
     reads_grad = dot_t(gy[0], full[...]) * ee[0].astype(F32)
     keys_grad = jnp.zeros((steps, 256), F32)
-    keys = bs[0]
-    reads = c[0]
     for q in range(2):
         values = u[0, :, 256 * q : 256 * q + 256]
         grads = gy[0, :, 256 * q : 256 * q + 256]
-        total = jnp.zeros((steps, 256), F32)
         for b in range(4):
-            h = 4 * q + b
-            masked = grads * lane_mask(256, HEADP, b)
-            scores = (dot_t(masked, values) * decay_pairs[0, h].astype(F32)).astype(BF16)
-            mask = lane_mask(256, STATE, h)
-            reads_grad += dot(scores, keys * mask)
-            keys_grad += t_dot(scores, reads * mask)
-            total += t_dot(pairs[0, h], masked)
-        gu[0, :, 256 * q : 256 * q + 256] = total
+            here = slice(steps * b, steps * (b + 1))
+            mask = lane_mask(256, STATE, 4 * q + b)
+            grads_by[here, :] = grads * lane_mask(256, HEADP, b)
+            keys_by[here, :] = bs[0] * mask
+            reads_by[here, :] = c[0] * mask
+        for b in range(4):
+            here = slice(steps * b, steps * (b + 1))
+            scores = dot_t(grads_by[here, :], values) * decay_pairs[0, 4 * q + b].astype(F32)
+            scores = scores.astype(BF16)
+            scores_rows[here, :] = scores
+            scores_lanes[:, here] = scores
+        heads = pairs[0, 4 * q : 4 * q + 4].reshape(4 * steps, steps)
+        gu[0, :, 256 * q : 256 * q + 256] = t_dot(heads, grads_by[...]).astype(BF16)
+        reads_grad += dot(scores_lanes[...], keys_by[...])
+        keys_grad += t_dot(scores_rows[...], reads_by[...])
     gc[0] = reads_grad.astype(BF16)
-    gb[0] = keys_grad
+    gb[0] = keys_grad.astype(BF16)
 
 
 def mix_end_kernel(
@@ -403,9 +411,9 @@
     full,
 ):
     unpack_state(end, full)
-    gp[0, :, :D] = (gu[0] + dot(bt[0], full[...])).astype(BF16)
+    gp[0, :, :D] = (gu[0].astype(F32) + dot(bt[0], full[...])).astype(BF16)
     gp[0, :, D : 2 * D] = gg[0]
-    keys_grad = gb[0] + te[0].astype(F32) * dot_t(u[0], full[...])
+    keys_grad = gb[0].astype(F32) + te[0].astype(F32) * dot_t(u[0], full[...])
     gp[0, :, 2 * D : 2 * D + 256] = (keys_grad * se[0].astype(F32)).astype(BF16)
     gp[0, :, 2 * D + 256 :] = gc[0]
     back, gain = norm_back(dot_t(gp[0], w_in[...]), a2[0], r2[0], g2[...])
@@ -604,7 +612,7 @@
 
 ROOM = {'front': 44, 'mix': 24, 'lift': 28, 'depth': 20, 'late': 44, 'late_weights': 36, 'depth_grad': 20, 'conv_back': 28, 'mix_back': 28, 'mix_end': 24, 'front_back': 32, 'weights': 28}
 HOP_COST = 30e9
-TIMES = {'front': 40.0, 'mix': 14.0, 'lift': 18.0, 'depth': 12.0, 'late': 46.0, 'late_weights': 22.0, 'depth_grad': 10.0, 'conv_back': 4, 'mix_back': 24.0, 'mix_end': 20.0, 'front_back': 60, 'weights': 20.0}
+TIMES = {'front': 40.0, 'mix': 14.0, 'lift': 18.0, 'depth': 12.0, 'late': 46.0, 'late_weights': 22.0, 'depth_grad': 26.0, 'conv_back': 4, 'mix_back': 24.0, 'mix_end': 4.0, 'front_back': 60, 'weights': 20.0}
 
 
 def call(kernel, grid, ins, outs, scratch=(), flops=0, name=None):
@@ -976,7 +984,7 @@
         mix_kernel,
         (rows,),
         [row(u), row(bs), row(c), row(cum), row(cum_t)],
-        [rows_of(D), pair_shape, pair_shape],
+        [rows_of(D, BF16), pair_shape, pair_shape],
         (),
         2 * tokens * 256 * 256 * 16,
         "mix",
@@ -1013,7 +1021,7 @@
         ],
         [
             rows_of(D, BF16), rows_of(D, BF16), rows_of(D, BF16), rows_of(FF, BF16), rows_of(D, BF16),
-            rows_of(FF, BF16), rows_of(D, BF16), rows_of(D), rows_of(D), two_lines, line, line,
+            rows_of(FF, BF16), rows_of(D, BF16), rows_of(D), rows_of(D, BF16), two_lines, line, line,
         ],
         [pltpu.VMEM((steps, FF), BF16)],
         2 * tokens * D * (4 * FF + 2 * D),
@@ -1046,7 +1054,7 @@
 
     def edge_grad(at):
         return batch_back(
-            lax.slice_in_dim(gbn, at, at + 8, axis=1),
+            lax.slice_in_dim(gbn, at, at + 8, axis=1).astype(F32),
             lax.slice_in_dim(dc, at, at + 8, axis=1),
             stats, back, bn_gain, count,
         )
@@ -1059,7 +1067,7 @@
             row(gbn), row(dc), every(stats), every(back), bg, row(v), row(v_before), row(v_after), keep,
             (late_token, anywhere()),
         ],
-        [rows_of(D), ((16, D), F32, "all")],
+        [rows_of(D, BF16), ((16, D), F32, "all")],
         [padded],
         2 * tokens * D * 64,
         "depth_grad",
@@ -1105,8 +1113,8 @@
                 row(u), row(bs), row(c), row(ee), row(gy), row(start), row(pairs), row(decay_pairs),
                 (token, anywhere()),
             ],
-            [rows_of(D), rows_of(256), rows_of(256, BF16)],
-            [full],
+            [rows_of(D, BF16), rows_of(256, BF16), rows_of(256, BF16)],
+            [full] + [pltpu.VMEM((4 * steps, 256), BF16)] * 4 + [pltpu.VMEM((steps, 4 * steps), BF16)],
             2 * tokens * 256 * 256 * 32,
             "mix_back",
         )
@@ -1115,21 +1123,21 @@
 
     end = entering(pulled, True, keep[0], beside)
     gu, gb, gc, mixed_token = found["mixed"]
-    token = together(bits, [early], [mixed_token])
     gp, gx1, gf1, ln2, end_token = call(
         mix_end_kernel,
         (rows,),
         [
             row(end), row(u), row(bt), row(te), row(se), row(gu), row(gb), row(gc), row(gg),
-            every(ssm_in), row(a2), row(r2), g2, row(gx2), (token, anywhere()),
+            every(ssm_in), row(a2), row(r2), g2, row(gx2), (mixed_token, anywhere()),
         ],
         [rows_of(PROJ, BF16), rows_of(D), rows_of(D, BF16), line],
         [full],
         2 * tokens * D * PROJ,
         "mix_end",
     )
+    token = together(bits, [early], [end_token])
     kept, sent, weights_token = weight_sums(
-        [(flatten(a2), flatten(gp)), (flatten(s1), flatten(gf1))], share, core, None, [end_token]
+        [(flatten(a2), flatten(gp)), (flatten(s1), flatten(gf1))], share, core, None, [token]
     )
     middle = Sum([(0, PROJ, False), (PROJ, FF, True)])
     middle.begin(kept, sent, (PROJ + FF) // 2)

time: 397 us -> 397 us (level)
  Pallas kernels: 176 us -> 172 us
    ppermute x27, waiting for transfers between devices: 95.5 us -> 87.9 us  [swap(): return lax.ppermute(value, axis, flip_pairs(lax.axis_size(axis), 1 << bit))]
    reduce_scatter x1, waiting for transfers between devices: 0.02 us -> 6.74 us  [scatter_sum(): return lax.psum_scatter(value, 'seq', scatter_dimension=0, tiled=True)]
    pallas_call x14, Pallas kernels: 156 us -> 152 us  [call(): pl.pallas_call(with_token, grid=grid, in_specs=[held_spec(a.shape) if kin...]
    unnamed x51 -> x53, local copies, waits for them, and re-layouts: 10.9 us -> 12.3 us
where the time goes in v6:
time: 397 us; the launch traced here: 395 us
  Pallas kernels  172 us (43%)
  waiting for transfers between devices  115 us (29%)
  starting transfers between devices  58.6 us (15%)
  local copies, waits for them, and re-layouts  17.1 us (4%)
  blocking collectives  15.6 us (4%)
  between operations  14.5 us (4%)
    pallas_call x14, Pallas kernels, call(): pl.pallas_call(with_token, grid=grid, in_specs=[held_spec(a.shape) if kin...  152 us
    ppermute x27, waiting for transfers between devices, swap(): return lax.ppermute(value, axis, flip_pairs(lax.axis_size(axis), 1 << bit))  87.9 us
    ppermute x27, starting transfers between devices, swap(): return lax.ppermute(value, axis, flip_pairs(lax.axis_size(axis), 1 << bit))  38 us
    ppermute x6, waiting for transfers between devices, entering(): other = lax.ppermute(value, 'seq', flip_pairs(count, 1 << bit))  17.3 us
    all_to_all x1, blocking collectives, sum_over_all(): return jnp.sum(lax.all_to_all(copies, ('rec', 'seq'), 0, 0), axis=0)  15.6 us
    pallas_call x13, Pallas kernels, in_vmem(): pl.pallas_call(kernel, in_specs=[scalars()] + [vmem] * len(ins) + [anywhe...  13.6 us
    unnamed x53, local copies, waits for them, and re-layouts  12.3 us
    ppermute x6, starting transfers between devices, entering(): other = lax.ppermute(value, 'seq', flip_pairs(count, 1 << bit))  11.9 us
  transfers between devices with their start and end apart: 39, of which 20 were waited for; matrix products, arithmetic and copies ran while one was open for 1% of the time, Pallas kernels for 27%

profile of v6, /device:TPU:0, one launch (start us, length us, event | category | flops | bytes accessed | tf_op | source)
XLA Modules:
  0.0 395.2 jit_solution(5089646550068748676)
XLA Ops:
  8.2 20.0 %front.1 = (bf16[4,256,512]{2,1,0:T(8,128)(2,1)}, f32[4,256,512]{2,1,0:T(8,128)}, bf16[4,256,512]{2,1,0:T(8,128)(2,1)}, f32[4,256,1]{2,1,0:T(8,128)}, bf16[4,256...) custom-call(bf16[4,80,1024]{2,1,0:T(8,128)(2,1)} %bitcast.59, ...), custom_call_target="tpu_custom_call" | custom-call | flops 46000001024 | tf_op jit(solution)/shard_map/front/pallas_call | solution.py:636
  35.1 7.0 %collective-permute-done.1.other = f32[4,136,128]{2,1,0:T(8,128)S(1)} collective-permute-done((f32[4,136,128]{2,1,0:T(8,128)S(1)}, f32[4,136,128]{2,1,0:T(8,128)S(1)}, u32[]{:S(2)}, u32[]{:S(2)}) %collective-permute-start.1) | collective-permute-done | bytes 278560 | tf_op jit(solution)/shard_map/ppermute | solution.py:699
  45.0 7.1 %mix.1 = (bf16[4,256,512]{2,1,0:T(8,128)(2,1)}, bf16[4,8,256,256]{3,2,1,0:T(8,128)(2,1)}, bf16[4,8,256,256]{3,2,1,0:T(8,128)(2,1)}, f32[8,128]{1,0:T(8,128)}) custom-call(bf16[4,256,512]{2,1,0:T(8,128)(2,1)} %get-tuple-element.177.refs_0_.refs_1_, bf16[4,256,256]{2,1,0:T(8,128)(2,1)} %get-tuple-element.178.refs_1_, ...), custom_call_target="tpu_custom_call" | custom-call | flops 16099999744 | tf_op jit(solution)/shard_map/mix/pallas_call | solution.py:636
  54.1 8.7 %lift.1 = (bf16[4,256,512]{2,1,0:T(8,128)(2,1)}, bf16[4,256,512]{2,1,0:T(8,128)(2,1)}, bf16[4,256,512]{2,1,0:T(8,128)(2,1)}, f32[4,256,512]{2,1,0:T(8,128)}, bf1...) custom-call(bf16[4,256,512]{2,1,0:T(8,128)(2,1)} %get-tuple-element., ...), custom_call_target="tpu_custom_call" | custom-call | flops 20700000256 | tf_op jit(solution)/shard_map/lift/pallas_call | solution.py:636
  76.1 15.6 %all_to_all.10 = f32[32,2,512]{2,1,0:T(2,128)S(1)} all-to-all(f32[32,2,512]{2,1,0:T(2,128)S(1)} %broadcast_in_dim.9), channel_id=1, replica_groups=mesh['seq'=8,'rec'=4] {'rec','seq'}, dimensions={0} | all-to-all | bytes 262144 | tf_op jit(solution)/shard_map/all_to_all | solution.py:730
  92.4 21.9 %late.1 = (bf16[4,256,512]{2,1,0:T(8,128)(2,1)}, bf16[4,256,512]{2,1,0:T(8,128)(2,1)}, bf16[4,256,512]{2,1,0:T(8,128)(2,1)}, bf16[4,256,2048]{2,1,0:T(8,128)(2,1...) custom-call(f32[4,256,512]{2,1,0:T(8,128)} %get-tuple-element.195.re, ...), custom_call_target="tpu_custom_call" | custom-call | flops 52899999744 | tf_op jit(solution)/shard_map/late/pallas_call | solution.py:636
  118.3 11.4 %late_weights.1 = (f32[512,4608]{1,0:T(8,128)}, f32[8,128]{1,0:T(8,128)}) custom-call(bf16[1024,512]{1,0:T(8,128)(2,1)} %bitcast.87, bf16[1024,512]{1,0:T(8,128)(2,1)} %bitcast.86, bf16[1024,2048]{1,0:T(8,128)(2,1)} %bitcast.73, bf16[1024,2048]{1,0:T(8,128)(2,1)} %bitcast.74, bf16[1024,512]{1,0:T(8,128)(2,1)} %bitcast.89, bf16[1024,512]{1,0:T(8,128)(2,1)} %bitcast.88), custom_call_target="tpu_custom_call" | custom-call | flops 25300000768 | tf_op jit(solution)/shard_map/late_weights/pallas_call | solution.py:636
  134.9 6.8 %depth_grad.1 = (bf16[4,256,512]{2,1,0:T(8,128)(2,1)}, f32[16,512]{1,0:T(8,128)}, f32[8,128]{1,0:T(8,128)}) custom-call(bf16[4,256,512]{2,1,0:T(8,128)(2,1)} %get-tuple-element.199.refs_0_, f32[4,256,512]{2,1,0:T(8,128)} %get-tuple-element.195.refs_0_.refs_1_, f32[2,512]{1,0:T(2,128)} %reduce_sum.18.refs_3_.refs_2_, f32[2,512]{1,0:T(2,128)} %copy-done.18, ...), custom_call_target="tpu_custom_call" | custom-call | flops 29899999232 | tf_op jit(solution)/shard_map/depth_grad/pallas_call | solution.py:636
  142.4 12.6 %conv_back.1 = (bf16[4,256,1024]{2,1,0:T(8,128)(2,1)}, f32[4,256,512]{2,1,0:T(8,128)}, bf16[4,256,512]{2,1,0:T(8,128)(2,1)}, bf16[4,256,512]{2,1,0:T(8,128)(2,1)...) custom-call(bf16[4,256,512]{2,1,0:T(8,128)(2,1)} %get-tuple-element.208.refs_0_, ...), custom_call_target="tpu_custom_call" | custom-call | flops 4600000000 | tf_op jit(solution)/shard_map/conv_back/pallas_call | solution.py:636
  161.8 6.3 %weights.3 = (f32[256,1536]{1,0:T(8,128)}, f32[256,1536]{1,0:T(8,128)}, f32[8,128]{1,0:T(8,128)}) custom-call(s32[1]{0:T(128)} %bitcast.26.refs_0_, bf16[1024,512]{1,0:T(8,128)(2,1)} %bitcast.82, bf16[1024,512]{1,0:T(8,128)(2,1)} %bitcast.81, bf16[1024,1024]{1,0:T(8,128)(2,1)} %bitcast.76, bf16[1024,512]{1,0:T(8,128)(2,1)} %bitcast.84, ...), custom_call_target="tpu_custom_call" | custom-call | flops 23000000512 | tf_op jit(solution)/shard_map/weights/pallas_call | solution.py:636
  168.2 7.0 %collective-permute-done.8.other = f32[4,136,128]{2,1,0:T(8,128)S(1)} collective-permute-done((f32[4,136,128]{2,1,0:T(8,128)S(1)}, f32[4,136,128]{2,1,0:T(8,128)S(1)}, u32[]{:S(2)}, u32[]{:S(2)}) %collective-permute-start.8) | collective-permute-done | bytes 278560 | tf_op jit(solution)/shard_map/ppermute | solution.py:699
  180.7 9.4 %mix_back.1 = (bf16[4,256,512]{2,1,0:T(8,128)(2,1)}, bf16[4,256,256]{2,1,0:T(8,128)(2,1)}, bf16[4,256,256]{2,1,0:T(8,128)(2,1)}, f32[8,128]{1,0:T(8,128)}) custom-call(bf16[4,256,512]{2,1,0:T(8,128)(2,1)} %get-tuple-element.177.refs_0_.refs_1_, bf16[4,256,256]{2,1,0:T(8,128)(2,1)} %get-tuple-element.178.refs_1_, ...), custom_call_target="tpu_custom_call" | custom-call | flops 27599998976 | tf_op jit(solution)/shard_map/mix_back/pallas_call | solution.py:636
  194.2 9.3 %mix_end.1 = (bf16[4,256,1536]{2,1,0:T(8,128)(2,1)}, f32[4,256,512]{2,1,0:T(8,128)}, bf16[4,256,512]{2,1,0:T(8,128)(2,1)}, f32[1,512]{1,0:T(1,128)}, f32[8,128]{1,0:T(8,128)}) custom-call(f32[4,136,128]{2,1,0:T(8,128)} %copy-done.13, bf16[4,256,512]{2,1,0:T(8,128)(2,1)} %get-tuple-element.177.refs_0_.refs_1_, ...), custom_call_target="tpu_custom_call" | custom-call | flops 4600000000 | tf_op jit(solution)/shard_map/mix_end/pallas_call | solution.py:636
  207.2 11.4 %weights.4 = (f32[256,3584]{1,0:T(8,128)}, f32[256,3584]{1,0:T(8,128)}, f32[8,128]{1,0:T(8,128)}) custom-call(s32[1]{0:T(128)} %bitcast.26.refs_0_, bf16[1024,512]{1,0:T(8,128)(2,1)} %bitcast.80, bf16[1024,2048]{1,0:T(8,128)(2,1)} %bitcast.71, bf16[1024,1536]{1,0:T(8,128)(2,1)} %bitcast.75, bf16[1024,512]{1,0:T(8,128)(2,1)} %bitcast.83, ...), custom_call_target="tpu_custom_call" | custom-call | flops 23000000512 | tf_op jit(solution)/shard_map/weights/pallas_call | solution.py:636
  218.6 6.7 %reduce-scatter.2.cloned.1.call-done.refs_0_ = f32[64,4608]{1,0:T(8,128)} async-done(((f32[512,4608]{1,0:T(8,128)}), f32[64,4608]{1,0:T(8,128)}) %reduce-scatter.2.cloned.1.call-update) | async-done | bytes 1179664 | tf_op jit(solution)/shard_map/reduce_scatter | solution.py:734
  229.7 12.6 %front_back.1 = (bf16[4,256,2048]{2,1,0:T(8,128)(2,1)}, bf16[4,256,512]{2,1,0:T(8,128)(2,1)}, f32[4,80,1024]{2,1,0:T(8,128)}, f32[1,512]{1,0:T(1,128)}, f32[8,128]{1,0:T(8,128)}) custom-call(f32[4,256,512]{2,1,0:T(8,128)} %get-tuple-element.246.refs_0_, bf16[4,256,512]{2,1,0:T(8,128)(2,1)} %get-tuple-element.247.refs_1_, bf16[2048,512]{1,0:T(8,128)(2,1)} %refs_2_.5, ...), custom_call_target="tpu_custom_call" | custom-call | flops 69000003584 | tf_op jit(solution)/shard_map/front_back/pallas_call | solution.py:636
  251.1 9.0 %weights.5 = (f32[256,2560]{1,0:T(8,128)}, f32[256,2560]{1,0:T(8,128)}, f32[8,128]{1,0:T(8,128)}) custom-call(s32[1]{0:T(128)} %bitcast.26.refs_0_, bf16[1024,512]{1,0:T(8,128)(2,1)} %bitcast.79, bf16[1024,512]{1,0:T(8,128)(2,1)} %bitcast.85, bf16[1024,2048]{1,0:T(8,128)(2,1)} %bitcast.72, bf16[1024,512]{1,0:T(8,128)(2,1)} %bitcast.78, ...), custom_call_target="tpu_custom_call" | custom-call | flops 23000000512 | tf_op jit(solution)/shard_map/weights/pallas_call | solution.py:636
  260.1 7.3 %collective-permute-done.18.refs_2_ = f32[128,1792]{1,0:T(8,128)S(1)} collective-permute-done((f32[128,1792]{1,0:T(8,128)S(1)}, f32[128,1792]{1,0:T(8,128)S(1)}, u32[]{:S(2)}, u32[]{:S(2)}) %collective-permute-start.18) | collective-permute-done | bytes 917536 | tf_op jit(solution)/shard_map/ppermute | solution.py:851
  278.0 16.3 %collective-permute-done.20.refs_1_ = f32[16,6144]{1,0:T(8,128)S(1)} collective-permute-done((f32[16,6144]{1,0:T(8,128)S(1)}, f32[16,6144]{1,0:T(8,128)S(1)}, u32[]{:S(2)}, u32[]{:S(2)}) %collective-permute-start.20) | collective-permute-done | bytes 393248 | tf_op jit(solution)/shard_map/ppermute | solution.py:851
  313.9 5.8 %collective-permute-start.30 = (f32[16,3584]{1,0:T(8,128)S(1)}, f32[16,3584]{1,0:T(8,128)S(1)}, u32[]{:S(2)}, u32[]{:S(2)}) collective-permute-start(f32[16,3584]{1,0:T(8,128)S(1)} %get-tuple-element.312), channel_id=1, source_target_pairs={{0,2},{1,3},{2,0},{3,1},{4,6},{5,7},{6,4},{7,5},{8,10},{9,11},{10,... | collective-permute-start | bytes 688136 | tf_op jit(solution)/shard_map/ppermute | solution.py:851
  319.7 17.1 %collective-permute-done.30.refs_3_ = f32[16,3584]{1,0:T(8,128)S(1)} collective-permute-done((f32[16,3584]{1,0:T(8,128)S(1)}, f32[16,3584]{1,0:T(8,128)S(1)}, u32[]{:S(2)}, u32[]{:S(2)}) %collective-permute-start.30) | collective-permute-done | bytes 229408 | tf_op jit(solution)/shard_map/ppermute | solution.py:851
  343.1 14.8 %collective-permute-done.33.refs_3_ = f32[16,2560]{1,0:T(8,128)S(1)} collective-permute-done((f32[16,2560]{1,0:T(8,128)S(1)}, f32[16,2560]{1,0:T(8,128)S(1)}, u32[]{:S(2)}, u32[]{:S(2)}) %collective-permute-start.33) | collective-permute-done | bytes 163872 | tf_op jit(solution)/shard_map/ppermute | solution.py:851
  362.3 10.1 %collective-permute-done.35.refs_3_ = f32[16,2560]{1,0:T(8,128)S(1)} collective-permute-done((f32[16,2560]{1,0:T(8,128)S(1)}, f32[16,2560]{1,0:T(8,128)S(1)}, u32[]{:S(2)}, u32[]{:S(2)}) %collective-permute-start.35) | collective-permute-done | bytes 163872 | tf_op jit(solution)/shard_map/ppermute | solution.py:851
  379.3 6.2 %collective-permute-done.36.refs_1_ = f32[32,2560]{1,0:T(8,128)S(1)} collective-permute-done((f32[32,2560]{1,0:T(8,128)S(1)}, f32[32,2560]{1,0:T(8,128)S(1)}, u32[]{:S(2)}, u32[]{:S(2)}) %collective-permute-start.36) | collective-permute-done | bytes 327712 | tf_op jit(solution)/shard_map/ppermute | solution.py:851
  (155 shorter events, 120.4 us)
Async XLA Ops:
  115.6 14.7 %all-to-all-start.1 = ((f32[32,2,512]{2,1,0:T(2,128)}), f32[32,2,512]{2,1,0:T(2,128)S(1)}, u32[]{:S(2)}, u32[]{:S(2)}) async-start(f32[32,2,512]{2,1,0:T(2,128)} %broadcast_in_dim.10), calls=%async_computation.1 | async-start | bytes 262144 | tf_op jit(solution)/shard_map/all_to_all | solution.py:730
  118.2 107.1 %reduce-scatter.2.cloned.1.call-start = ((), (), s32[]{:S(2)}) async-start(), calls=%async_computation.3 | async-start | bytes 10616832 | tf_op jit(solution)/shard_map/reduce_scatter | solution.py:734
  159.8 15.3 %collective-permute-start.8 = (f32[4,136,128]{2,1,0:T(8,128)S(1)}, f32[4,136,128]{2,1,0:T(8,128)S(1)}, u32[]{:S(2)}, u32[]{:S(2)}) collective-permute-start(f32[4,136,128]{2,1,0:T(8,128)S(1)} %get-tuple-element.217.value), channel_id=1, source_target_pairs={{0,8},{4,12},{8,0},{12,4},{16,24},{20,28},{24,16},{28,20},{1,9},{5... | collective-permute-start | bytes 835592 | tf_op jit(solution)/shard_map/ppermute | solution.py:699
  175.8 15.0 %collective-permute-start.9 = (f32[4,136,128]{2,1,0:T(8,128)S(1)}, f32[4,136,128]{2,1,0:T(8,128)S(1)}, u32[]{:S(2)}, u32[]{:S(2)}) collective-permute-start(f32[4,136,128]{2,1,0:T(8,128)S(1)} %get-tuple-element.219.value), channel_id=1, source_target_pairs={{0,16},{4,20},{8,24},{12,28},{16,0},{20,4},{24,8},{28,12},{1,17},{... | collective-permute-start | bytes 835592 | tf_op jit(solution)/shard_map/ppermute | solution.py:699
  179.4 24.1 %collective-permute-start.11 = (f32[128,768]{1,0:T(8,128)S(1)}, f32[128,768]{1,0:T(8,128)S(1)}, u32[]{:S(2)}, u32[]{:S(2)}) collective-permute-start(f32[128,768]{1,0:T(8,128)S(1)} %get-tuple-element.252), channel_id=1, source_target_pairs={{0,8},{4,12},{8,0},{12,4},{16,24},{20,28},{24,16},{28,20},{1,9},{5... | collective-permute-start | bytes 1179656 | tf_op jit(solution)/shard_map/ppermute | solution.py:851
  180.0 23.5 %collective-permute-start.12 = (f32[128,768]{1,0:T(8,128)S(1)}, f32[128,768]{1,0:T(8,128)S(1)}, u32[]{:S(2)}, u32[]{:S(2)}) collective-permute-start(f32[128,768]{1,0:T(8,128)S(1)} %get-tuple-element.254), channel_id=1, source_target_pairs={{0,16},{4,20},{8,24},{12,28},{16,0},{20,4},{24,8},{28,12},{1,17},{... | collective-permute-start | bytes 1179656 | tf_op jit(solution)/shard_map/ppermute | solution.py:851
  204.8 13.7 %collective-permute-start.13 = (f32[64,768]{1,0:T(8,128)S(1)}, f32[64,768]{1,0:T(8,128)S(1)}, u32[]{:S(2)}, u32[]{:S(2)}) collective-permute-start(f32[64,768]{1,0:T(8,128)S(1)} %get-tuple-element.257), channel_id=1, source_target_pairs={{0,16},{4,20},{8,24},{12,28},{16,0},{20,4},{24,8},{28,12},{1,17},{... | collective-permute-start | bytes 589832 | tf_op jit(solution)/shard_map/ppermute | solution.py:851
  218.5 23.7 %collective-permute-start.16 = (f32[256,3584]{1,0:T(8,128)}, f32[256,3584]{1,0:T(8,128)}, u32[]{:S(2)}, u32[]{:S(2)}) collective-permute-start(f32[256,3584]{1,0:T(8,128)} %get-tuple-element.269), channel_id=1, source_target_pairs={{0,4},{4,0},{8,12},{12,8},{16,20},{20,16},{24,28},{28,24},{1,5},{5... | collective-permute-start | bytes 11010056 | tf_op jit(solution)/shard_map/ppermute | solution.py:851
  227.9 20.1 %collective-permute-start.15 = (f32[32,6144]{1,0:T(8,128)S(1)}, f32[32,6144]{1,0:T(8,128)S(1)}, u32[]{:S(2)}, u32[]{:S(2)}) collective-permute-start(f32[32,6144]{1,0:T(8,128)S(1)} %get-tuple-element.267), channel_id=1, source_target_pairs={{0,1},{1,0},{2,3},{3,2},{4,5},{5,4},{6,7},{7,6},{8,9},{9,8},{10,11... | collective-permute-start | bytes 2359304 | tf_op jit(solution)/shard_map/ppermute | solution.py:851
  245.4 22.0 %collective-permute-start.18 = (f32[128,1792]{1,0:T(8,128)S(1)}, f32[128,1792]{1,0:T(8,128)S(1)}, u32[]{:S(2)}, u32[]{:S(2)}) collective-permute-start(f32[128,1792]{1,0:T(8,128)S(1)} %get-tuple-element.275), channel_id=1, source_target_pairs={{0,8},{4,12},{8,0},{12,4},{16,24},{20,28},{24,16},{28,20},{1,9},{5... | collective-permute-start | bytes 2752520 | tf_op jit(solution)/shard_map/ppermute | solution.py:851
  246.5 21.7 %collective-permute-start.19 = (f32[128,1792]{1,0:T(8,128)S(1)}, f32[128,1792]{1,0:T(8,128)S(1)}, u32[]{:S(2)}, u32[]{:S(2)}) collective-permute-start(f32[128,1792]{1,0:T(8,128)S(1)} %get-tuple-element.277), channel_id=1, source_target_pairs={{0,16},{4,20},{8,24},{12,28},{16,0},{20,4},{24,8},{28,12},{1,17},{... | collective-permute-start | bytes 2752520 | tf_op jit(solution)/shard_map/ppermute | solution.py:851
  248.7 19.6 %collective-permute-start.17 = (f32[16,6144]{1,0:T(8,128)S(1)}, f32[16,6144]{1,0:T(8,128)S(1)}, u32[]{:S(2)}, u32[]{:S(2)}) collective-permute-start(f32[16,6144]{1,0:T(8,128)S(1)} %get-tuple-element.274), channel_id=1, source_target_pairs={{0,2},{1,3},{2,0},{3,1},{4,6},{5,7},{6,4},{7,5},{8,10},{9,11},{10,... | collective-permute-start | bytes 1179656 | tf_op jit(solution)/shard_map/ppermute | solution.py:851
  271.5 26.4 %collective-permute-start.24 = (f32[128,1280]{1,0:T(8,128)S(1)}, f32[128,1280]{1,0:T(8,128)S(1)}, u32[]{:S(2)}, u32[]{:S(2)}) collective-permute-start(f32[128,1280]{1,0:T(8,128)S(1)} %get-tuple-element.298), channel_id=1, source_target_pairs={{0,8},{4,12},{8,0},{12,4},{16,24},{20,28},{24,16},{28,20},{1,9},{5... | collective-permute-start | bytes 1966088 | tf_op jit(solution)/shard_map/ppermute | solution.py:851
  272.5 25.4 %collective-permute-start.25 = (f32[128,1280]{1,0:T(8,128)S(1)}, f32[128,1280]{1,0:T(8,128)S(1)}, u32[]{:S(2)}, u32[]{:S(2)}) collective-permute-start(f32[128,1280]{1,0:T(8,128)S(1)} %get-tuple-element.300), channel_id=1, source_target_pairs={{0,16},{4,20},{8,24},{12,28},{16,0},{20,4},{24,8},{28,12},{1,17},{... | collective-permute-start | bytes 1966088 | tf_op jit(solution)/shard_map/ppermute | solution.py:851
  274.0 23.9 %collective-permute-start.21 = (f32[64,1792]{1,0:T(8,128)S(1)}, f32[64,1792]{1,0:T(8,128)S(1)}, u32[]{:S(2)}, u32[]{:S(2)}) collective-permute-start(f32[64,1792]{1,0:T(8,128)S(1)} %get-tuple-element.291), channel_id=1, source_target_pairs={{0,16},{4,20},{8,24},{12,28},{16,0},{20,4},{24,8},{28,12},{1,17},{... | collective-permute-start | bytes 1376264 | tf_op jit(solution)/shard_map/ppermute | solution.py:851
  274.5 23.4 %collective-permute-start.22 = (f32[64,1792]{1,0:T(8,128)S(1)}, f32[64,1792]{1,0:T(8,128)S(1)}, u32[]{:S(2)}, u32[]{:S(2)}) collective-permute-start(f32[64,1792]{1,0:T(8,128)S(1)} %get-tuple-element.293), channel_id=1, source_target_pairs={{0,8},{4,12},{8,0},{12,4},{16,24},{20,28},{24,16},{28,20},{1,9},{5... | collective-permute-start | bytes 1376264 | tf_op jit(solution)/shard_map/ppermute | solution.py:851
  275.6 18.7 %collective-permute-start.20 = (f32[16,6144]{1,0:T(8,128)S(1)}, f32[16,6144]{1,0:T(8,128)S(1)}, u32[]{:S(2)}, u32[]{:S(2)}) collective-permute-start(f32[16,6144]{1,0:T(8,128)S(1)} %get-tuple-element.290.refs_0_), channel_id=1, source_target_pairs={{0,2},{1,3},{2,0},{3,1},{4,6},{5,7},{6,4},{7,5},{8,10},{9,11},{10,... | collective-permute-start | bytes 1179656 | tf_op jit(solution)/shard_map/ppermute | solution.py:851
  298.8 13.5 %collective-permute-start.27 = (f32[32,3584]{1,0:T(8,128)S(1)}, f32[32,3584]{1,0:T(8,128)S(1)}, u32[]{:S(2)}, u32[]{:S(2)}) collective-permute-start(f32[32,3584]{1,0:T(8,128)S(1)} %get-tuple-element.304), channel_id=1, source_target_pairs={{0,1},{1,0},{2,3},{3,2},{4,5},{5,4},{6,7},{7,6},{8,9},{9,8},{10,11... | collective-permute-start | bytes 1376264 | tf_op jit(solution)/shard_map/ppermute | solution.py:851
  299.7 38.7 %collective-permute-start.26 = (f32[32,6144]{1,0:T(8,128)S(1)}, f32[32,6144]{1,0:T(8,128)S(1)}, u32[]{:S(2)}, u32[]{:S(2)}) collective-permute-start(f32[32,6144]{1,0:T(8,128)S(1)} %get-tuple-element.303.refs_0_), channel_id=1, source_target_pairs={{0,1},{1,0},{2,3},{3,2},{4,5},{5,4},{6,7},{7,6},{8,9},{9,8},{10,11... | collective-permute-start | bytes 2359304 | tf_op jit(solution)/shard_map/ppermute | solution.py:851
  313.0 25.4 %collective-permute-start.31 = (f32[32,2560]{1,0:T(8,128)S(1)}, f32[32,2560]{1,0:T(8,128)S(1)}, u32[]{:S(2)}, u32[]{:S(2)}) collective-permute-start(f32[32,2560]{1,0:T(8,128)S(1)} %get-tuple-element.313), channel_id=1, source_target_pairs={{0,1},{1,0},{2,3},{3,2},{4,5},{5,4},{6,7},{7,6},{8,9},{9,8},{10,11... | collective-permute-start | bytes 983048 | tf_op jit(solution)/shard_map/ppermute | solution.py:851
  313.9 22.9 %collective-permute-start.30 = (f32[16,3584]{1,0:T(8,128)S(1)}, f32[16,3584]{1,0:T(8,128)S(1)}, u32[]{:S(2)}, u32[]{:S(2)}) collective-permute-start(f32[16,3584]{1,0:T(8,128)S(1)} %get-tuple-element.312), channel_id=1, source_target_pairs={{0,2},{1,3},{2,0},{3,1},{4,6},{5,7},{6,4},{7,5},{8,10},{9,11},{10,... | collective-permute-start | bytes 688136 | tf_op jit(solution)/shard_map/ppermute | solution.py:851
  340.2 17.7 %collective-permute-start.32 = (f32[16,3584]{1,0:T(8,128)S(1)}, f32[16,3584]{1,0:T(8,128)S(1)}, u32[]{:S(2)}, u32[]{:S(2)}) collective-permute-start(f32[16,3584]{1,0:T(8,128)S(1)} %get-tuple-element.316.refs_0_), channel_id=1, source_target_pairs={{0,2},{1,3},{2,0},{3,1},{4,6},{5,7},{6,4},{7,5},{8,10},{9,11},{10,... | collective-permute-start | bytes 688136 | tf_op jit(solution)/shard_map/ppermute | solution.py:851
  342.2 15.7 %collective-permute-start.33 = (f32[16,2560]{1,0:T(8,128)S(1)}, f32[16,2560]{1,0:T(8,128)S(1)}, u32[]{:S(2)}, u32[]{:S(2)}) collective-permute-start(f32[16,2560]{1,0:T(8,128)S(1)} %get-tuple-element.318), channel_id=1, source_target_pairs={{0,2},{1,3},{2,0},{3,1},{4,6},{5,7},{6,4},{7,5},{8,10},{9,11},{10,... | collective-permute-start | bytes 491528 | tf_op jit(solution)/shard_map/ppermute | solution.py:851
  358.5 14.7 %collective-permute-start.34 = (f32[32,3584]{1,0:T(8,128)S(1)}, f32[32,3584]{1,0:T(8,128)S(1)}, u32[]{:S(2)}, u32[]{:S(2)}) collective-permute-start(f32[32,3584]{1,0:T(8,128)S(1)} %get-tuple-element.320.refs_0_), channel_id=1, source_target_pairs={{0,1},{1,0},{2,3},{3,2},{4,5},{5,4},{6,7},{7,6},{8,9},{9,8},{10,11... | collective-permute-start | bytes 1376264 | tf_op jit(solution)/shard_map/ppermute | solution.py:851
  (41 other events, 203.0 us)
Sparse Core Ops, SparseCore 0:
  129.8 95.4 reduce-scatter.1

commit v7 on v6

--- a/solution.py
+++ b/solution.py
@@ -457,13 +457,12 @@
 
 
 def late_weights_kernel(share):
-    def kernel(a4, e, s4, gh, ge, gf, out):
+    def kernel(a4, s4, gh, gf, out):
         left = a4[...].T
         for at in range(0, FF, D):
             out[:, at : at + D] = dot(left, gh[:, at : at + D])
         for at in range(0, 1024, 256):
             by_share_store(out, FF, share, at, dot(s4[:, at : at + 256].T, gf[...]))
-        out[:, 2 * FF :] = dot(e[...].T, ge[...])
 
     return kernel
 
@@ -1042,12 +1041,11 @@
         late_weights_kernel(share),
         (2,),
         [
-            column_block(a4, 256), column_block(e, 256), column_block(s4, 1024),
-            every(flatten(gh4)), every(flatten(ge)), every(flatten(gf4)),
+            column_block(a4, 256), column_block(s4, 1024), every(flatten(gh4)), every(flatten(gf4)),
         ],
-        [row_block(2 * FF + D)],
+        [row_block(2 * FF)],
         (),
-        2 * tokens * D * (2 * FF + D),
+        2 * tokens * D * 2 * FF,
         "late_weights",
     )
     scattered_a = scatter_sum(late_grads)
@@ -1094,7 +1092,7 @@
     )
     early = Sum(
         [
-            (0, FF, False), (FF, FF, True), (2 * FF, D, False), (2 * FF + D, 2 * D, False),
+            (0, FF, False), (FF, FF, True), (2 * FF, 2 * D, False), (2 * FF + 2 * D, D, False),
             (2 * FF + 3 * D, D, False),
         ],
     )
@@ -1102,9 +1100,9 @@
 
     def beside(hops):
         kept, sent, weights_token = weight_sums(
-            [(flatten(a3), flatten(gq)), (flatten(z), flatten(gz))], share, core, None, hops[-2:-1]
+            [(flatten(a3), flatten(gq)), (flatten(z), flatten(gz)), (flatten(e), flatten(ge))], share, core, None, hops[-2:-1]
         )
-        early.begin(kept, sent, 3 * D // 2)
+        early.begin(kept, sent, 2 * D)
         token = together(bits, [early], [weights_token, hops[-1]])
         gu, gb, gc, mixed_token = call(
             mix_back_kernel,
@@ -1174,7 +1172,7 @@
         now = [one for one in now if one.steps]
         if now:
             token = together(bits, now, [token])
-    ffn2_in_grad, ffn2_out_grad, conv_out_grad, conv_in_grad, ssm_out_grad = early.done
+    ffn2_in_grad, ffn2_out_grad, conv_in_grad, ssm_out_grad, conv_out_grad = early.done
     ssm_in_grad, ffn1_out_grad = middle.done
     ffn1_in_grad, w_sub_grad, gains = last.done
 

time: 397 us -> 390 us (0.982)
  waiting for transfers between devices: 115 us -> 110 us
    reduce_scatter x1, waiting for transfers between devices: 6.74 us -> 0.29 us  [scatter_sum(): return lax.psum_scatter(value, 'seq', scatter_dimension=0, tiled=True)]
  transfers between devices with their start and end apart: 39 -> 39, of which waited for: 20 -> 21; matrix products, arithmetic and copies ran while one was open for 1% -> 1% of each run, Pallas kernels for 27% -> 27%
where the time goes in v7:
time: 390 us; the launch traced here: 389 us
  Pallas kernels  172 us (44%)
  waiting for transfers between devices  110 us (28%)
  starting transfers between devices  56.6 us (15%)
  local copies, waits for them, and re-layouts  17 us (4%)
  blocking collectives  15.6 us (4%)
  between operations  14.5 us (4%)
    pallas_call x14, Pallas kernels, call(): pl.pallas_call(with_token, grid=grid, in_specs=[held_spec(a.shape) if kin...  153 us
    ppermute x27, waiting for transfers between devices, swap(): return lax.ppermute(value, axis, flip_pairs(lax.axis_size(axis), 1 << bit))  91.8 us
    ppermute x27, starting transfers between devices, swap(): return lax.ppermute(value, axis, flip_pairs(lax.axis_size(axis), 1 << bit))  35.9 us
    all_to_all x1, blocking collectives, sum_over_all(): return jnp.sum(lax.all_to_all(copies, ('rec', 'seq'), 0, 0), axis=0)  15.6 us
    ppermute x6, waiting for transfers between devices, entering(): other = lax.ppermute(value, 'seq', flip_pairs(count, 1 << bit))  14.5 us
    pallas_call x13, Pallas kernels, in_vmem(): pl.pallas_call(kernel, in_specs=[scalars()] + [vmem] * len(ins) + [anywhe...  13.6 us
    unnamed x53, local copies, waits for them, and re-layouts  12.2 us
    ppermute x6, starting transfers between devices, entering(): other = lax.ppermute(value, 'seq', flip_pairs(count, 1 << bit))  12 us
  transfers between devices with their start and end apart: 39, of which 21 were waited for; matrix products, arithmetic and copies ran while one was open for 1% of the time, Pallas kernels for 27%

profile of v7, /device:TPU:0, one launch (start us, length us, event | category | flops | bytes accessed | tf_op | source)
XLA Modules:
  0.0 388.5 jit_solution(3096633760164705610)
XLA Ops:
  8.2 20.0 %front.1 = (bf16[4,256,512]{2,1,0:T(8,128)(2,1)}, f32[4,256,512]{2,1,0:T(8,128)}, bf16[4,256,512]{2,1,0:T(8,128)(2,1)}, f32[4,256,1]{2,1,0:T(8,128)}, bf16[4,256...) custom-call(bf16[4,80,1024]{2,1,0:T(8,128)(2,1)} %bitcast.59, ...), custom_call_target="tpu_custom_call" | custom-call | flops 46000001024 | tf_op jit(solution)/shard_map/front/pallas_call | solution.py:635
  35.1 7.0 %collective-permute-done.1.other = f32[4,136,128]{2,1,0:T(8,128)S(1)} collective-permute-done((f32[4,136,128]{2,1,0:T(8,128)S(1)}, f32[4,136,128]{2,1,0:T(8,128)S(1)}, u32[]{:S(2)}, u32[]{:S(2)}) %collective-permute-start.1) | collective-permute-done | bytes 278560 | tf_op jit(solution)/shard_map/ppermute | solution.py:698
  45.0 7.1 %mix.1 = (bf16[4,256,512]{2,1,0:T(8,128)(2,1)}, bf16[4,8,256,256]{3,2,1,0:T(8,128)(2,1)}, bf16[4,8,256,256]{3,2,1,0:T(8,128)(2,1)}, f32[8,128]{1,0:T(8,128)}) custom-call(bf16[4,256,512]{2,1,0:T(8,128)(2,1)} %get-tuple-element.177.refs_0_.refs_1_, bf16[4,256,256]{2,1,0:T(8,128)(2,1)} %get-tuple-element.178.refs_1_, ...), custom_call_target="tpu_custom_call" | custom-call | flops 16099999744 | tf_op jit(solution)/shard_map/mix/pallas_call | solution.py:635
  54.1 8.7 %lift.1 = (bf16[4,256,512]{2,1,0:T(8,128)(2,1)}, bf16[4,256,512]{2,1,0:T(8,128)(2,1)}, bf16[4,256,512]{2,1,0:T(8,128)(2,1)}, f32[4,256,512]{2,1,0:T(8,128)}, bf1...) custom-call(bf16[4,256,512]{2,1,0:T(8,128)(2,1)} %get-tuple-element., ...), custom_call_target="tpu_custom_call" | custom-call | flops 20700000256 | tf_op jit(solution)/shard_map/lift/pallas_call | solution.py:635
  69.8 5.6 %depth.1 = (f32[4,256,512]{2,1,0:T(8,128)}, f32[2,512]{1,0:T(2,128)}, f32[8,128]{1,0:T(8,128)}) custom-call(f32[4,256,512]{2,1,0:T(8,128)} %get-tuple-element.192.refs_0_.refs_5_, f32[4,8,512]{2,1,0:T(8,128)} %copy-done.22, f32[4,8,512]{2,1,0:T(8,128)} %copy-done.23, f32[2,4]{1,0:T(2,128)S(1)} %pad_maximum_fusion.refs_4_.keep.refs_3_.refs_8_, ...), custom_call_target="tpu_custom_call" | custom-call | flops 13799999488 | tf_op jit(solution)/shard_map/depth/pallas_call | solution.py:635
  76.1 15.6 %all_to_all.10 = f32[32,2,512]{2,1,0:T(2,128)S(1)} all-to-all(f32[32,2,512]{2,1,0:T(2,128)S(1)} %broadcast_in_dim.9), channel_id=1, replica_groups=mesh['seq'=8,'rec'=4] {'rec','seq'}, dimensions={0} | all-to-all | bytes 262144 | tf_op jit(solution)/shard_map/all_to_all | solution.py:729
  92.3 21.9 %late.1 = (bf16[4,256,512]{2,1,0:T(8,128)(2,1)}, bf16[4,256,512]{2,1,0:T(8,128)(2,1)}, bf16[4,256,512]{2,1,0:T(8,128)(2,1)}, bf16[4,256,2048]{2,1,0:T(8,128)(2,1...) custom-call(f32[4,256,512]{2,1,0:T(8,128)} %get-tuple-element.195.re, ...), custom_call_target="tpu_custom_call" | custom-call | flops 52899999744 | tf_op jit(solution)/shard_map/late/pallas_call | solution.py:635
  118.2 10.0 %late_weights.1 = (f32[512,4096]{1,0:T(8,128)}, f32[8,128]{1,0:T(8,128)}) custom-call(bf16[1024,512]{1,0:T(8,128)(2,1)} %bitcast.88, bf16[1024,2048]{1,0:T(8,128)(2,1)} %bitcast.73, bf16[1024,2048]{1,0:T(8,128)(2,1)} %bitcast.74, bf16[1024,512]{1,0:T(8,128)(2,1)} %bitcast.89), custom_call_target="tpu_custom_call" | custom-call | flops 25300000768 | tf_op jit(solution)/shard_map/late_weights/pallas_call | solution.py:635
  133.5 6.8 %depth_grad.1 = (bf16[4,256,512]{2,1,0:T(8,128)(2,1)}, f32[16,512]{1,0:T(8,128)}, f32[8,128]{1,0:T(8,128)}) custom-call(bf16[4,256,512]{2,1,0:T(8,128)(2,1)} %get-tuple-element.199.refs_0_, f32[4,256,512]{2,1,0:T(8,128)} %get-tuple-element.195.refs_0_.refs_1_, f32[2,512]{1,0:T(2,128)} %reduce_sum.18.refs_3_.refs_2_, f32[2,512]{1,0:T(2,128)} %copy-done.18, ...), custom_call_target="tpu_custom_call" | custom-call | flops 29899999232 | tf_op jit(solution)/shard_map/depth_grad/pallas_call | solution.py:635
  141.0 12.3 %conv_back.1 = (bf16[4,256,1024]{2,1,0:T(8,128)(2,1)}, f32[4,256,512]{2,1,0:T(8,128)}, bf16[4,256,512]{2,1,0:T(8,128)(2,1)}, bf16[4,256,512]{2,1,0:T(8,128)(2,1)...) custom-call(bf16[4,256,512]{2,1,0:T(8,128)(2,1)} %get-tuple-element.206.refs_0_, ...), custom_call_target="tpu_custom_call" | custom-call | flops 4600000000 | tf_op jit(solution)/shard_map/conv_back/pallas_call | solution.py:635
  160.2 8.5 %weights.3 = (f32[256,2048]{1,0:T(8,128)}, f32[256,2048]{1,0:T(8,128)}, f32[8,128]{1,0:T(8,128)}) custom-call(s32[1]{0:T(128)} %bitcast.24.refs_0_, bf16[1024,512]{1,0:T(8,128)(2,1)} %bitcast.82, bf16[1024,512]{1,0:T(8,128)(2,1)} %bitcast.81, bf16[1024,512]{1,0:T(8,128)(2,1)} %bitcast.83, bf16[1024,1024]{1,0:T(8,128)(2,1)} %bitcast.76, ...), custom_call_target="tpu_custom_call" | custom-call | flops 23000000512 | tf_op jit(solution)/shard_map/weights/pallas_call | solution.py:635
  168.7 4.8 %collective-permute-done.8.other = f32[4,136,128]{2,1,0:T(8,128)S(1)} collective-permute-done((f32[4,136,128]{2,1,0:T(8,128)S(1)}, f32[4,136,128]{2,1,0:T(8,128)S(1)}, u32[]{:S(2)}, u32[]{:S(2)}) %collective-permute-start.8) | collective-permute-done | bytes 278560 | tf_op jit(solution)/shard_map/ppermute | solution.py:698
  179.5 9.4 %mix_back.1 = (bf16[4,256,512]{2,1,0:T(8,128)(2,1)}, bf16[4,256,256]{2,1,0:T(8,128)(2,1)}, bf16[4,256,256]{2,1,0:T(8,128)(2,1)}, f32[8,128]{1,0:T(8,128)}) custom-call(bf16[4,256,512]{2,1,0:T(8,128)(2,1)} %get-tuple-element.177.refs_0_.refs_1_, bf16[4,256,256]{2,1,0:T(8,128)(2,1)} %get-tuple-element.178.refs_1_, ...), custom_call_target="tpu_custom_call" | custom-call | flops 27599998976 | tf_op jit(solution)/shard_map/mix_back/pallas_call | solution.py:635
  192.2 9.5 %mix_end.1 = (bf16[4,256,1536]{2,1,0:T(8,128)(2,1)}, f32[4,256,512]{2,1,0:T(8,128)}, bf16[4,256,512]{2,1,0:T(8,128)(2,1)}, f32[1,512]{1,0:T(1,128)}, f32[8,128]{1,0:T(8,128)}) custom-call(f32[4,136,128]{2,1,0:T(8,128)} %copy-done.13, bf16[4,256,512]{2,1,0:T(8,128)(2,1)} %get-tuple-element.177.refs_0_.refs_1_, ...), custom_call_target="tpu_custom_call" | custom-call | flops 4600000000 | tf_op jit(solution)/shard_map/mix_end/pallas_call | solution.py:635
  206.0 11.4 %weights.4 = (f32[256,3584]{1,0:T(8,128)}, f32[256,3584]{1,0:T(8,128)}, f32[8,128]{1,0:T(8,128)}) custom-call(s32[1]{0:T(128)} %bitcast.24.refs_0_, bf16[1024,512]{1,0:T(8,128)(2,1)} %bitcast.80, bf16[1024,2048]{1,0:T(8,128)(2,1)} %bitcast.71, bf16[1024,1536]{1,0:T(8,128)(2,1)} %bitcast.75, bf16[1024,512]{1,0:T(8,128)(2,1)} %bitcast.85, ...), custom_call_target="tpu_custom_call" | custom-call | flops 23000000512 | tf_op jit(solution)/shard_map/weights/pallas_call | solution.py:635
  221.8 12.6 %front_back.1 = (bf16[4,256,2048]{2,1,0:T(8,128)(2,1)}, bf16[4,256,512]{2,1,0:T(8,128)(2,1)}, f32[4,80,1024]{2,1,0:T(8,128)}, f32[1,512]{1,0:T(1,128)}, f32[8,128]{1,0:T(8,128)}) custom-call(f32[4,256,512]{2,1,0:T(8,128)} %get-tuple-element.246.refs_0_, bf16[4,256,512]{2,1,0:T(8,128)(2,1)} %get-tuple-element.247.refs_1_, bf16[2048,512]{1,0:T(8,128)(2,1)} %refs_2_.5, ...), custom_call_target="tpu_custom_call" | custom-call | flops 69000003584 | tf_op jit(solution)/shard_map/front_back/pallas_call | solution.py:635
  243.2 9.0 %weights.5 = (f32[256,2560]{1,0:T(8,128)}, f32[256,2560]{1,0:T(8,128)}, f32[8,128]{1,0:T(8,128)}) custom-call(s32[1]{0:T(128)} %bitcast.24.refs_0_, bf16[1024,512]{1,0:T(8,128)(2,1)} %bitcast.79, bf16[1024,512]{1,0:T(8,128)(2,1)} %bitcast.87, bf16[1024,2048]{1,0:T(8,128)(2,1)} %bitcast.72, bf16[1024,512]{1,0:T(8,128)(2,1)} %bitcast.78, ...), custom_call_target="tpu_custom_call" | custom-call | flops 23000000512 | tf_op jit(solution)/shard_map/weights/pallas_call | solution.py:635
  252.2 7.7 %collective-permute-done.18.refs_2_ = f32[128,1792]{1,0:T(8,128)S(1)} collective-permute-done((f32[128,1792]{1,0:T(8,128)S(1)}, f32[128,1792]{1,0:T(8,128)S(1)}, u32[]{:S(2)}, u32[]{:S(2)}) %collective-permute-start.18) | collective-permute-done | bytes 917536 | tf_op jit(solution)/shard_map/ppermute | solution.py:850
  270.1 15.9 %collective-permute-done.20.refs_1_ = f32[16,6144]{1,0:T(8,128)S(1)} collective-permute-done((f32[16,6144]{1,0:T(8,128)S(1)}, f32[16,6144]{1,0:T(8,128)S(1)}, u32[]{:S(2)}, u32[]{:S(2)}) %collective-permute-start.20) | collective-permute-done | bytes 393248 | tf_op jit(solution)/shard_map/ppermute | solution.py:850
  294.9 5.5 %collective-permute-done.28.refs_2_ = f32[64,1280]{1,0:T(8,128)S(1)} collective-permute-done((f32[64,1280]{1,0:T(8,128)S(1)}, f32[64,1280]{1,0:T(8,128)S(1)}, u32[]{:S(2)}, u32[]{:S(2)}) %collective-permute-start.28) | collective-permute-done | bytes 327712 | tf_op jit(solution)/shard_map/ppermute | solution.py:850
  309.5 20.2 %collective-permute-done.30.refs_3_ = f32[16,3584]{1,0:T(8,128)S(1)} collective-permute-done((f32[16,3584]{1,0:T(8,128)S(1)}, f32[16,3584]{1,0:T(8,128)S(1)}, u32[]{:S(2)}, u32[]{:S(2)}) %collective-permute-start.30) | collective-permute-done | bytes 229408 | tf_op jit(solution)/shard_map/ppermute | solution.py:850
  335.2 15.7 %collective-permute-done.33.refs_3_ = f32[16,2560]{1,0:T(8,128)S(1)} collective-permute-done((f32[16,2560]{1,0:T(8,128)S(1)}, f32[16,2560]{1,0:T(8,128)S(1)}, u32[]{:S(2)}, u32[]{:S(2)}) %collective-permute-start.33) | collective-permute-done | bytes 163872 | tf_op jit(solution)/shard_map/ppermute | solution.py:850
  355.7 10.1 %collective-permute-done.35.refs_3_ = f32[16,2560]{1,0:T(8,128)S(1)} collective-permute-done((f32[16,2560]{1,0:T(8,128)S(1)}, f32[16,2560]{1,0:T(8,128)S(1)}, u32[]{:S(2)}, u32[]{:S(2)}) %collective-permute-start.35) | collective-permute-done | bytes 163872 | tf_op jit(solution)/shard_map/ppermute | solution.py:850
  372.7 6.2 %collective-permute-done.36.refs_1_ = f32[32,2560]{1,0:T(8,128)S(1)} collective-permute-done((f32[32,2560]{1,0:T(8,128)S(1)}, f32[32,2560]{1,0:T(8,128)S(1)}, u32[]{:S(2)}, u32[]{:S(2)}) %collective-permute-start.36) | collective-permute-done | bytes 327712 | tf_op jit(solution)/shard_map/ppermute | solution.py:850
  (155 shorter events, 112.7 us)
Async XLA Ops:
  118.1 99.6 %reduce-scatter.2.cloned.1.call-start = ((), (), s32[]{:S(2)}) async-start(), calls=%async_computation.3 | async-start | bytes 9437184 | tf_op jit(solution)/shard_map/reduce_scatter | solution.py:733
  158.1 15.3 %collective-permute-start.8 = (f32[4,136,128]{2,1,0:T(8,128)S(1)}, f32[4,136,128]{2,1,0:T(8,128)S(1)}, u32[]{:S(2)}, u32[]{:S(2)}) collective-permute-start(f32[4,136,128]{2,1,0:T(8,128)S(1)} %get-tuple-element.215.value), channel_id=1, source_target_pairs={{0,8},{4,12},{8,0},{12,4},{16,24},{20,28},{24,16},{28,20},{1,9},{5... | collective-permute-start | bytes 835592 | tf_op jit(solution)/shard_map/ppermute | solution.py:698
  174.1 14.7 %collective-permute-start.9 = (f32[4,136,128]{2,1,0:T(8,128)S(1)}, f32[4,136,128]{2,1,0:T(8,128)S(1)}, u32[]{:S(2)}, u32[]{:S(2)}) collective-permute-start(f32[4,136,128]{2,1,0:T(8,128)S(1)} %get-tuple-element.217.value), channel_id=1, source_target_pairs={{0,16},{4,20},{8,24},{12,28},{16,0},{20,4},{24,8},{28,12},{1,17},{... | collective-permute-start | bytes 835592 | tf_op jit(solution)/shard_map/ppermute | solution.py:698
  177.9 23.9 %collective-permute-start.11 = (f32[128,1024]{1,0:T(8,128)S(1)}, f32[128,1024]{1,0:T(8,128)S(1)}, u32[]{:S(2)}, u32[]{:S(2)}) collective-permute-start(f32[128,1024]{1,0:T(8,128)S(1)} %get-tuple-element.252), channel_id=1, source_target_pairs={{0,8},{4,12},{8,0},{12,4},{16,24},{20,28},{24,16},{28,20},{1,9},{5... | collective-permute-start | bytes 1572872 | tf_op jit(solution)/shard_map/ppermute | solution.py:850
  178.4 23.4 %collective-permute-start.12 = (f32[128,1024]{1,0:T(8,128)S(1)}, f32[128,1024]{1,0:T(8,128)S(1)}, u32[]{:S(2)}, u32[]{:S(2)}) collective-permute-start(f32[128,1024]{1,0:T(8,128)S(1)} %get-tuple-element.254), channel_id=1, source_target_pairs={{0,16},{4,20},{8,24},{12,28},{16,0},{20,4},{24,8},{28,12},{1,17},{... | collective-permute-start | bytes 1572872 | tf_op jit(solution)/shard_map/ppermute | solution.py:850
  203.1 14.3 %collective-permute-start.13 = (f32[64,1024]{1,0:T(8,128)S(1)}, f32[64,1024]{1,0:T(8,128)S(1)}, u32[]{:S(2)}, u32[]{:S(2)}) collective-permute-start(f32[64,1024]{1,0:T(8,128)S(1)} %get-tuple-element.257), channel_id=1, source_target_pairs={{0,16},{4,20},{8,24},{12,28},{16,0},{20,4},{24,8},{28,12},{1,17},{... | collective-permute-start | bytes 786440 | tf_op jit(solution)/shard_map/ppermute | solution.py:850
  217.4 17.1 %collective-permute-start.16 = (f32[256,3584]{1,0:T(8,128)}, f32[256,3584]{1,0:T(8,128)}, u32[]{:S(2)}, u32[]{:S(2)}) collective-permute-start(f32[256,3584]{1,0:T(8,128)} %get-tuple-element.269), channel_id=1, source_target_pairs={{0,4},{4,0},{8,12},{12,8},{16,20},{20,16},{24,28},{28,24},{1,5},{5... | collective-permute-start | bytes 11010056 | tf_op jit(solution)/shard_map/ppermute | solution.py:850
  220.3 19.7 %collective-permute-start.15 = (f32[32,6144]{1,0:T(8,128)S(1)}, f32[32,6144]{1,0:T(8,128)S(1)}, u32[]{:S(2)}, u32[]{:S(2)}) collective-permute-start(f32[32,6144]{1,0:T(8,128)S(1)} %get-tuple-element.267), channel_id=1, source_target_pairs={{0,1},{1,0},{2,3},{3,2},{4,5},{5,4},{6,7},{7,6},{8,9},{9,8},{10,11... | collective-permute-start | bytes 2359304 | tf_op jit(solution)/shard_map/ppermute | solution.py:850
  237.6 22.3 %collective-permute-start.18 = (f32[128,1792]{1,0:T(8,128)S(1)}, f32[128,1792]{1,0:T(8,128)S(1)}, u32[]{:S(2)}, u32[]{:S(2)}) collective-permute-start(f32[128,1792]{1,0:T(8,128)S(1)} %get-tuple-element.275), channel_id=1, source_target_pairs={{0,8},{4,12},{8,0},{12,4},{16,24},{20,28},{24,16},{28,20},{1,9},{5... | collective-permute-start | bytes 2752520 | tf_op jit(solution)/shard_map/ppermute | solution.py:850
  239.0 21.3 %collective-permute-start.19 = (f32[128,1792]{1,0:T(8,128)S(1)}, f32[128,1792]{1,0:T(8,128)S(1)}, u32[]{:S(2)}, u32[]{:S(2)}) collective-permute-start(f32[128,1792]{1,0:T(8,128)S(1)} %get-tuple-element.277), channel_id=1, source_target_pairs={{0,16},{4,20},{8,24},{12,28},{16,0},{20,4},{24,8},{28,12},{1,17},{... | collective-permute-start | bytes 2752520 | tf_op jit(solution)/shard_map/ppermute | solution.py:850
  240.6 19.8 %collective-permute-start.17 = (f32[16,6144]{1,0:T(8,128)S(1)}, f32[16,6144]{1,0:T(8,128)S(1)}, u32[]{:S(2)}, u32[]{:S(2)}) collective-permute-start(f32[16,6144]{1,0:T(8,128)S(1)} %get-tuple-element.274), channel_id=1, source_target_pairs={{0,2},{1,3},{2,0},{3,1},{4,6},{5,7},{6,4},{7,5},{8,10},{9,11},{10,... | collective-permute-start | bytes 1179656 | tf_op jit(solution)/shard_map/ppermute | solution.py:850
  263.7 26.2 %collective-permute-start.24 = (f32[128,1280]{1,0:T(8,128)S(1)}, f32[128,1280]{1,0:T(8,128)S(1)}, u32[]{:S(2)}, u32[]{:S(2)}) collective-permute-start(f32[128,1280]{1,0:T(8,128)S(1)} %get-tuple-element.298), channel_id=1, source_target_pairs={{0,8},{4,12},{8,0},{12,4},{16,24},{20,28},{24,16},{28,20},{1,9},{5... | collective-permute-start | bytes 1966088 | tf_op jit(solution)/shard_map/ppermute | solution.py:850
  264.9 25.0 %collective-permute-start.25 = (f32[128,1280]{1,0:T(8,128)S(1)}, f32[128,1280]{1,0:T(8,128)S(1)}, u32[]{:S(2)}, u32[]{:S(2)}) collective-permute-start(f32[128,1280]{1,0:T(8,128)S(1)} %get-tuple-element.300), channel_id=1, source_target_pairs={{0,16},{4,20},{8,24},{12,28},{16,0},{20,4},{24,8},{28,12},{1,17},{... | collective-permute-start | bytes 1966088 | tf_op jit(solution)/shard_map/ppermute | solution.py:850
  265.7 24.2 %collective-permute-start.21 = (f32[64,1792]{1,0:T(8,128)S(1)}, f32[64,1792]{1,0:T(8,128)S(1)}, u32[]{:S(2)}, u32[]{:S(2)}) collective-permute-start(f32[64,1792]{1,0:T(8,128)S(1)} %get-tuple-element.291), channel_id=1, source_target_pairs={{0,16},{4,20},{8,24},{12,28},{16,0},{20,4},{24,8},{28,12},{1,17},{... | collective-permute-start | bytes 1376264 | tf_op jit(solution)/shard_map/ppermute | solution.py:850
  267.0 23.0 %collective-permute-start.22 = (f32[64,1792]{1,0:T(8,128)S(1)}, f32[64,1792]{1,0:T(8,128)S(1)}, u32[]{:S(2)}, u32[]{:S(2)}) collective-permute-start(f32[64,1792]{1,0:T(8,128)S(1)} %get-tuple-element.293), channel_id=1, source_target_pairs={{0,8},{4,12},{8,0},{12,4},{16,24},{20,28},{24,16},{28,20},{1,9},{5... | collective-permute-start | bytes 1376264 | tf_op jit(solution)/shard_map/ppermute | solution.py:850
  267.8 18.2 %collective-permute-start.20 = (f32[16,6144]{1,0:T(8,128)S(1)}, f32[16,6144]{1,0:T(8,128)S(1)}, u32[]{:S(2)}, u32[]{:S(2)}) collective-permute-start(f32[16,6144]{1,0:T(8,128)S(1)} %get-tuple-element.290.refs_0_), channel_id=1, source_target_pairs={{0,2},{1,3},{2,0},{3,1},{4,6},{5,7},{6,4},{7,5},{8,10},{9,11},{10,... | collective-permute-start | bytes 1179656 | tf_op jit(solution)/shard_map/ppermute | solution.py:850
  290.8 13.5 %collective-permute-start.27 = (f32[32,3584]{1,0:T(8,128)S(1)}, f32[32,3584]{1,0:T(8,128)S(1)}, u32[]{:S(2)}, u32[]{:S(2)}) collective-permute-start(f32[32,3584]{1,0:T(8,128)S(1)} %get-tuple-element.304), channel_id=1, source_target_pairs={{0,1},{1,0},{2,3},{3,2},{4,5},{5,4},{6,7},{7,6},{8,9},{9,8},{10,11... | collective-permute-start | bytes 1376264 | tf_op jit(solution)/shard_map/ppermute | solution.py:850
  291.9 38.6 %collective-permute-start.26 = (f32[32,6144]{1,0:T(8,128)S(1)}, f32[32,6144]{1,0:T(8,128)S(1)}, u32[]{:S(2)}, u32[]{:S(2)}) collective-permute-start(f32[32,6144]{1,0:T(8,128)S(1)} %get-tuple-element.303.refs_0_), channel_id=1, source_target_pairs={{0,1},{1,0},{2,3},{3,2},{4,5},{5,4},{6,7},{7,6},{8,9},{9,8},{10,11... | collective-permute-start | bytes 2359304 | tf_op jit(solution)/shard_map/ppermute | solution.py:850
  305.0 25.5 %collective-permute-start.31 = (f32[32,2560]{1,0:T(8,128)S(1)}, f32[32,2560]{1,0:T(8,128)S(1)}, u32[]{:S(2)}, u32[]{:S(2)}) collective-permute-start(f32[32,2560]{1,0:T(8,128)S(1)} %get-tuple-element.313), channel_id=1, source_target_pairs={{0,1},{1,0},{2,3},{3,2},{4,5},{5,4},{6,7},{7,6},{8,9},{9,8},{10,11... | collective-permute-start | bytes 983048 | tf_op jit(solution)/shard_map/ppermute | solution.py:850
  306.2 23.6 %collective-permute-start.30 = (f32[16,3584]{1,0:T(8,128)S(1)}, f32[16,3584]{1,0:T(8,128)S(1)}, u32[]{:S(2)}, u32[]{:S(2)}) collective-permute-start(f32[16,3584]{1,0:T(8,128)S(1)} %get-tuple-element.312), channel_id=1, source_target_pairs={{0,2},{1,3},{2,0},{3,1},{4,6},{5,7},{6,4},{7,5},{8,10},{9,11},{10,... | collective-permute-start | bytes 688136 | tf_op jit(solution)/shard_map/ppermute | solution.py:850
  332.3 18.6 %collective-permute-start.32 = (f32[16,3584]{1,0:T(8,128)S(1)}, f32[16,3584]{1,0:T(8,128)S(1)}, u32[]{:S(2)}, u32[]{:S(2)}) collective-permute-start(f32[16,3584]{1,0:T(8,128)S(1)} %get-tuple-element.316.refs_0_), channel_id=1, source_target_pairs={{0,2},{1,3},{2,0},{3,1},{4,6},{5,7},{6,4},{7,5},{8,10},{9,11},{10,... | collective-permute-start | bytes 688136 | tf_op jit(solution)/shard_map/ppermute | solution.py:850
  335.0 15.9 %collective-permute-start.33 = (f32[16,2560]{1,0:T(8,128)S(1)}, f32[16,2560]{1,0:T(8,128)S(1)}, u32[]{:S(2)}, u32[]{:S(2)}) collective-permute-start(f32[16,2560]{1,0:T(8,128)S(1)} %get-tuple-element.318), channel_id=1, source_target_pairs={{0,2},{1,3},{2,0},{3,1},{4,6},{5,7},{6,4},{7,5},{8,10},{9,11},{10,... | collective-permute-start | bytes 491528 | tf_op jit(solution)/shard_map/ppermute | solution.py:850
  351.5 15.0 %collective-permute-start.34 = (f32[32,3584]{1,0:T(8,128)S(1)}, f32[32,3584]{1,0:T(8,128)S(1)}, u32[]{:S(2)}, u32[]{:S(2)}) collective-permute-start(f32[32,3584]{1,0:T(8,128)S(1)} %get-tuple-element.320.refs_0_), channel_id=1, source_target_pairs={{0,1},{1,0},{2,3},{3,2},{4,5},{5,4},{6,7},{7,6},{8,9},{9,8},{10,11... | collective-permute-start | bytes 1376264 | tf_op jit(solution)/shard_map/ppermute | solution.py:850
  352.3 13.5 %collective-permute-start.35 = (f32[16,2560]{1,0:T(8,128)S(1)}, f32[16,2560]{1,0:T(8,128)S(1)}, u32[]{:S(2)}, u32[]{:S(2)}) collective-permute-start(f32[16,2560]{1,0:T(8,128)S(1)} %get-tuple-element.321.refs_2_), channel_id=1, source_target_pairs={{0,2},{1,3},{2,0},{3,1},{4,6},{5,7},{6,4},{7,5},{8,10},{9,11},{10,... | collective-permute-start | bytes 491528 | tf_op jit(solution)/shard_map/ppermute | solution.py:850
  (41 other events, 201.3 us)
Sparse Core Ops, SparseCore 0:
  128.4 89.2 reduce-scatter.1
